TPU v7x, 256 devices: a whole 4x4x8 slice. The times are simulated.
256 devices in a mesh: layer: 8 (over y, z_hi), latent: 32 (over z_lo, x, core).
Axes of the slice: x: 4, y: 4, z: 8 (z_hi: 2, z_lo: 4; z = z_hi * 4 + z_lo), core: 2. Of those that a mesh axis runs over, the one named last changes fastest.
Arguments:
- acts: bfloat16 [512, 8, 2048], P(None, 'layer'), may hold values from -6 to 6
- mask: int32 [512, 16384], P(None, 'latent'), may hold values 0 or 1
- w_enc: bfloat16 [8, 2048, 16384], P('layer', None, 'latent'), may hold values from -0.046875 to 0.046875
- b_enc: float32 [16384], P('latent'), may hold values from -3 to 3
- w_dec: bfloat16 [16384, 8, 2048], P('latent', 'layer'), may hold values from -8 to 8
- b_dec: float32 [8, 2048], P('layer'), may hold values from -3 to 3
Outputs:
- grad_enc: bfloat16 [8, 2048, 16384], P('layer', None, 'latent')
- grad_dec: bfloat16 [16384, 8, 2048], P('latent', 'layer')
All inputs are finite; a program needn't handle non-finite values. No bound on the sum of `mask` on one device may be relied on, other than what follows from the above.
Results may differ from a plain program's by a relative error of at most 0.007.
Values may be sent and summed in bfloat16 or wider, within the bound.
No kernel may reach another device: no remote copies, remote signals or barrier semaphores. Data moves between devices by JAX's collectives and lax.ppermute only.
A program may use at most 64 MiB of HBM per device.

v0:
```python
import jax
import jax.numpy as jnp
from jax import lax
from jax.sharding import PartitionSpec as P

loss_scale = 0.0625
sparsity = 0.25


def body(acts, mask, w_enc, b_enc, w_dec, b_dec):
    rows = acts.shape[0]
    width = acts.shape[1] * acts.shape[2]
    latents = w_enc.shape[2]
    flat = acts.reshape(rows, width)
    enc_flat = w_enc.reshape(width, latents)
    dec_flat = w_dec.reshape(latents, width)
    active = mask.astype(jnp.float32)
    wide = w_dec.astype(jnp.float32)
    lengths = jnp.sqrt(jnp.sum(wide * wide, axis=2) + 1e-06)
    local_norms = jnp.sum(lengths, axis=1)
    partial_pre = jnp.dot(flat, enc_flat, preferred_element_type=jnp.float32)
    pre, norms = lax.psum((partial_pre, local_norms), "layer")
    codes = (active * (pre + b_enc[None, :])).astype(jnp.bfloat16)
    bias_flat = b_dec.reshape(width)
    recon = lax.psum(jnp.dot(codes, dec_flat, preferred_element_type=jnp.float32), "latent")
    error = (recon + bias_flat[None, :] - flat.astype(jnp.float32)).astype(jnp.bfloat16)
    partial_back = lax.dot_general(
        error, dec_flat, (((1,), (1,)), ((), ())), preferred_element_type=jnp.float32
    )
    back = lax.psum(partial_back, "layer")
    dpre = (loss_scale * active * (back + sparsity * norms[None, :])).astype(jnp.bfloat16)
    grad_enc = lax.dot_general(
        flat, dpre, (((0,), (0,)), ((), ())), preferred_element_type=jnp.float32
    )
    grad_enc = grad_enc.reshape(w_enc.shape).astype(jnp.bfloat16)
    usage = jnp.sum(codes.astype(jnp.float32), axis=0)
    cross = lax.dot_general(
        codes, error, (((0,), (0,)), ((), ())), preferred_element_type=jnp.float32
    )
    grad_dec = loss_scale * (
        cross.reshape(w_dec.shape) + sparsity * usage[:, None, None] * wide / lengths[:, :, None]
    )
    return (grad_enc, grad_dec.astype(jnp.bfloat16))


def solution(mesh):
    return jax.shard_map(
        body,
        mesh=mesh,
        in_specs=(
            P(None, "layer", None),
            P(None, "latent"),
            P("layer", None, "latent"),
            P("latent"),
            P("latent", "layer", None),
            P("layer", None),
        ),
        out_specs=(P("layer", None, "latent"), P("latent", "layer", None)),
        check_vma=False,
    )
```

profile of v0, /device:TPU:32, one launch (start us, length us, event | category | flops | bytes accessed | tf_op | source)
XLA Modules:
  0.0 594.7 jit_solution(9926800383568461104)
XLA Ops:
  7.2 0.0 copy-start
  7.2 0.0 copy-start.5
  7.2 0.0 all-reduce.4.cloned.1.call-start
  7.2 1.5 copy-done
  8.8 3.8 fusion.10
  12.6 0.0 all-reduce.4.cloned.1.call-update
  12.6 0.0 all-reduce.6.cloned.1.call-start
  12.6 136.3 %all-reduce.4.cloned.1.call-done = f32[512,512]{1,0:T(8,128)} async-done(((f32[512,512]{1,0:T(8,128)}), f32[512,512]{1,0:T(8,128)}) %all-reduce.4.cloned.1.call-update) | async-done | bytes 1048592 | tf_op jit(solution)/shard_map/psum | solution.py:22
  148.9 0.0 copy-done.5
  148.9 0.0 copy-start.1
  148.9 2.0 convert_reduce_fusion
  150.9 0.3 copy-done.1
  151.2 3.3 fusion.8
  154.4 0.0 all-reduce.6.cloned.1.call-update
  154.5 0.0 copy-start.4
  154.5 0.0 all-reduce.8.cloned.1.call-start
  154.5 2.1 fusion
  156.6 26.5 %psum.31 = f32[512]{0:T(512)S(1)} all-reduce(f32[512]{0:T(512)S(1)} %add_sqrt_fusion), channel_id=1, replica_groups=mesh['layer'=8,'latent'=32] {'layer'}, use_global_device_ids=true, to_apply=%region_4.0 | all-reduce | flops 512 | bytes 4096 | tf_op jit(solution)/shard_map/psum | solution.py:22
  183.1 242.2 %all-reduce.6.cloned.1.call-done = f32[512,2048]{1,0:T(8,128)} async-done(((f32[512,2048]{1,0:T(8,128)}), f32[512,2048]{1,0:T(8,128)}) %all-reduce.6.cloned.1.call-update) | async-done | bytes 4194320 | tf_op jit(solution)/shard_map/psum | solution.py:25
  425.3 0.0 copy-done.4
  425.3 0.0 copy-start.2
  425.3 3.7 subtract_convert_fusion
  429.0 0.0 copy-start.3
  429.0 1.3 copy-done.3
  430.3 0.0 copy-done.2
  430.3 2.3 fusion.6
  432.6 0.0 all-reduce.8.cloned.1.call-update
  432.7 5.1 fusion.4
  437.8 141.5 %all-reduce.8.cloned.1.call-done = f32[512,512]{1,0:T(8,128)} async-done(((f32[512,512]{1,0:T(8,128)}), f32[512,512]{1,0:T(8,128)}) %all-reduce.8.cloned.1.call-update) | async-done | bytes 1048592 | tf_op jit(solution)/shard_map/psum | solution.py:30
  579.3 5.0 fusion.5
  584.2 3.9 copy.8
  (3 shorter events, 0.0 us)
Async XLA Ops:
  7.2 1.6 copy-start
  7.2 141.8 %copy-start.5 = (f32[512]{0:T(512)S(1)}, f32[512]{0:T(512)}, u32[]{:S(2)}) copy-start(f32[512]{0:T(512)} %param.9) | copy-start | bytes 6148
  7.2 141.7 %all-reduce.4.cloned.1.call-start = ((), (), s32[]{:S(2)}) async-start(), calls=%async_computation | async-start | bytes 2097152 | tf_op jit(solution)/shard_map/psum | solution.py:22
  12.6 412.7 %all-reduce.6.cloned.1.call-start = ((), (), s32[]{:S(2)}) async-start(), calls=%async_computation.1 | async-start | bytes 8388608 | tf_op jit(solution)/shard_map/psum | solution.py:25
  148.9 2.2 copy-start.1
  154.5 270.8 %copy-start.4 = (f32[1,2048]{1,0:T(1,128)S(1)}, f32[1,2048]{1,0:T(1,128)}, u32[]{:S(2)}) copy-start(f32[1,2048]{1,0:T(1,128)} %param.11) | copy-start | bytes 24580
  154.5 424.8 %all-reduce.8.cloned.1.call-start = ((), (), s32[]{:S(2)}) async-start(), calls=%async_computation.2 | async-start | bytes 2097152 | tf_op jit(solution)/shard_map/psum | solution.py:30
  425.3 5.0 copy-start.2
  429.0 1.3 copy-start.3
Sparse Core Ops, SparseCore 0:
  12.7 136.1 all-reduce.3
  154.6 270.6 all-reduce.5
  432.8 146.4 all-reduce.7
where the time goes:
time: 596 us; the launch traced here: 595 us
  waiting for transfers between devices  520 us (87%)
  blocking collectives  26.5 us (4%)
  matrix products  19.4 us (3%)
  between operations  13.8 us (2%)
  other arithmetic  7.77 us (1%)
  local copies, waits for them, and re-layouts  7.03 us (1%)
    psum x1, waiting for transfers between devices, body(): lax.psum(jnp.dot(codes, dec_flat, preferred_element_type=jnp.float32), 'l...  242 us
    psum x1, waiting for transfers between devices, body(): back = lax.psum(partial_back, 'layer')  142 us
    psum x1, waiting for transfers between devices, body(): pre, norms = lax.psum((partial_pre, local_norms), 'layer')  136 us
    psum x1, blocking collectives, body(): pre, norms = lax.psum((partial_pre, local_norms), 'layer')  26.5 us
  transfers between devices with their start and end apart: 3, of which 3 were waited for; matrix products, arithmetic and copies ran while one was open for 1% of the time, Pallas kernels for 0%

commit v1 on v0

v1 whole, which is shorter than its diff:
```python
import jax
import jax.numpy as jnp
from jax import lax
from jax.sharding import PartitionSpec as P

loss_scale = 0.0625
sparsity = 0.25
bf16 = jnp.bfloat16
f32 = jnp.float32


def layer_perm(dy, flip):
    return [(i, (((i // 2) + dy) % 4) * 2 + ((i % 2) ^ flip)) for i in range(8)]


def latent_perm(dx=0, zxor=0, cxor=0):
    out = []
    for i in range(32):
        z, x, c = i // 8, (i // 2) % 4, i % 2
        out.append((i, ((z ^ zxor) * 4 + (x + dx) % 4) * 2 + (c ^ cxor)))
    return out


def shift_y(v, k):
    return lax.ppermute(v, "layer", layer_perm(k, 0))


def swap_h(v):
    return lax.ppermute(v, "layer", layer_perm(0, 1))


def shift_x(v, k):
    return lax.ppermute(v, "latent", latent_perm(dx=k))


def xor_z(v, k):
    return lax.ppermute(v, "latent", latent_perm(zxor=k))


def swap_c(v):
    return lax.ppermute(v, "latent", latent_perm(cxor=1))


def block(v, index, size, axis):
    return lax.dynamic_slice_in_dim(v, index * size, size, axis)


def roll_blocks(v, shift, axis):
    return lax.dynamic_slice_in_dim(
        jnp.concatenate([v, v], axis), shift, v.shape[axis], axis
    )


def dot(a, b):
    return jnp.dot(a, b, preferred_element_type=f32)


def dot_t(a, b):
    return lax.dot_general(a, b, (((1,), (1,)), ((), ())), preferred_element_type=f32)


def body(acts, mask, w_enc, b_enc, w_dec, b_dec):
    rows, _, width = acts.shape
    latents = w_enc.shape[2]
    ny, nx, nz = 4, 4, 4
    rb = rows // ny
    r = rb // nx
    half = width // 2
    q = half // nz
    y = lax.axis_index("layer") // 2
    la = lax.axis_index("latent")
    z, x, c = la // 8, (la // 2) % 4, la % 2

    flat = acts.reshape(rows, width)
    enc = w_enc.reshape(width, latents)
    dec = w_dec.reshape(latents, width)

    dec_own = block(dec, c, half, 1)
    dec_other = swap_c(block(dec, 1 - c, half, 1))

    partial = dot(flat, enc)
    got = [shift_y(block(partial, (y + k) % ny, rb, 0).astype(bf16), k) for k in (2, 1, 3)]
    mine = block(partial, y, rb, 0)
    for g in got:
        mine = mine + g.astype(f32)
    pre = mine + swap_h(mine.astype(bf16)).astype(f32) + b_enc[None, :]
    active = block(mask, y, rb, 0).astype(f32)
    shard = (active * pre).astype(bf16)
    shard = roll_blocks(shard.reshape(nx, r, latents), x, 0)
    codes = [shard] + [shift_y(shard, -k) for k in (1, 2, 3)]
    codes = jnp.stack(codes)
    codes_other = swap_c(codes)

    def piece(k):
        return dot(codes[:, k].reshape(rb, latents), dec_own) + dot(
            codes_other[:, k].reshape(rb, latents), dec_other
        )

    got = [shift_x(piece(k).astype(bf16), k) for k in (2, 1, 3)]
    total = piece(0)
    for g in got:
        total = total + g.astype(f32)
    got = [xor_z(block(total, z ^ k, q, 1).astype(bf16), k) for k in (3, 2, 1)]
    recon = block(total, z, q, 1)
    for g in got:
        recon = recon + g.astype(f32)
    column = c * half + z * q
    acts_here = lax.dynamic_slice(flat.reshape(ny, nx, r, width), (0, x, 0, column), (ny, 1, r, q))
    acts_here = roll_blocks(acts_here, y, 0).reshape(rb, q).astype(f32)
    bias_here = lax.dynamic_slice(b_dec, (0, column), (1, q))
    error = (recon + bias_here - acts_here).astype(bf16)
    parts = [error] + [xor_z(error, k) for k in (1, 2, 3)]
    spread = []
    for m in range(nz):
        v = parts[0]
        for k in (1, 2, 3):
            v = jnp.where((z ^ k) == m, parts[k], v)
        spread.append(v)
    error = jnp.concatenate(spread, axis=1)
    errors = [error] + [shift_x(error, -k) for k in (1, 2, 3)]
    others = [swap_c(e) for e in errors]
    first = c == 0
    errors = [
        jnp.concatenate([jnp.where(first, e, o), jnp.where(first, o, e)], axis=1)
        for e, o in zip(errors, others)
    ]

    wide = dec.astype(f32)
    lengths = jnp.sqrt(jnp.sum(wide * wide, axis=1) + 1e-06)
    back = jnp.stack([dot_t(e, dec).reshape(ny, r, latents) for e in errors], axis=1)
    back = back + sparsity * lengths
    got = [shift_y(back[k].astype(bf16), k) for k in (2, 1, 3)]
    mine = back[0]
    for g in got:
        mine = mine + g.astype(f32)
    mine = mine + swap_h(mine.astype(bf16)).astype(f32)
    active_rolled = roll_blocks(active.reshape(nx, r, latents), x, 0)
    shard = (loss_scale * active_rolled * mine).astype(bf16)
    dpre = jnp.concatenate([shard] + [shift_y(shard, -k) for k in (1, 2, 3)])
    dpre = dpre.reshape(rows, latents)

    acts_rolled = flat.reshape(ny, nx, r, width)
    acts_rolled = roll_blocks(roll_blocks(acts_rolled, y, 0), x, 1).reshape(rows, width)
    grad_enc = lax.dot_general(
        acts_rolled, dpre, (((0,), (0,)), ((), ())), preferred_element_type=f32
    )
    grad_enc = grad_enc.astype(bf16).reshape(w_enc.shape)

    usage = jnp.sum(codes.astype(f32), axis=(0, 1, 2))
    codes_x = codes.swapaxes(0, 1).reshape(rows, latents)
    cross = lax.dot_general(
        codes_x, jnp.concatenate(errors), (((0,), (0,)), ((), ())), preferred_element_type=f32
    )
    grad_dec = loss_scale * (cross + (sparsity * usage / lengths)[:, None] * wide)
    return (grad_enc, grad_dec.astype(bf16).reshape(w_dec.shape))


def solution(mesh):
    return jax.shard_map(
        body,
        mesh=mesh,
        in_specs=(
            P(None, "layer", None),
            P(None, "latent"),
            P("layer", None, "latent"),
            P("latent"),
            P("latent", "layer", None),
            P("layer", None),
        ),
        out_specs=(P("layer", None, "latent"), P("latent", "layer", None)),
        check_vma=False,
    )
```

time: 596 us -> 142 us (0.24)
  waiting for transfers between devices: 520 us -> 51 us
  starting transfers between devices: 0.12 us -> 47.3 us
  blocking collectives: 26.5 us -> 0 us
  between operations: 13.8 us -> 1.09 us
  matrix products: 19.4 us -> 25.6 us
    psum x3 -> x0, waiting for transfers between devices: 520 us -> none  [the longest x1 242 us: body(): lax.psum(jnp.dot(codes, dec_flat, preferred_element_type=jnp.float32), 'l...]
    ppermute x0 -> x32, waiting for transfers between devices: none -> 51 us  [the longest x12 17.3 us: shift_y(): return lax.ppermute(v, 'layer', layer_perm(k, 0))]
    ppermute x0 -> x32, starting transfers between devices: none -> 47.3 us  [the longest x12 16.8 us: shift_y(): return lax.ppermute(v, 'layer', layer_perm(k, 0))]
    psum x1 -> x0, blocking collectives: 26.5 us -> none  [body(): pre, norms = lax.psum((partial_pre, local_norms), 'layer')]
    dot_general x5 -> x15, matrix products: 19.4 us -> 25.6 us  [the longest x9 9.84 us: dot(): return jnp.dot(a, b, preferred_element_type=f32)]
  transfers between devices with their start and end apart: 3 -> 32, of which waited for: 3 -> 24; matrix products, arithmetic and copies ran while one was open for 1% -> 21% of each run, Pallas kernels for 0% -> 0%
where the time goes in v1:
time: 142 us
  waiting for transfers between devices  51 us (36%)
  starting transfers between devices  47.3 us (33%)
  matrix products  25.6 us (18%)
  other arithmetic  9.24 us (7%)
  local copies, waits for them, and re-layouts  7.64 us (5%)
    ppermute x12, waiting for transfers between devices, shift_y(): return lax.ppermute(v, 'layer', layer_perm(k, 0))  17.3 us
    ppermute x12, starting transfers between devices, shift_y(): return lax.ppermute(v, 'layer', layer_perm(k, 0))  16.8 us
    ppermute x6, waiting for transfers between devices, shift_x(): return lax.ppermute(v, 'latent', latent_perm(dx=k))  13.7 us
    ppermute x6, starting transfers between devices, shift_x(): return lax.ppermute(v, 'latent', latent_perm(dx=k))  11.6 us
    ppermute x2, starting transfers between devices, swap_h(): return lax.ppermute(v, 'layer', layer_perm(0, 1))  10.9 us
    ppermute x2, waiting for transfers between devices, swap_h(): return lax.ppermute(v, 'layer', layer_perm(0, 1))  9.89 us
    dot_general x9, matrix products, dot(): return jnp.dot(a, b, preferred_element_type=f32)  9.84 us
    dot_general x1, matrix products, body(): lax.dot_general(codes_x, jnp.concatenate(errors), (((0,), (0,)), ((), ())...  9.75 us
  transfers between devices with their start and end apart: 32, of which 24 were waited for; matrix products, arithmetic and copies ran while one was open for 21% of the time, Pallas kernels for 0%

profile of v1, /device:TPU:32, one launch (start us, length us, event | category | flops | bytes accessed | tf_op | source)
XLA Modules:
  0.0 141.9 jit_solution(793120706366058159)
XLA Ops:
  0.7 1.5 %copy-done = bf16[1,2048,512]{2,1,0:T(8,128)(2,1)S(1)} copy-done((bf16[1,2048,512]{2,1,0:T(8,128)(2,1)S(1)}, bf16[1,2048,512]{2,1,0:T(8,128)(2,1)}, u32[]{:S(2)}) %copy-start) | copy-done | bytes 2097176
  2.2 2.8 %fusion.31 = f32[512,512]{1,0:T(8,128)S(1)} fusion(bf16[1,2048,512]{2,1,0:T(8,128)(2,1)S(1)} %copy-done, bf16[512,1,2048]{2,0,1:T(8,128)(2,1)} %param.6), kind=kOutput, calls=%fused_computation.38 | convolution fusion | flops 1073741824 | bytes 5242880 | tf_op jit(solution)/shard_map/dot_general | solution.py:55
  5.9 3.2 %collective-permute-start = (bf16[128,512]{1,0:T(8,128)(2,1)}, bf16[128,512]{1,0:T(8,128)(2,1)S(1)}, u32[]{:S(2)}, u32[]{:S(2)}) collective-permute-start(bf16[128,512]{1,0:T(8,128)(2,1)} %get-tuple-element.8), channel_id=1, source_target_pairs={{0,128},{32,160},{64,192},{96,224},{128,0},{160,32},{192,64},{224,... | collective-permute-start | bytes 393224 | tf_op jit(solution)/shard_map/ppermute | solution.py:25
  9.1 1.1 collective-permute-start.2
  10.2 1.0 collective-permute-start.1
  11.2 2.4 %collective-permute-done = bf16[128,512]{1,0:T(8,128)(2,1)S(1)} collective-permute-done((bf16[128,512]{1,0:T(8,128)(2,1)}, bf16[128,512]{1,0:T(8,128)(2,1)S(1)}, u32[]{:S(2)}, u32[]{:S(2)}) %collective-permute-start) | collective-permute-done | bytes 131104 | tf_op jit(solution)/shard_map/ppermute | solution.py:25
  13.6 2.5 %collective-permute-done.2 = bf16[128,512]{1,0:T(8,128)(2,1)S(1)} collective-permute-done((bf16[128,512]{1,0:T(8,128)(2,1)}, bf16[128,512]{1,0:T(8,128)(2,1)S(1)}, u32[]{:S(2)}, u32[]{:S(2)}) %collective-permute-start.2) | collective-permute-done | bytes 131104 | tf_op jit(solution)/shard_map/ppermute | solution.py:25
  17.3 6.3 %collective-permute-start.3 = (bf16[128,512]{1,0:T(8,128)(2,1)}, bf16[128,512]{1,0:T(8,128)(2,1)}, u32[]{:S(2)}, u32[]{:S(2)}) collective-permute-start(bf16[128,512]{1,0:T(8,128)(2,1)} %fusion.79), channel_id=1, source_target_pairs={{0,32},{32,0},{64,96},{96,64},{128,160},{160,128},{192,224},{224,1... | collective-permute-start | bytes 393224 | tf_op jit(solution)/shard_map/ppermute | solution.py:29
  23.6 2.3 %dynamic-slice_bitcast_fusion = bf16[512,1024]{1,0:T(8,128)(2,1)} fusion(bf16[512,1,2048]{2,0,1:T(8,128)(2,1)} %param.10, s32[]{:T(128)S(6)} %select_n.207), kind=kLoop, calls=%fused_computation.65 | loop fusion | bytes 2097156 | tf_op jit(solution)/shard_map/dynamic_slice | solution.py:45
  25.9 3.0 %collective-permute-done.3 = bf16[128,512]{1,0:T(8,128)(2,1)} collective-permute-done((bf16[128,512]{1,0:T(8,128)(2,1)}, bf16[128,512]{1,0:T(8,128)(2,1)}, u32[]{:S(2)}, u32[]{:S(2)}) %collective-permute-start.3) | collective-permute-done | bytes 131104 | tf_op jit(solution)/shard_map/ppermute | solution.py:29
  28.9 1.4 multiply_convert_fusion
  31.0 3.6 %collective-permute-start.4 = (bf16[4,32,512]{2,1,0:T(8,128)(2,1)}, bf16[4,32,512]{2,1,0:T(8,128)(2,1)}, u32[]{:S(2)}, u32[]{:S(2)}) collective-permute-start(bf16[4,32,512]{2,1,0:T(8,128)(2,1)} %fusion.71), channel_id=1, source_target_pairs={{0,192},{32,224},{64,0},{96,32},{128,64},{160,96},{192,128},{224,1... | collective-permute-start | bytes 393224 | tf_op jit(solution)/shard_map/ppermute | solution.py:25
  36.0 1.5 %dynamic-slice_bitcast_fusion.1 = bf16[4,1,32,256]{3,2,0,1:T(8,128)(2,1)} fusion(bf16[4,4,32,2048]{3,2,1,0:T(8,128)(2,1)} %bitcast.127, s32[]{:T(128)S(6)} %select_n.213, s32[]{:T(128)S(6)} %select_n.212), kind=kLoop, calls=%fused_computation.119 | loop fusion | bytes 131080
  37.5 1.4 collective-permute-done.4
  38.9 2.7 %collective-permute-done.5 = bf16[4,32,512]{2,1,0:T(8,128)(2,1)} collective-permute-done((bf16[4,32,512]{2,1,0:T(8,128)(2,1)}, bf16[4,32,512]{2,1,0:T(8,128)(2,1)}, u32[]{:S(2)}, u32[]{:S(2)}) %collective-permute-start.5) | collective-permute-done | bytes 131104 | tf_op jit(solution)/shard_map/ppermute | solution.py:25
  41.5 1.3 collective-permute-done.6
  42.8 1.2 convert_reduce_fusion
  46.7 1.0 fusion.37
  47.8 3.0 %collective-permute-start.9 = (bf16[128,1024]{1,0:T(8,128)(2,1)}, bf16[128,1024]{1,0:T(8,128)(2,1)}, u32[]{:S(2)}, u32[]{:S(2)}) collective-permute-start(bf16[128,1024]{1,0:T(8,128)(2,1)} %fusion.37), channel_id=1, source_target_pairs={{0,4},{1,5},{2,6},{3,7},{4,0},{5,1},{6,2},{7,3},{8,12},{9,13},{10,... | collective-permute-start | bytes 786440 | tf_op jit(solution)/shard_map/ppermute | solution.py:33
  50.8 1.0 fusion.38
  52.4 1.0 fusion.39
  53.4 2.6 %collective-permute-start.11 = (bf16[128,1024]{1,0:T(8,128)(2,1)}, bf16[128,1024]{1,0:T(8,128)(2,1)}, u32[]{:S(2)}, u32[]{:S(2)}) collective-permute-start(bf16[128,1024]{1,0:T(8,128)(2,1)} %fusion.39), channel_id=1, source_target_pairs={{0,6},{1,7},{2,0},{3,1},{4,2},{5,3},{6,4},{7,5},{8,14},{9,15},{10,... | collective-permute-start | bytes 786440 | tf_op jit(solution)/shard_map/ppermute | solution.py:33
  56.7 1.5 %fusion.58 = f32[128,1024]{1,0:T(8,128)S(1)} fusion(bf16[128,512]{1,0:T(8,128)(2,1)S(1)} %bitcast.139, bf16[512,1,2048]{2,0,1:T(8,128)(2,1)} %param.10, s32[]{:T(128)S(6)} %select_n.206), kind=kOutput, calls=%fused_computation.62 | convolution fusion | flops 134217728 | bytes 1703940 | tf_op jit(solution)/shard_map/dot_general | solution.py:55
  58.7 4.8 %collective-permute-done.10 = bf16[128,1024]{1,0:T(8,128)(2,1)} collective-permute-done((bf16[128,1024]{1,0:T(8,128)(2,1)}, bf16[128,1024]{1,0:T(8,128)(2,1)}, u32[]{:S(2)}, u32[]{:S(2)}) %collective-permute-start.10) | collective-permute-done | bytes 262176 | tf_op jit(solution)/shard_map/ppermute | solution.py:33
  63.6 1.5 %fusion.36 = f32[128,1024]{1,0:T(8,128)S(1)} fusion(f32[128,1024]{1,0:T(8,128)S(1)} %fusion.58, bf16[128,512]{1,0:T(8,128)(2,1)} %bitcast.140, bf16[512,1024]{1,0:T(8,128)(2,1)S(1)} %collective-permute-done.8, bf16[128,1024]{1,0:T(8,128)(2,1)} %collective-permute-done.11, bf16[128,1024]{1,0:T(8,128)(2,1)} %collective-permute-done.10, ...), kind=kOutput, calls=%fused_computation.47 | convolution fusion | flops 135135232 | bytes 3014656 | tf_op jit(solution)/shard_map/dot_general | solution.py:55
  65.2 2.4 %collective-permute-start.12 = (bf16[128,256]{1,0:T(8,128)(2,1)S(1)}, bf16[128,256]{1,0:T(8,128)(2,1)S(1)}, u32[]{:S(2)}, u32[]{:S(2)}) collective-permute-start(bf16[128,256]{1,0:T(8,128)(2,1)S(1)} %get-tuple-element.22), channel_id=1, source_target_pairs={{0,24},{1,25},{2,26},{3,27},{4,28},{5,29},{6,30},{7,31},{8,16},{9,... | collective-permute-start | bytes 196616 | tf_op jit(solution)/shard_map/ppermute | solution.py:37
  67.6 1.6 %collective-permute-start.13 = (bf16[128,256]{1,0:T(8,128)(2,1)S(1)}, bf16[128,256]{1,0:T(8,128)(2,1)S(1)}, u32[]{:S(2)}, u32[]{:S(2)}) collective-permute-start(bf16[128,256]{1,0:T(8,128)(2,1)S(1)} %get-tuple-element.24), channel_id=1, source_target_pairs={{0,16},{1,17},{2,18},{3,19},{4,20},{5,21},{6,22},{7,23},{8,24},{9,... | collective-permute-start | bytes 196616 | tf_op jit(solution)/shard_map/ppermute | solution.py:37
  70.7 1.3 collective-permute-done.14
  72.0 0.9 collective-permute-done.13
  73.0 2.4 %collective-permute-start.17 = (bf16[128,256]{1,0:T(8,128)(2,1)S(1)}, bf16[128,256]{1,0:T(8,128)(2,1)S(1)}, u32[]{:S(2)}, u32[]{:S(2)}) collective-permute-start(bf16[128,256]{1,0:T(8,128)(2,1)S(1)} %fusion.72), channel_id=1, source_target_pairs={{0,8},{1,9},{2,10},{3,11},{4,12},{5,13},{6,14},{7,15},{8,0},{9,1},... | collective-permute-start | bytes 196616 | tf_op jit(solution)/shard_map/ppermute | solution.py:37
  77.6 3.3 %collective-permute-done.16 = bf16[128,256]{1,0:T(8,128)(2,1)S(1)} collective-permute-done((bf16[128,256]{1,0:T(8,128)(2,1)S(1)}, bf16[128,256]{1,0:T(8,128)(2,1)S(1)}, u32[]{:S(2)}, u32[]{:S(2)}) %collective-permute-start.16) | collective-permute-done | bytes 65568 | tf_op jit(solution)/shard_map/ppermute | solution.py:37
  80.9 2.2 %collective-permute-done.15 = bf16[128,256]{1,0:T(8,128)(2,1)S(1)} collective-permute-done((bf16[128,256]{1,0:T(8,128)(2,1)S(1)}, bf16[128,256]{1,0:T(8,128)(2,1)S(1)}, u32[]{:S(2)}, u32[]{:S(2)}) %collective-permute-start.15) | collective-permute-done | bytes 65568 | tf_op jit(solution)/shard_map/ppermute | solution.py:37
  83.2 3.2 %collective-permute-start.21 = (bf16[128,1024]{1,0:T(8,128)(2,1)S(1)}, bf16[128,1024]{1,0:T(8,128)(2,1)S(1)}, u32[]{:S(2)}, u32[]{:S(2)}) collective-permute-start(bf16[128,1024]{1,0:T(8,128)(2,1)S(1)} %pad_maximum_fusion.6), channel_id=1, source_target_pairs={{0,4},{1,5},{2,6},{3,7},{4,0},{5,1},{6,2},{7,3},{8,12},{9,13},{10,... | collective-permute-start | bytes 786440 | tf_op jit(solution)/shard_map/ppermute | solution.py:33
  86.4 2.1 %fusion = f32[512]{0:T(512)S(1)} fusion(bf16[512,1,2048]{2,0,1:T(8,128)(2,1)} %param.10), kind=kLoop, calls=%fused_computation.2 | loop fusion | flops 3145216 | bytes 2099200 | tf_op jit(solution)/shard_map/reduce_sum | solution.py:129
  88.5 0.9 collective-permute-start.19
  89.4 1.2 collective-permute-start.23
  91.5 5.8 %collective-permute-done.19 = bf16[128,1024]{1,0:T(8,128)(2,1)S(1)} collective-permute-done((bf16[128,1024]{1,0:T(8,128)(2,1)S(1)}, bf16[128,1024]{1,0:T(8,128)(2,1)S(1)}, u32[]{:S(2)}, u32[]{:S(2)}) %collective-permute-start.19) | collective-permute-done | bytes 262176 | tf_op jit(solution)/shard_map/ppermute | solution.py:33
  97.3 1.8 %collective-permute-done.23 = bf16[128,1024]{1,0:T(8,128)(2,1)S(1)} collective-permute-done((bf16[128,1024]{1,0:T(8,128)(2,1)S(1)}, bf16[128,1024]{1,0:T(8,128)(2,1)S(1)}, u32[]{:S(2)}, u32[]{:S(2)}) %collective-permute-start.23) | collective-permute-done | bytes 262176 | tf_op jit(solution)/shard_map/ppermute | solution.py:33
  103.0 1.0 collective-permute-start.25
  104.0 1.2 collective-permute-start.27
  106.8 4.1 %collective-permute-done.25 = bf16[4,32,512]{2,1,0:T(8,128)(2,1)S(1)} collective-permute-done((bf16[4,32,512]{2,1,0:T(8,128)(2,1)S(1)}, bf16[4,32,512]{2,1,0:T(8,128)(2,1)S(1)}, u32[]{:S(2)}, u32[]{:S(2)}) %collective-permute-start.25) | collective-permute-done | bytes 131104 | tf_op jit(solution)/shard_map/ppermute | solution.py:25
  111.2 2.1 %collective-permute-done.26 = bf16[4,32,512]{2,1,0:T(8,128)(2,1)S(1)} collective-permute-done((bf16[4,32,512]{2,1,0:T(8,128)(2,1)S(1)}, bf16[4,32,512]{2,1,0:T(8,128)(2,1)S(1)}, u32[]{:S(2)}, u32[]{:S(2)}) %collective-permute-start.26) | collective-permute-done | bytes 131104 | tf_op jit(solution)/shard_map/ppermute | solution.py:25
  113.4 4.6 %collective-permute-start.28 = (bf16[4,32,512]{2,1,0:T(8,128)(2,1)S(1)}, bf16[4,32,512]{2,1,0:T(8,128)(2,1)S(1)}, u32[]{:S(2)}, u32[]{:S(2)}) collective-permute-start(bf16[4,32,512]{2,1,0:T(8,128)(2,1)S(1)} %fusion.78), channel_id=1, source_target_pairs={{0,32},{32,0},{64,96},{96,64},{128,160},{160,128},{192,224},{224,1... | collective-permute-start | bytes 393224 | tf_op jit(solution)/shard_map/ppermute | solution.py:29
  118.8 6.9 %collective-permute-done.28 = bf16[4,32,512]{2,1,0:T(8,128)(2,1)S(1)} collective-permute-done((bf16[4,32,512]{2,1,0:T(8,128)(2,1)S(1)}, bf16[4,32,512]{2,1,0:T(8,128)(2,1)S(1)}, u32[]{:S(2)}, u32[]{:S(2)}) %collective-permute-start.28) | collective-permute-done | bytes 131104 | tf_op jit(solution)/shard_map/ppermute | solution.py:29
  125.9 2.1 %collective-permute-start.30 = (bf16[4,32,512]{2,1,0:T(8,128)(2,1)S(1)}, bf16[4,32,512]{2,1,0:T(8,128)(2,1)S(1)}, u32[]{:S(2)}, u32[]{:S(2)}) collective-permute-start(bf16[4,32,512]{2,1,0:T(8,128)(2,1)S(1)} %fusion.67), channel_id=1, source_target_pairs={{0,128},{32,160},{64,192},{96,224},{128,0},{160,32},{192,64},{224,... | collective-permute-start | bytes 393224 | tf_op jit(solution)/shard_map/ppermute | solution.py:25
  128.0 1.5 %collective-permute-start.29 = (bf16[4,32,512]{2,1,0:T(8,128)(2,1)S(1)}, bf16[4,32,512]{2,1,0:T(8,128)(2,1)S(1)}, u32[]{:S(2)}, u32[]{:S(2)}) collective-permute-start(bf16[4,32,512]{2,1,0:T(8,128)(2,1)S(1)} %fusion.67), channel_id=1, source_target_pairs={{0,192},{32,224},{64,0},{96,32},{128,64},{160,96},{192,128},{224,1... | collective-permute-start | bytes 393224 | tf_op jit(solution)/shard_map/ppermute | solution.py:25
  129.5 9.7 %fusion.5 = bf16[512,1,2048]{2,0,1:T(8,128)(2,1)} fusion(bf16[512,512]{1,0:T(8,128)(2,1)S(1)} %bitcast.130, bf16[128,1024]{1,0:T(8,128)(2,1)S(1)} %get-tuple-element.21, bf16[128,1024]{1,0:T(8,128)(2,1)S(1)} %get-tuple-element.20, bf16[128,1024]{1,0:T(8,128)(2,1)S(1)} %get-tuple-element.19, bf16[128,1024]{1,0:T(8,128)(2,1)S(1)} %get-tuple-element.18, ...), kind=kOutput, calls=%fused_computation.12 | convolution fusion | flops 1095761920 | bytes 6817792 | tf_op jit(solution)/shard_map/dot_general | solution.py:151
  139.3 2.6 %fusion.4 = bf16[1,2048,512]{2,1,0:T(8,128)(2,1)} fusion(bf16[512,2048]{1,0:T(8,128)(2,1)S(1)} %bitcast.129, bf16[512,512]{1,0:T(8,128)(2,1)S(1)} %bitcast.138), kind=kOutput, calls=%fused_computation.11 | convolution fusion | flops 1074790400 | bytes 4718592 | tf_op jit(solution)/shard_map/dot_general | solution.py:144
  (90 shorter events, 20.4 us)
Async XLA Ops:
  0.6 1.6 %copy-start = (bf16[1,2048,512]{2,1,0:T(8,128)(2,1)S(1)}, bf16[1,2048,512]{2,1,0:T(8,128)(2,1)}, u32[]{:S(2)}) copy-start(bf16[1,2048,512]{2,1,0:T(8,128)(2,1)} %param.8) | copy-start | bytes 6291460
  5.1 18.5 %copy-start.6 = (f32[512,512]{1,0:T(8,128)}, f32[512,512]{1,0:T(8,128)S(1)}, u32[]{:S(2)}) copy-start(f32[512,512]{1,0:T(8,128)S(1)} %fusion.31) | copy-start | bytes 3145732
  5.1 23.8 %copy-start.12 = (f32[512]{0:T(512)S(1)}, f32[512]{0:T(512)}, u32[]{:S(2)}) copy-start(f32[512]{0:T(512)} %param.9) | copy-start | bytes 6148
  5.9 7.6 %collective-permute-start = (bf16[128,512]{1,0:T(8,128)(2,1)}, bf16[128,512]{1,0:T(8,128)(2,1)S(1)}, u32[]{:S(2)}, u32[]{:S(2)}) collective-permute-start(bf16[128,512]{1,0:T(8,128)(2,1)} %get-tuple-element.8), channel_id=1, source_target_pairs={{0,128},{32,160},{64,192},{96,224},{128,0},{160,32},{192,64},{224,... | collective-permute-start | bytes 393224 | tf_op jit(solution)/shard_map/ppermute | solution.py:25
  9.1 6.9 %collective-permute-start.2 = (bf16[128,512]{1,0:T(8,128)(2,1)}, bf16[128,512]{1,0:T(8,128)(2,1)S(1)}, u32[]{:S(2)}, u32[]{:S(2)}) collective-permute-start(bf16[128,512]{1,0:T(8,128)(2,1)} %get-tuple-element.9), channel_id=1, source_target_pairs={{0,192},{32,224},{64,0},{96,32},{128,64},{160,96},{192,128},{224,1... | collective-permute-start | bytes 393224 | tf_op jit(solution)/shard_map/ppermute | solution.py:25
  10.2 6.4 %collective-permute-start.1 = (bf16[128,512]{1,0:T(8,128)(2,1)}, bf16[128,512]{1,0:T(8,128)(2,1)S(1)}, u32[]{:S(2)}, u32[]{:S(2)}) collective-permute-start(bf16[128,512]{1,0:T(8,128)(2,1)} %get-tuple-element.10), channel_id=1, source_target_pairs={{0,64},{32,96},{64,128},{96,160},{128,192},{160,224},{192,0},{224,... | collective-permute-start | bytes 393224 | tf_op jit(solution)/shard_map/ppermute | solution.py:25
  13.6 10.0 %copy-start.7 = (bf16[128,512]{1,0:T(8,128)(2,1)}, bf16[128,512]{1,0:T(8,128)(2,1)S(1)}, u32[]{:S(2)}) copy-start(bf16[128,512]{1,0:T(8,128)(2,1)S(1)} %collective-permute-done) | copy-start | bytes 393220
  16.1 7.6 %copy-start.8 = (bf16[128,512]{1,0:T(8,128)(2,1)}, bf16[128,512]{1,0:T(8,128)(2,1)S(1)}, u32[]{:S(2)}) copy-start(bf16[128,512]{1,0:T(8,128)(2,1)S(1)} %collective-permute-done.2) | copy-start | bytes 393220
  16.6 9.3 %copy-start.9 = (bf16[128,512]{1,0:T(8,128)(2,1)}, bf16[128,512]{1,0:T(8,128)(2,1)S(1)}, u32[]{:S(2)}) copy-start(bf16[128,512]{1,0:T(8,128)(2,1)S(1)} %collective-permute-done.1) | copy-start | bytes 393220
  17.3 11.6 %collective-permute-start.3 = (bf16[128,512]{1,0:T(8,128)(2,1)}, bf16[128,512]{1,0:T(8,128)(2,1)}, u32[]{:S(2)}, u32[]{:S(2)}) collective-permute-start(bf16[128,512]{1,0:T(8,128)(2,1)} %fusion.79), channel_id=1, source_target_pairs={{0,32},{32,0},{64,96},{96,64},{128,160},{160,128},{192,224},{224,1... | collective-permute-start | bytes 393224 | tf_op jit(solution)/shard_map/ppermute | solution.py:29
  25.9 20.9 %collective-permute-start.8 = (bf16[512,1024]{1,0:T(8,128)(2,1)}, bf16[512,1024]{1,0:T(8,128)(2,1)S(1)}, u32[]{:S(2)}, u32[]{:S(2)}) collective-permute-start(bf16[512,1024]{1,0:T(8,128)(2,1)} %dynamic-slice_bitcast_fusion), channel_id=1, source_target_pairs={{0,1},{1,0},{2,3},{3,2},{4,5},{5,4},{6,7},{7,6},{8,9},{9,8},{10,11... | collective-permute-start | bytes 3145736 | tf_op jit(solution)/shard_map/ppermute | solution.py:41
  31.0 7.9 %collective-permute-start.4 = (bf16[4,32,512]{2,1,0:T(8,128)(2,1)}, bf16[4,32,512]{2,1,0:T(8,128)(2,1)}, u32[]{:S(2)}, u32[]{:S(2)}) collective-permute-start(bf16[4,32,512]{2,1,0:T(8,128)(2,1)} %fusion.71), channel_id=1, source_target_pairs={{0,192},{32,224},{64,0},{96,32},{128,64},{160,96},{192,128},{224,1... | collective-permute-start | bytes 393224 | tf_op jit(solution)/shard_map/ppermute | solution.py:25
  34.6 6.9 %collective-permute-start.5 = (bf16[4,32,512]{2,1,0:T(8,128)(2,1)}, bf16[4,32,512]{2,1,0:T(8,128)(2,1)}, u32[]{:S(2)}, u32[]{:S(2)}) collective-permute-start(bf16[4,32,512]{2,1,0:T(8,128)(2,1)} %fusion.71), channel_id=1, source_target_pairs={{0,128},{32,160},{64,192},{96,224},{128,0},{160,32},{192,64},{224,... | collective-permute-start | bytes 393224 | tf_op jit(solution)/shard_map/ppermute | solution.py:25
  35.3 7.5 %collective-permute-start.6 = (bf16[4,32,512]{2,1,0:T(8,128)(2,1)}, bf16[4,32,512]{2,1,0:T(8,128)(2,1)}, u32[]{:S(2)}, u32[]{:S(2)}) collective-permute-start(bf16[4,32,512]{2,1,0:T(8,128)(2,1)} %fusion.71), channel_id=1, source_target_pairs={{0,64},{32,96},{64,128},{96,160},{128,192},{160,224},{192,0},{224,... | collective-permute-start | bytes 393224 | tf_op jit(solution)/shard_map/ppermute | solution.py:25
  37.4 6.7 %copy-start.1 = (bf16[512,1,2048]{2,0,1:T(8,128)(2,1)S(1)}, bf16[512,1,2048]{2,0,1:T(8,128)(2,1)}, u32[]{:S(2)}) copy-start(bf16[512,1,2048]{2,0,1:T(8,128)(2,1)} %param.10) | copy-start | bytes 6291460
  44.0 0.8 copy-start.4
  44.1 2.0 %collective-permute-start.7 = (bf16[4,4,32,512]{3,2,0,1:T(8,128)(2,1)S(1)}, bf16[4,4,32,512]{3,2,0,1:T(8,128)(2,1)S(1)}, u32[]{:S(2)}, u32[]{:S(2)}) collective-permute-start(bf16[4,4,32,512]{3,2,0,1:T(8,128)(2,1)S(1)} %get-tuple-element.3), channel_id=1, source_target_pairs={{0,1},{1,0},{2,3},{3,2},{4,5},{5,4},{6,7},{7,6},{8,9},{9,8},{10,11... | collective-permute-start | bytes 1572872 | tf_op jit(solution)/shard_map/ppermute | solution.py:41
  47.8 8.3 %copy-start.10 = (bf16[4,1,32,256]{3,2,0,1:T(8,128)(2,1)S(1)}, bf16[4,1,32,256]{3,2,0,1:T(8,128)(2,1)}, u32[]{:S(2)}) copy-start(bf16[4,1,32,256]{3,2,0,1:T(8,128)(2,1)} %dynamic-slice_bitcast_fusion.1) | copy-start | bytes 196612
  47.8 11.0 %collective-permute-start.9 = (bf16[128,1024]{1,0:T(8,128)(2,1)}, bf16[128,1024]{1,0:T(8,128)(2,1)}, u32[]{:S(2)}, u32[]{:S(2)}) collective-permute-start(bf16[128,1024]{1,0:T(8,128)(2,1)} %fusion.37), channel_id=1, source_target_pairs={{0,4},{1,5},{2,6},{3,7},{4,0},{5,1},{6,2},{7,3},{8,12},{9,13},{10,... | collective-permute-start | bytes 786440 | tf_op jit(solution)/shard_map/ppermute | solution.py:33
  51.8 11.8 %collective-permute-start.10 = (bf16[128,1024]{1,0:T(8,128)(2,1)}, bf16[128,1024]{1,0:T(8,128)(2,1)}, u32[]{:S(2)}, u32[]{:S(2)}) collective-permute-start(bf16[128,1024]{1,0:T(8,128)(2,1)} %fusion.38), channel_id=1, source_target_pairs={{0,2},{1,3},{2,4},{3,5},{4,6},{5,7},{6,0},{7,1},{8,10},{9,11},{10,... | collective-permute-start | bytes 786440 | tf_op jit(solution)/shard_map/ppermute | solution.py:33
  53.4 10.2 %collective-permute-start.11 = (bf16[128,1024]{1,0:T(8,128)(2,1)}, bf16[128,1024]{1,0:T(8,128)(2,1)}, u32[]{:S(2)}, u32[]{:S(2)}) collective-permute-start(bf16[128,1024]{1,0:T(8,128)(2,1)} %fusion.39), channel_id=1, source_target_pairs={{0,6},{1,7},{2,0},{3,1},{4,2},{5,3},{6,4},{7,5},{8,14},{9,15},{10,... | collective-permute-start | bytes 786440 | tf_op jit(solution)/shard_map/ppermute | solution.py:33
  58.3 14.7 %copy-start.11 = (bf16[4,1,32,256]{3,2,0,1:T(8,128)(2,1)S(1)}, bf16[4,1,32,256]{3,2,0,1:T(8,128)(2,1)}, u32[]{:S(2)}) copy-start(bf16[4,1,32,256]{3,2,0,1:T(8,128)(2,1)} %fusion.73) | copy-start | bytes 196612
  65.2 5.5 %collective-permute-start.12 = (bf16[128,256]{1,0:T(8,128)(2,1)S(1)}, bf16[128,256]{1,0:T(8,128)(2,1)S(1)}, u32[]{:S(2)}, u32[]{:S(2)}) collective-permute-start(bf16[128,256]{1,0:T(8,128)(2,1)S(1)} %get-tuple-element.22), channel_id=1, source_target_pairs={{0,24},{1,25},{2,26},{3,27},{4,28},{5,29},{6,30},{7,31},{8,16},{9,... | collective-permute-start | bytes 196616 | tf_op jit(solution)/shard_map/ppermute | solution.py:37
  67.6 4.4 %collective-permute-start.14 = (bf16[128,256]{1,0:T(8,128)(2,1)S(1)}, bf16[128,256]{1,0:T(8,128)(2,1)S(1)}, u32[]{:S(2)}, u32[]{:S(2)}) collective-permute-start(bf16[128,256]{1,0:T(8,128)(2,1)S(1)} %get-tuple-element.23), channel_id=1, source_target_pairs={{0,8},{1,9},{2,10},{3,11},{4,12},{5,13},{6,14},{7,15},{8,0},{9,1},... | collective-permute-start | bytes 196616 | tf_op jit(solution)/shard_map/ppermute | solution.py:37
  67.6 5.3 %collective-permute-start.13 = (bf16[128,256]{1,0:T(8,128)(2,1)S(1)}, bf16[128,256]{1,0:T(8,128)(2,1)S(1)}, u32[]{:S(2)}, u32[]{:S(2)}) collective-permute-start(bf16[128,256]{1,0:T(8,128)(2,1)S(1)} %get-tuple-element.24), channel_id=1, source_target_pairs={{0,16},{1,17},{2,18},{3,19},{4,20},{5,21},{6,22},{7,23},{8,24},{9,... | collective-permute-start | bytes 196616 | tf_op jit(solution)/shard_map/ppermute | solution.py:37
  73.0 4.6 %collective-permute-start.17 = (bf16[128,256]{1,0:T(8,128)(2,1)S(1)}, bf16[128,256]{1,0:T(8,128)(2,1)S(1)}, u32[]{:S(2)}, u32[]{:S(2)}) collective-permute-start(bf16[128,256]{1,0:T(8,128)(2,1)S(1)} %fusion.72), channel_id=1, source_target_pairs={{0,8},{1,9},{2,10},{3,11},{4,12},{5,13},{6,14},{7,15},{8,0},{9,1},... | collective-permute-start | bytes 196616 | tf_op jit(solution)/shard_map/ppermute | solution.py:37
  75.3 5.5 %collective-permute-start.16 = (bf16[128,256]{1,0:T(8,128)(2,1)S(1)}, bf16[128,256]{1,0:T(8,128)(2,1)S(1)}, u32[]{:S(2)}, u32[]{:S(2)}) collective-permute-start(bf16[128,256]{1,0:T(8,128)(2,1)S(1)} %fusion.72), channel_id=1, source_target_pairs={{0,16},{1,17},{2,18},{3,19},{4,20},{5,21},{6,22},{7,23},{8,24},{9,... | collective-permute-start | bytes 196616 | tf_op jit(solution)/shard_map/ppermute | solution.py:37
  76.2 6.9 %collective-permute-start.15 = (bf16[128,256]{1,0:T(8,128)(2,1)S(1)}, bf16[128,256]{1,0:T(8,128)(2,1)S(1)}, u32[]{:S(2)}, u32[]{:S(2)}) collective-permute-start(bf16[128,256]{1,0:T(8,128)(2,1)S(1)} %fusion.72), channel_id=1, source_target_pairs={{0,24},{1,25},{2,26},{3,27},{4,28},{5,29},{6,30},{7,31},{8,16},{9,... | collective-permute-start | bytes 196616 | tf_op jit(solution)/shard_map/ppermute | solution.py:37
  83.2 8.2 %collective-permute-start.21 = (bf16[128,1024]{1,0:T(8,128)(2,1)S(1)}, bf16[128,1024]{1,0:T(8,128)(2,1)S(1)}, u32[]{:S(2)}, u32[]{:S(2)}) collective-permute-start(bf16[128,1024]{1,0:T(8,128)(2,1)S(1)} %pad_maximum_fusion.6), channel_id=1, source_target_pairs={{0,4},{1,5},{2,6},{3,7},{4,0},{5,1},{6,2},{7,3},{8,12},{9,13},{10,... | collective-permute-start | bytes 786440 | tf_op jit(solution)/shard_map/ppermute | solution.py:33
  86.4 5.0 %collective-permute-start.18 = (bf16[128,1024]{1,0:T(8,128)(2,1)S(1)}, bf16[128,1024]{1,0:T(8,128)(2,1)S(1)}, u32[]{:S(2)}, u32[]{:S(2)}) collective-permute-start(bf16[128,1024]{1,0:T(8,128)(2,1)S(1)} %pad_maximum_fusion.6), channel_id=1, source_target_pairs={{0,1},{1,0},{2,3},{3,2},{4,5},{5,4},{6,7},{7,6},{8,9},{9,8},{10,11... | collective-permute-start | bytes 786440 | tf_op jit(solution)/shard_map/ppermute | solution.py:41
  88.4 10.6 %copy-start.2 = (bf16[512,1,2048]{2,0,1:T(8,128)(2,1)S(1)}, bf16[512,1,2048]{2,0,1:T(8,128)(2,1)}, u32[]{:S(2)}) copy-start(bf16[512,1,2048]{2,0,1:T(8,128)(2,1)} %param.10) | copy-start | bytes 6291460
  88.5 8.8 %collective-permute-start.19 = (bf16[128,1024]{1,0:T(8,128)(2,1)S(1)}, bf16[128,1024]{1,0:T(8,128)(2,1)S(1)}, u32[]{:S(2)}, u32[]{:S(2)}) collective-permute-start(bf16[128,1024]{1,0:T(8,128)(2,1)S(1)} %pad_maximum_fusion.6), channel_id=1, source_target_pairs={{0,6},{1,7},{2,0},{3,1},{4,2},{5,3},{6,4},{7,5},{8,14},{9,15},{10,... | collective-permute-start | bytes 786440 | tf_op jit(solution)/shard_map/ppermute | solution.py:33
  89.4 9.6 %collective-permute-start.23 = (bf16[128,1024]{1,0:T(8,128)(2,1)S(1)}, bf16[128,1024]{1,0:T(8,128)(2,1)S(1)}, u32[]{:S(2)}, u32[]{:S(2)}) collective-permute-start(bf16[128,1024]{1,0:T(8,128)(2,1)S(1)} %pad_maximum_fusion.6), channel_id=1, source_target_pairs={{0,2},{1,3},{2,4},{3,5},{4,6},{5,7},{6,0},{7,1},{8,10},{9,11},{10,... | collective-permute-start | bytes 786440 | tf_op jit(solution)/shard_map/ppermute | solution.py:33
  91.3 8.6 %collective-permute-start.22 = (bf16[128,1024]{1,0:T(8,128)(2,1)S(1)}, bf16[128,1024]{1,0:T(8,128)(2,1)S(1)}, u32[]{:S(2)}, u32[]{:S(2)}) collective-permute-start(bf16[128,1024]{1,0:T(8,128)(2,1)S(1)} %collective-permute-done.21), channel_id=1, source_target_pairs={{0,1},{1,0},{2,3},{3,2},{4,5},{5,4},{6,7},{7,6},{8,9},{9,8},{10,11... | collective-permute-start | bytes 786440 | tf_op jit(solution)/shard_map/ppermute | solution.py:41
  97.3 3.6 %collective-permute-start.20 = (bf16[128,1024]{1,0:T(8,128)(2,1)S(1)}, bf16[128,1024]{1,0:T(8,128)(2,1)S(1)}, u32[]{:S(2)}, u32[]{:S(2)}) collective-permute-start(bf16[128,1024]{1,0:T(8,128)(2,1)S(1)} %collective-permute-done.19), channel_id=1, source_target_pairs={{0,1},{1,0},{2,3},{3,2},{4,5},{5,4},{6,7},{7,6},{8,9},{9,8},{10,11... | collective-permute-start | bytes 786440 | tf_op jit(solution)/shard_map/ppermute | solution.py:41
  99.0 2.8 %collective-permute-start.24 = (bf16[128,1024]{1,0:T(8,128)(2,1)S(1)}, bf16[128,1024]{1,0:T(8,128)(2,1)S(1)}, u32[]{:S(2)}, u32[]{:S(2)}) collective-permute-start(bf16[128,1024]{1,0:T(8,128)(2,1)S(1)} %collective-permute-done.23), channel_id=1, source_target_pairs={{0,1},{1,0},{2,3},{3,2},{4,5},{5,4},{6,7},{7,6},{8,9},{9,8},{10,11... | collective-permute-start | bytes 786440 | tf_op jit(solution)/shard_map/ppermute | solution.py:41
  102.8 3.2 %copy-start.3 = (bf16[512,1,2048]{2,0,1:T(8,128)(2,1)S(1)}, bf16[512,1,2048]{2,0,1:T(8,128)(2,1)}, u32[]{:S(2)}) copy-start(bf16[512,1,2048]{2,0,1:T(8,128)(2,1)} %param.6) | copy-start | bytes 6291460
  103.0 7.9 %collective-permute-start.25 = (bf16[4,32,512]{2,1,0:T(8,128)(2,1)S(1)}, bf16[4,32,512]{2,1,0:T(8,128)(2,1)S(1)}, u32[]{:S(2)}, u32[]{:S(2)}) collective-permute-start(bf16[4,32,512]{2,1,0:T(8,128)(2,1)S(1)} %get-tuple-element.11), channel_id=1, source_target_pairs={{0,128},{32,160},{64,192},{96,224},{128,0},{160,32},{192,64},{224,... | collective-permute-start | bytes 393224 | tf_op jit(solution)/shard_map/ppermute | solution.py:25
  104.0 7.2 %collective-permute-start.27 = (bf16[4,32,512]{2,1,0:T(8,128)(2,1)S(1)}, bf16[4,32,512]{2,1,0:T(8,128)(2,1)S(1)}, u32[]{:S(2)}, u32[]{:S(2)}) collective-permute-start(bf16[4,32,512]{2,1,0:T(8,128)(2,1)S(1)} %get-tuple-element.12), channel_id=1, source_target_pairs={{0,192},{32,224},{64,0},{96,32},{128,64},{160,96},{192,128},{224,1... | collective-permute-start | bytes 393224 | tf_op jit(solution)/shard_map/ppermute | solution.py:25
  105.2 8.2 %collective-permute-start.26 = (bf16[4,32,512]{2,1,0:T(8,128)(2,1)S(1)}, bf16[4,32,512]{2,1,0:T(8,128)(2,1)S(1)}, u32[]{:S(2)}, u32[]{:S(2)}) collective-permute-start(bf16[4,32,512]{2,1,0:T(8,128)(2,1)S(1)} %get-tuple-element.13), channel_id=1, source_target_pairs={{0,64},{32,96},{64,128},{96,160},{128,192},{160,224},{192,0},{224,... | collective-permute-start | bytes 393224 | tf_op jit(solution)/shard_map/ppermute | solution.py:25
  113.4 16.1 %copy-start.5 = (bf16[4,4,32,512]{3,2,0,1:T(8,128)(2,1)S(1)}, bf16[4,4,32,512]{3,2,0,1:T(8,128)(2,1)}, u32[]{:S(2)}) copy-start(bf16[4,4,32,512]{3,2,0,1:T(8,128)(2,1)} %copy-done.4) | copy-start | bytes 1572868
  113.4 12.3 %collective-permute-start.28 = (bf16[4,32,512]{2,1,0:T(8,128)(2,1)S(1)}, bf16[4,32,512]{2,1,0:T(8,128)(2,1)S(1)}, u32[]{:S(2)}, u32[]{:S(2)}) collective-permute-start(bf16[4,32,512]{2,1,0:T(8,128)(2,1)S(1)} %fusion.78), channel_id=1, source_target_pairs={{0,32},{32,0},{64,96},{96,64},{128,160},{160,128},{192,224},{224,1... | collective-permute-start | bytes 393224 | tf_op jit(solution)/shard_map/ppermute | solution.py:29
  125.8 13.4 %collective-permute-start.31 = (bf16[4,32,512]{2,1,0:T(8,128)(2,1)S(1)}, bf16[4,32,512]{2,1,0:T(8,128)(2,1)S(1)}, u32[]{:S(2)}, u32[]{:S(2)}) collective-permute-start(bf16[4,32,512]{2,1,0:T(8,128)(2,1)S(1)} %fusion.67), channel_id=1, source_target_pairs={{0,64},{32,96},{64,128},{96,160},{128,192},{160,224},{192,0},{224,... | collective-permute-start | bytes 393224 | tf_op jit(solution)/shard_map/ppermute | solution.py:25
  125.9 13.3 %collective-permute-start.30 = (bf16[4,32,512]{2,1,0:T(8,128)(2,1)S(1)}, bf16[4,32,512]{2,1,0:T(8,128)(2,1)S(1)}, u32[]{:S(2)}, u32[]{:S(2)}) collective-permute-start(bf16[4,32,512]{2,1,0:T(8,128)(2,1)S(1)} %fusion.67), channel_id=1, source_target_pairs={{0,128},{32,160},{64,192},{96,224},{128,0},{160,32},{192,64},{224,... | collective-permute-start | bytes 393224 | tf_op jit(solution)/shard_map/ppermute | solution.py:25
  128.0 11.2 %collective-permute-start.29 = (bf16[4,32,512]{2,1,0:T(8,128)(2,1)S(1)}, bf16[4,32,512]{2,1,0:T(8,128)(2,1)S(1)}, u32[]{:S(2)}, u32[]{:S(2)}) collective-permute-start(bf16[4,32,512]{2,1,0:T(8,128)(2,1)S(1)} %fusion.67), channel_id=1, source_target_pairs={{0,192},{32,224},{64,0},{96,32},{128,64},{160,96},{192,128},{224,1... | collective-permute-start | bytes 393224 | tf_op jit(solution)/shard_map/ppermute | solution.py:25

commit v2 on v0

v2 whole, which is shorter than its diff:
```python
import jax
import jax.numpy as jnp
from jax import lax
from jax.experimental import pallas as pl
from jax.experimental.pallas import tpu as pltpu
from jax.sharding import PartitionSpec as P

loss_scale = 0.0625
sparsity = 0.25
bf16 = jnp.bfloat16
f32 = jnp.float32
MIB = 1024 * 1024
LIMIT = pltpu.CompilerParams(vmem_limit_bytes=40 * MIB)
FIRST = pltpu.CompilerParams(vmem_limit_bytes=56 * MIB)
after = lax.optimization_barrier


def place():
    y = lax.axis_index("layer") // 2
    latent = lax.axis_index("latent")
    return y, latent // 2 % 4, latent // 8, latent % 2


def ahead(v, k):
    return (v + k) % 4


def exchange(v, axis, k=1):
    perm = []
    for i in range(256):
        layer, latent = i // 32, i % 32
        y, h = layer // 2, layer % 2
        z, x, c = latent // 8, (latent // 2) % 4, latent % 2
        if axis == "y":
            y = ahead(y, k)
        elif axis == "x":
            x = ahead(x, k)
        elif axis == "z":
            z ^= k
        elif axis == "h":
            h ^= k
        else:
            c ^= k
        perm.append((i, (y * 2 + h) * 32 + (z * 4 + x) * 2 + c))
    return lax.ppermute(v, ("layer", "latent"), perm)


FAR_FIRST = (2, 1, 3)
PARTS = 4
LINE = (3, 2, 1)


def gather(v, axis, ks):
    got = {k: exchange(v, axis, k if axis == "z" else -k) for k in ks}
    return [v, got[1], got[2], got[3]]


def sds(shape, dtype):
    return jax.ShapeDtypeStruct(shape, dtype)


def cost(flops, size):
    return pl.CostEstimate(flops=flops, bytes_accessed=size, transcendentals=0)


def local(kernel, outs, *args, flops=0, scratch=()):
    in_specs = [
        pl.BlockSpec(memory_space=pltpu.SMEM if a.dtype == jnp.int32 and a.ndim == 1 else pltpu.VMEM) for a in args
    ]
    size = sum(a.size * a.dtype.itemsize for a in args) + sum(o.size * o.dtype.itemsize for o in outs)
    return pl.pallas_call(
        kernel,
        out_shape=outs,
        in_specs=in_specs,
        out_specs=[pl.BlockSpec(memory_space=pltpu.VMEM) for _ in outs],
        scratch_shapes=scratch,
        compiler_params=LIMIT,
        cost_estimate=cost(flops, size),
    )(*args)


def dot(a, b):
    return jnp.dot(a, b, preferred_element_type=f32)


def dot_t(a, b):
    return lax.dot_general(a, b, (((1,), (1,)), ((), ())), preferred_element_type=f32)


def wide(ref):
    return ref[...].astype(f32)


def pre_kernel(acts, enc, *refs):
    sends, keep, total, acts_here, enc_here, sems = refs[:3], *refs[3:]
    m = keep.shape[0]
    k = acts.shape[1] // PARTS
    copies = []
    for i in range(PARTS):
        part = slice(i * k, (i + 1) * k)
        pair = (
            pltpu.make_async_copy(acts.at[:, part], acts_here.at[:, part], sems.at[0, i]),
            pltpu.make_async_copy(enc.at[part, :], enc_here.at[part, :], sems.at[1, i]),
        )
        for copy in pair:
            copy.start()
        copies.append(pair)
    for i, pair in enumerate(copies):
        part = slice(i * k, (i + 1) * k)
        for copy in pair:
            copy.wait()
        value = dot(acts_here[:, part], enc_here[part, :])
        total[...] = value if i == 0 else total[...] + value
    y = place()[0]
    for j, ref in enumerate((keep, *sends)):
        ref[...] = total[pl.ds(pl.multiple_of(ahead(y, j) * m, m), m), :].astype(ref.dtype)


def sum_kernel(keep, a, b, c, out, send):
    total = keep[...] + wide(a) + wide(b) + wide(c)
    out[...] = total
    send[...] = total.astype(bf16)


def codes_kernel(keep, got, bias, active, out):
    r = keep.shape[0] // 4
    for j in range(4):
        rows = pl.ds(pl.multiple_of(ahead(place()[1], j) * r, r), r)
        pre = keep[rows, :] + got[rows, :].astype(f32) + bias[...]
        out[j * r : (j + 1) * r, :] = (active[j * r : (j + 1) * r, :] * pre).astype(bf16)


def recon_own_kernel(*refs):
    own, dec, out, lhs = refs[:4], *refs[4:]
    ny = own[0].shape[0]
    r, half = ny // 4, dec.shape[1] // 2
    for b in range(4):
        for a in range(4):
            lhs[b * ny + a * r : b * ny + (a + 1) * r, :] = own[a][b * r : (b + 1) * r, :]
    c = place()[3]
    out[...] = dot(lhs[...], dec[:, pl.ds(pl.multiple_of(c * half, half), half)])


def recon_kernel(blocks, *refs):
    other, dec, own, outs, lhs = refs[:4], refs[4], refs[5], refs[6:-1], refs[-1]
    ny = other[0].shape[0]
    r = ny // 4
    for i, b in enumerate(blocks):
        for a in range(4):
            lhs[i * ny + a * r : i * ny + (a + 1) * r, :] = other[a][b * r : (b + 1) * r, :]
    value = dot(lhs[...], dec[...])
    for i, (b, out) in enumerate(zip(blocks, outs)):
        out[...] = (value[i * ny : (i + 1) * ny] + own[b * ny : (b + 1) * ny, :]).astype(out.dtype)


def split_kernel(keep, a, b, c, out, *sends):
    q = out.shape[1]
    for j, ref in enumerate((out, *sends)):
        column = pl.ds(pl.multiple_of((place()[2] ^ j) * q, q), q)
        total = keep[:, column] + a[:, column].astype(f32) + b[:, column].astype(f32) + c[:, column].astype(f32)
        ref[...] = total.astype(ref.dtype)


def error_kernel(keep, a, b, c, offset, out):
    out[...] = (keep[...] + wide(a) + wide(b) + wide(c) + offset[...]).astype(bf16)


def columns_kernel(a, b, c, d, out):
    q = a.shape[1]
    for j, ref in enumerate((a, b, c, d)):
        out[:, pl.ds(pl.multiple_of((place()[2] ^ j) * q, q), q)] = ref[...]


def back_own_kernel(*refs):
    own, dec, extra, error, out = refs[:4], *refs[4:]
    rows, half = error.shape
    r, ny = rows // 16, rows // 4
    for a in range(4):
        for b in range(4):
            error[a * ny + b * r : a * ny + (b + 1) * r, :] = own[b][a * r : (a + 1) * r, :]
    c = place()[3]
    out[...] = dot_t(error[...], dec[:, pl.ds(pl.multiple_of(c * half, half), half)]) + sparsity * extra[...]


def back_kernel(*refs):
    other, dec, own, error = refs[:4], *refs[4:7]
    sends, keep = refs[7:10], refs[10]
    rows, half = error.shape
    r, ny = rows // 16, rows // 4
    for a in range(4):
        for b in range(4):
            error[a * ny + b * r : a * ny + (b + 1) * r, :] = other[b][a * r : (a + 1) * r, :]
    c = 1 - place()[3]
    total = own[...] + dot_t(error[...], dec[:, pl.ds(pl.multiple_of(c * half, half), half)])
    for j, ref in enumerate((keep, *sends)):
        ref[...] = total[j * ny : (j + 1) * ny].astype(ref.dtype)


def dpre_kernel(keep, got, active, out):
    out[...] = (loss_scale * active[...] * (keep[...] + wide(got))).astype(bf16)


def copy_kernel(idx, src, out):
    out[...] = src[...].astype(out.dtype)


def offset_kernel(idx, acts, bias, out):
    out[...] = bias[...] - wide(acts)


def turn_acts_kernel(idx, a, b, c, d, out):
    out[...] = jnp.concatenate([a[...], b[...], c[...], d[...]], 0).T


def turn_codes_kernel(a, b, c, d, lengths, out, factor):
    m = a.shape[0]
    for j, ref in enumerate((a, b, c, d)):
        out[:, j * m : (j + 1) * m] = ref[...].T
    usage = jnp.sum(wide(out), axis=1, keepdims=True)
    factor[...] = sparsity * usage / lengths[...]


def cross_kernel(codes, own, other, dec, factor, out):
    half = own.shape[1]
    for c, ref in ((place()[3], own), (1 - place()[3], other)):
        at = pl.ds(pl.multiple_of(c * half, half), half)
        out[:, at] = (loss_scale * (dot(codes[...], ref[...]) + factor[...] * dec[:, at].astype(f32))).astype(bf16)


def grad_kernel(acts, a, b, c, d, out, rhs):
    m, n = a.shape[0], out.shape[0]
    step = pl.program_id(0)

    @pl.when(step == 0)
    def _():
        for j, ref in enumerate((a, b, c, d)):
            rhs[j * m : (j + 1) * m, :] = ref[...]

    out[...] = dot(acts[pl.ds(pl.multiple_of(step * n, n), n), :], rhs[...]).astype(bf16)


def placed(kernel, idx, grid, ins, outs, *args, flops=0, size=MIB, scratch=(), limit=LIMIT):
    return pl.pallas_call(
        kernel,
        out_shape=[sds(o[0], o[1]) for o in outs],
        grid_spec=pltpu.PrefetchScalarGridSpec(
            num_scalar_prefetch=1,
            grid=(grid,),
            in_specs=[pl.BlockSpec(*i) for i in ins],
            out_specs=[pl.BlockSpec(*o[2:]) for o in outs],
            scratch_shapes=scratch,
        ),
        compiler_params=limit,
        cost_estimate=cost(flops, size),
    )(idx, *args)


def body(acts, mask, w_enc, b_enc, w_dec, b_dec):
    rows, _, width = acts.shape
    latents = w_enc.shape[2]
    ny = rows // 4
    r = ny // 4
    half = width // 2
    q = half // 4
    y, x, z, c = place()
    blocks = [ahead(v, k) for v in (y, x) for k in range(4)] + [z ^ k for k in range(4)]
    idx = jnp.stack(blocks + [c, 1 - c]).astype(jnp.int32)
    matmul = 2 * rows * width * latents

    flat = acts.reshape(rows, width)
    enc = w_enc.reshape(width, latents)
    dec = w_dec.reshape(latents, width)
    tile = sds((ny, latents), bf16)

    whole = lambda j, idx: (0, 0)
    *sends, keep = pl.pallas_call(
        pre_kernel,
        out_shape=[tile] * 3 + [sds((ny, latents), f32)],
        in_specs=[pl.BlockSpec(memory_space=pl.ANY)] * 2,
        out_specs=[pl.BlockSpec(memory_space=pltpu.VMEM)] * 4,
        scratch_shapes=[
            pltpu.VMEM((rows, latents), f32),
            pltpu.VMEM((rows, width), bf16),
            pltpu.VMEM((width, latents), bf16),
            pltpu.SemaphoreType.DMA((2, PARTS)),
        ],
        compiler_params=FIRST,
        cost_estimate=cost(matmul, 6 * MIB),
    )(flat, enc)

    def over_layers(sends, keep):
        got = {j: exchange(sends[j - 1], "y", j) for j in FAR_FIRST}
        keep, send = local(sum_kernel, [sds((ny, latents), f32), tile], keep, got[1], got[2], got[3])
        return keep, exchange(send, "h")

    keep, got = over_layers(sends, keep)

    dec_a, mask_a, flat_a, _ = after((dec, mask, flat, keep))
    (dec_send,) = placed(
        copy_kernel, idx, 1, [((latents, half), lambda j, idx: (0, idx[13]))],
        [((latents, half), bf16, (latents, half), whole)], dec_a, size=2 * MIB,
    )
    dec_other = exchange(dec_send, "c")
    (active,) = placed(
        copy_kernel, idx, 4, [((r, latents), lambda j, idx: (idx[0] * 4 + idx[4 + j], 0))],
        [((ny, latents), f32, (r, latents), lambda j, idx: (j, 0))], mask_a,
    )
    (offset,) = placed(
        offset_kernel, idx, 4,
        [
            ((r, q), lambda j, idx: (idx[j] * 4 + idx[4], idx[12] * 4 + idx[8])),
            ((1, q), lambda j, idx: (0, idx[12] * 4 + idx[8])),
        ],
        [((ny, q), f32, (r, q), lambda j, idx: (j, 0))], flat_a, b_dec,
    )
    wide_dec = dec_a.astype(f32)
    lengths = jnp.sqrt(jnp.sum(wide_dec * wide_dec, axis=1) + 1e-06)

    (shard,) = local(codes_kernel, [tile], keep, got, b_enc[None, :], active)
    codes = gather(shard, "y", FAR_FIRST)
    codes_other = [exchange(v, "c") for v in codes]

    (recon_own,) = local(
        recon_own_kernel, [sds((rows, half), f32)], *codes, dec, flops=matmul // 2,
        scratch=[pltpu.VMEM((rows, latents), bf16)],
    )

    def recon(blocks, dtypes):
        return local(
            lambda *refs: recon_kernel(blocks, *refs),
            [sds((ny, half), t) for t in dtypes],
            *codes_other, dec_other, recon_own,
            flops=matmul * len(blocks) // 8,
            scratch=[pltpu.VMEM((len(blocks) * ny, latents), bf16)],
        )

    (far,) = recon((2,), (bf16,))
    near_1, near_3, keep = recon((1, 3, 0), (bf16, bf16, f32))
    got = {2: exchange(far, "x", 2), 1: exchange(near_1, "x", 1), 3: exchange(near_3, "x", 3)}
    flat_b, near_3 = after((flat, near_3))
    (acts_t,) = placed(
        turn_acts_kernel, idx, 4,
        [((r, width), lambda j, idx, b=b: (idx[j] * 4 + idx[4 + b], 0)) for b in range(4)],
        [((width, rows), bf16, (width, ny), lambda j, idx: (0, j))], *[flat_b] * 4, size=4 * MIB,
    )
    codes_t, factor = local(
        turn_codes_kernel, [sds((latents, rows), bf16), sds((latents, 1), f32)], *codes, lengths[:, None]
    )
    got[1], acts_t, codes_t = after((got[1], acts_t, codes_t))
    keep, *sends = local(
        split_kernel, [sds((ny, q), f32)] + [sds((ny, q), bf16)] * 3, keep, got[1], got[2], got[3]
    )
    got = {j: exchange(sends[j - 1], "z", j) for j in LINE}
    (error,) = local(error_kernel, [sds((ny, q), bf16)], keep, got[1], got[2], got[3], offset)
    (error,) = local(columns_kernel, [sds((ny, half), bf16)], *gather(error, "z", LINE))
    errors = gather(error, "x", FAR_FIRST)
    errors_other = [exchange(v, "c") for v in errors]

    error_own, back_own = local(
        back_own_kernel, [sds((rows, half), bf16), sds((rows, latents), f32)], *errors, dec, lengths[None, :],
        flops=matmul // 2,
    )
    error_other, *sends, keep = local(
        back_kernel, [sds((rows, half), bf16)] + [tile] * 3 + [sds((ny, latents), f32)],
        *errors_other, dec, back_own,
        flops=matmul // 2,
    )
    keep, got = over_layers(sends, keep)

    m = latents // 4
    grad_dec = pl.pallas_call(
        cross_kernel,
        out_shape=sds((latents, width), bf16),
        grid=(4,),
        in_specs=[
            pl.BlockSpec((m, rows), lambda j: (j, 0)),
            pl.BlockSpec((rows, half), lambda j: (0, 0)),
            pl.BlockSpec((rows, half), lambda j: (0, 0)),
            pl.BlockSpec((m, width), lambda j: (j, 0)),
            pl.BlockSpec((m, 1), lambda j: (j, 0)),
        ],
        out_specs=pl.BlockSpec((m, width), lambda j: (j, 0)),
        compiler_params=LIMIT,
        cost_estimate=cost(matmul, 8 * MIB),
    )(codes_t, error_own, error_other, dec, factor)
    keep, grad_dec = after((keep, grad_dec))
    (shard,) = local(dpre_kernel, [tile], keep, got, active)
    dpre = gather(shard, "y", FAR_FIRST)

    m = width // 8
    grad_enc = pl.pallas_call(
        grad_kernel,
        out_shape=sds((width, latents), bf16),
        grid=(8,),
        in_specs=[pl.BlockSpec(memory_space=pltpu.VMEM)] * 5,
        out_specs=pl.BlockSpec((m, latents), lambda j: (j, 0)),
        scratch_shapes=[pltpu.VMEM((rows, latents), bf16)],
        compiler_params=LIMIT,
        cost_estimate=cost(matmul, 5 * MIB),
    )(acts_t, *dpre)
    return (grad_enc.reshape(w_enc.shape), grad_dec.reshape(w_dec.shape))


def solution(mesh):
    return jax.shard_map(
        body,
        mesh=mesh,
        in_specs=(
            P(None, "layer", None),
            P(None, "latent"),
            P("layer", None, "latent"),
            P("latent"),
            P("latent", "layer", None),
            P("layer", None),
        ),
        out_specs=(P("layer", None, "latent"), P("latent", "layer", None)),
        check_vma=False,
    )
```

time: 596 us -> 128 us (0.21)
  waiting for transfers between devices: 520 us -> 52.1 us
  starting transfers between devices: 0.12 us -> 49.7 us
  blocking collectives: 26.5 us -> 0 us
  Pallas kernels: 0 us -> 21.2 us
  matrix products: 19.4 us -> 0 us
  between operations: 13.8 us -> 0.88 us
  other arithmetic: 7.77 us -> 0.49 us
    psum x3 -> x0, waiting for transfers between devices: 520 us -> none  [the longest x1 242 us: body(): lax.psum(jnp.dot(codes, dec_flat, preferred_element_type=jnp.float32), 'l...]
    ppermute x0 -> x35, waiting for transfers between devices: none -> 52.1 us  [exchange(): return lax.ppermute(v, ('layer', 'latent'), perm)]
    ppermute x0 -> x35, starting transfers between devices: none -> 49.7 us  [exchange(): return lax.ppermute(v, ('layer', 'latent'), perm)]
    psum x1 -> x0, blocking collectives: 26.5 us -> none  [body(): pre, norms = lax.psum((partial_pre, local_norms), 'layer')]
    pallas_call x0 -> x20, Pallas kernels: none -> 21.2 us  [the longest x13 6.39 us: local(): pl.pallas_call(kernel, out_shape=outs, in_specs=in_specs, out_specs=[pl.B...]
    dot_general x5 -> x0, matrix products: 19.4 us -> none  [the longest x1 5.11 us: body(): lax.dot_general(codes, error, (((0,), (0,)), ((), ())), preferred_element...]
  transfers between devices with their start and end apart: 3 -> 35, of which waited for: 3 -> 26; matrix products, arithmetic and copies ran while one was open for 1% -> 1% of each run, Pallas kernels for 0% -> 7%
where the time goes in v2:
time: 128 us
  waiting for transfers between devices  52.1 us (41%)
  starting transfers between devices  49.7 us (39%)
  Pallas kernels  21.2 us (17%)
  local copies, waits for them, and re-layouts  3.71 us (3%)
    ppermute x35, waiting for transfers between devices, exchange(): return lax.ppermute(v, ('layer', 'latent'), perm)  52.1 us
    ppermute x35, starting transfers between devices, exchange(): return lax.ppermute(v, ('layer', 'latent'), perm)  49.7 us
    pallas_call x13, Pallas kernels, local(): pl.pallas_call(kernel, out_shape=outs, in_specs=in_specs, out_specs=[pl.B...  6.39 us
    pallas_call x1, Pallas kernels, body(): pl.pallas_call(grad_kernel, out_shape=sds((width, latents), bf16), grid=(...  4.38 us
    pallas_call x1, Pallas kernels, body(): pl.pallas_call(pre_kernel, out_shape=[tile] * 3 + [sds((ny, latents), f32...  3.68 us
    pallas_call x4, Pallas kernels, placed(): pl.pallas_call(kernel, out_shape=[sds(o[0], o[1]) for o in outs], grid_sp...  3.66 us
    unnamed x18, local copies, waits for them, and re-layouts  3.47 us
    pallas_call x1, Pallas kernels, body(): pl.pallas_call(cross_kernel, out_shape=sds((latents, width), bf16), grid=...  3.1 us
  transfers between devices with their start and end apart: 35, of which 26 were waited for; matrix products, arithmetic and copies ran while one was open for 1% of the time, Pallas kernels for 7%

profile of v2, /device:TPU:32, one launch (start us, length us, event | category | flops | bytes accessed | tf_op | source)
XLA Modules:
  0.0 128.1 jit_solution(13505094141375586076)
XLA Ops:
  0.6 3.7 %shard_map.77 = (bf16[128,512]{1,0:T(8,128)(2,1)}, bf16[128,512]{1,0:T(8,128)(2,1)}, bf16[128,512]{1,0:T(8,128)(2,1)}, f32[128,512]{1,0:T(8,128)}) custom-call(bf16[512,2048]{1,0:T(8,128)(2,1)} %bitcast.28, bf16[2048,512]{1,0:T(8,128)(2,1)} %bitcast.38), custom_call_target="tpu_custom_call" | custom-call | flops 1073741824 | bytes 6291456 | tf_op jit(solution)/shard_map/pallas_call | solution.py:276
  4.3 1.7 %collective-permute-start = (bf16[128,512]{1,0:T(8,128)(2,1)}, bf16[128,512]{1,0:T(8,128)(2,1)S(1)}, u32[]{:S(2)}, u32[]{:S(2)}) collective-permute-start(bf16[128,512]{1,0:T(8,128)(2,1)} %get-tuple-element.36), channel_id=1, source_target_pairs={{0,64},{1,65},{2,66},{3,67},{4,68},{5,69},{6,70},{7,71},{8,72},{9,... | collective-permute-start | bytes 393224 | tf_op jit(solution)/shard_map/ppermute | solution.py:45
  6.0 2.9 %collective-permute-start.1 = (bf16[128,512]{1,0:T(8,128)(2,1)}, bf16[128,512]{1,0:T(8,128)(2,1)S(1)}, u32[]{:S(2)}, u32[]{:S(2)}) collective-permute-start(bf16[128,512]{1,0:T(8,128)(2,1)} %get-tuple-element.37), channel_id=1, source_target_pairs={{0,128},{1,129},{2,130},{3,131},{4,132},{5,133},{6,134},{7,135},{8... | collective-permute-start | bytes 393224 | tf_op jit(solution)/shard_map/ppermute | solution.py:45
  8.9 1.3 %collective-permute-start.2 = (bf16[128,512]{1,0:T(8,128)(2,1)}, bf16[128,512]{1,0:T(8,128)(2,1)S(1)}, u32[]{:S(2)}, u32[]{:S(2)}) collective-permute-start(bf16[128,512]{1,0:T(8,128)(2,1)} %get-tuple-element.38), channel_id=1, source_target_pairs={{0,192},{1,193},{2,194},{3,195},{4,196},{5,197},{6,198},{7,199},{8... | collective-permute-start | bytes 393224 | tf_op jit(solution)/shard_map/ppermute | solution.py:45
  11.1 4.0 %collective-permute-done.1.b = bf16[128,512]{1,0:T(8,128)(2,1)S(1)} collective-permute-done((bf16[128,512]{1,0:T(8,128)(2,1)}, bf16[128,512]{1,0:T(8,128)(2,1)S(1)}, u32[]{:S(2)}, u32[]{:S(2)}) %collective-permute-start.1) | collective-permute-done | bytes 131104 | tf_op jit(solution)/shard_map/ppermute | solution.py:45
  15.1 0.9 copy-done.6
  16.9 6.4 %collective-permute-start.3 = (bf16[128,512]{1,0:T(8,128)(2,1)S(1)}, bf16[128,512]{1,0:T(8,128)(2,1)S(1)}, u32[]{:S(2)}, u32[]{:S(2)}) collective-permute-start(bf16[128,512]{1,0:T(8,128)(2,1)S(1)} %get-tuple-element.40), channel_id=1, source_target_pairs={{0,32},{1,33},{2,34},{3,35},{4,36},{5,37},{6,38},{7,39},{8,40},{9,... | collective-permute-start | bytes 393224 | tf_op jit(solution)/shard_map/ppermute | solution.py:45
  23.9 6.3 %collective-permute-done.3.got = bf16[128,512]{1,0:T(8,128)(2,1)S(1)} collective-permute-done((bf16[128,512]{1,0:T(8,128)(2,1)S(1)}, bf16[128,512]{1,0:T(8,128)(2,1)S(1)}, u32[]{:S(2)}, u32[]{:S(2)}) %collective-permute-start.3) | collective-permute-done | bytes 131104 | tf_op jit(solution)/shard_map/ppermute | solution.py:45
  30.2 1.3 %collective-permute-start.9 = (bf16[128,512]{1,0:T(8,128)(2,1)S(1)}, bf16[128,512]{1,0:T(8,128)(2,1)S(1)}, u32[]{:S(2)}, u32[]{:S(2)}) collective-permute-start(bf16[128,512]{1,0:T(8,128)(2,1)S(1)} %shard_map.80.refs_0_.a), channel_id=1, source_target_pairs={{0,64},{1,65},{2,66},{3,67},{4,68},{5,69},{6,70},{7,71},{8,72},{9,... | collective-permute-start | bytes 393224 | tf_op jit(solution)/shard_map/ppermute | solution.py:45
  31.6 2.4 %collective-permute-start.7 = (bf16[128,512]{1,0:T(8,128)(2,1)S(1)}, bf16[128,512]{1,0:T(8,128)(2,1)S(1)}, u32[]{:S(2)}, u32[]{:S(2)}) collective-permute-start(bf16[128,512]{1,0:T(8,128)(2,1)S(1)} %shard_map.80.refs_0_.a), channel_id=1, source_target_pairs={{0,128},{1,129},{2,130},{3,131},{4,132},{5,133},{6,134},{7,135},{8... | collective-permute-start | bytes 393224 | tf_op jit(solution)/shard_map/ppermute | solution.py:45
  34.0 1.6 %collective-permute-start.5 = (bf16[128,512]{1,0:T(8,128)(2,1)S(1)}, bf16[128,512]{1,0:T(8,128)(2,1)S(1)}, u32[]{:S(2)}, u32[]{:S(2)}) collective-permute-start(bf16[128,512]{1,0:T(8,128)(2,1)S(1)} %shard_map.80.refs_0_.a), channel_id=1, source_target_pairs={{0,192},{1,193},{2,194},{3,195},{4,196},{5,197},{6,198},{7,199},{8... | collective-permute-start | bytes 393224 | tf_op jit(solution)/shard_map/ppermute | solution.py:45
  35.5 2.0 %collective-permute-done.9.refs_3_.d = bf16[128,512]{1,0:T(8,128)(2,1)S(1)} collective-permute-done((bf16[128,512]{1,0:T(8,128)(2,1)S(1)}, bf16[128,512]{1,0:T(8,128)(2,1)S(1)}, u32[]{:S(2)}, u32[]{:S(2)}) %collective-permute-start.9) | collective-permute-done | bytes 131104 | tf_op jit(solution)/shard_map/ppermute | solution.py:45
  37.5 2.4 %collective-permute-done.7.refs_2_.c = bf16[128,512]{1,0:T(8,128)(2,1)S(1)} collective-permute-done((bf16[128,512]{1,0:T(8,128)(2,1)S(1)}, bf16[128,512]{1,0:T(8,128)(2,1)S(1)}, u32[]{:S(2)}, u32[]{:S(2)}) %collective-permute-start.7) | collective-permute-done | bytes 131104 | tf_op jit(solution)/shard_map/ppermute | solution.py:45
  41.5 1.3 %shard_map.83 = (bf16[128,1024]{1,0:T(8,128)(2,1)}, bf16[128,1024]{1,0:T(8,128)(2,1)}, f32[128,1024]{1,0:T(8,128)S(1)}) custom-call(bf16[128,512]{1,0:T(8,128)(2,1)S(1)} %collective-permute-done.4.refs_0_, bf16[128,512]{1,0:T(8,128)(2,1)S(1)} %collective-permute-done.6.refs_1_, bf16[128,512]{1,0:T(8,128)(2,1)S(1)} %collective-permute-done.8.refs_2_, ...), custom_call_target="tpu_custom_call" | custom-call | flops 402653184 | bytes 4718592 | tf_op jit(solution)/shard_map/pallas_call | solution.py:71
  42.8 1.5 %collective-permute-start.12 = (bf16[128,1024]{1,0:T(8,128)(2,1)}, bf16[128,1024]{1,0:T(8,128)(2,1)}, u32[]{:S(2)}, u32[]{:S(2)}) collective-permute-start(bf16[128,1024]{1,0:T(8,128)(2,1)} %get-tuple-element.43), channel_id=1, source_target_pairs={{0,2},{1,3},{2,4},{3,5},{4,6},{5,7},{6,0},{7,1},{8,10},{9,11},{10,... | collective-permute-start | bytes 786440 | tf_op jit(solution)/shard_map/ppermute | solution.py:45
  44.3 1.7 %collective-permute-start.14 = (bf16[128,1024]{1,0:T(8,128)(2,1)}, bf16[128,1024]{1,0:T(8,128)(2,1)}, u32[]{:S(2)}, u32[]{:S(2)}) collective-permute-start(bf16[128,1024]{1,0:T(8,128)(2,1)} %get-tuple-element.44), channel_id=1, source_target_pairs={{0,6},{1,7},{2,0},{3,1},{4,2},{5,3},{6,4},{7,5},{8,14},{9,15},{10,... | collective-permute-start | bytes 786440 | tf_op jit(solution)/shard_map/ppermute | solution.py:45
  46.0 1.0 shard_map.86
  47.0 1.8 %collective-permute-start.13 = (bf16[128,1024]{1,0:T(8,128)(2,1)}, bf16[128,1024]{1,0:T(8,128)(2,1)}, u32[]{:S(2)}, u32[]{:S(2)}) collective-permute-start(bf16[128,1024]{1,0:T(8,128)(2,1)} %shard_map.86), channel_id=1, source_target_pairs={{0,4},{1,5},{2,6},{3,7},{4,0},{5,1},{6,2},{7,3},{8,12},{9,13},{10,... | collective-permute-start | bytes 786440 | tf_op jit(solution)/shard_map/ppermute | solution.py:45
  49.5 0.9 copy-done.5
  50.7 1.6 %copy-done.1 = bf16[512,1,2048]{2,0,1:T(8,128)(2,1)S(1)} copy-done((bf16[512,1,2048]{2,0,1:T(8,128)(2,1)S(1)}, bf16[512,1,2048]{2,0,1:T(8,128)(2,1)}, u32[]{:S(2)}) %copy-start.1) | copy-done | bytes 2097176
  52.3 1.7 %shard_map.84.acts = bf16[2048,512]{1,0:T(8,128)(2,1)S(1)} custom-call(s32[14]{0:T(128)S(1)} %stack.59.idx, bf16[512,2048]{1,0:T(8,128)(2,1)S(1)} %bitcast.29, bf16[512,2048]{1,0:T(8,128)(2,1)S(1)} %bitcast.30, bf16[512,2048]{1,0:T(8,128)(2,1)S(1)} %bitcast.31, bf16[512,2048]{1,0:T(8,128)(2,1)S(1)} %bitcast.32), custom_call_target="tpu_custom_call" | custom-call | bytes 4194304 | tf_op jit(solution)/shard_map/pallas_call | solution.py:243
  54.0 3.7 %collective-permute-done.14.c = bf16[128,1024]{1,0:T(8,128)(2,1)} collective-permute-done((bf16[128,1024]{1,0:T(8,128)(2,1)}, bf16[128,1024]{1,0:T(8,128)(2,1)}, u32[]{:S(2)}, u32[]{:S(2)}) %collective-permute-start.14) | collective-permute-done | bytes 262176 | tf_op jit(solution)/shard_map/ppermute | solution.py:45
  57.8 1.7 %collective-permute-done.13.b = bf16[128,1024]{1,0:T(8,128)(2,1)} collective-permute-done((bf16[128,1024]{1,0:T(8,128)(2,1)}, bf16[128,1024]{1,0:T(8,128)(2,1)}, u32[]{:S(2)}, u32[]{:S(2)}) %collective-permute-start.13) | collective-permute-done | bytes 262176 | tf_op jit(solution)/shard_map/ppermute | solution.py:45
  59.5 1.3 shard_map.87
  60.8 2.5 %collective-permute-start.16 = (bf16[128,256]{1,0:T(8,128)(2,1)S(1)}, bf16[128,256]{1,0:T(8,128)(2,1)S(1)}, u32[]{:S(2)}, u32[]{:S(2)}) collective-permute-start(bf16[128,256]{1,0:T(8,128)(2,1)S(1)} %get-tuple-element.52), channel_id=1, source_target_pairs={{0,16},{1,17},{2,18},{3,19},{4,20},{5,21},{6,22},{7,23},{8,24},{9,... | collective-permute-start | bytes 196616 | tf_op jit(solution)/shard_map/ppermute | solution.py:45
  63.4 0.9 collective-permute-start.17
  65.1 2.5 %collective-permute-done.16.b = bf16[128,256]{1,0:T(8,128)(2,1)S(1)} collective-permute-done((bf16[128,256]{1,0:T(8,128)(2,1)S(1)}, bf16[128,256]{1,0:T(8,128)(2,1)S(1)}, u32[]{:S(2)}, u32[]{:S(2)}) %collective-permute-start.16) | collective-permute-done | bytes 65568 | tf_op jit(solution)/shard_map/ppermute | solution.py:45
  67.5 2.2 %collective-permute-done.17.c = bf16[128,256]{1,0:T(8,128)(2,1)S(1)} collective-permute-done((bf16[128,256]{1,0:T(8,128)(2,1)S(1)}, bf16[128,256]{1,0:T(8,128)(2,1)S(1)}, u32[]{:S(2)}, u32[]{:S(2)}) %collective-permute-start.17) | collective-permute-done | bytes 65568 | tf_op jit(solution)/shard_map/ppermute | solution.py:45
  69.8 1.1 collective-permute-start.20
  70.8 2.1 %collective-permute-start.19 = (bf16[128,256]{1,0:T(8,128)(2,1)S(1)}, bf16[128,256]{1,0:T(8,128)(2,1)S(1)}, u32[]{:S(2)}, u32[]{:S(2)}) collective-permute-start(bf16[128,256]{1,0:T(8,128)(2,1)S(1)} %shard_map.89.a), channel_id=1, source_target_pairs={{0,16},{1,17},{2,18},{3,19},{4,20},{5,21},{6,22},{7,23},{8,24},{9,... | collective-permute-start | bytes 196616 | tf_op jit(solution)/shard_map/ppermute | solution.py:45
  73.3 2.9 %collective-permute-done.20.d = bf16[128,256]{1,0:T(8,128)(2,1)S(1)} collective-permute-done((bf16[128,256]{1,0:T(8,128)(2,1)S(1)}, bf16[128,256]{1,0:T(8,128)(2,1)S(1)}, u32[]{:S(2)}, u32[]{:S(2)}) %collective-permute-start.20) | collective-permute-done | bytes 65568 | tf_op jit(solution)/shard_map/ppermute | solution.py:45
  76.2 1.0 collective-permute-done.18.b
  77.3 0.9 collective-permute-start.26
  78.2 2.1 %collective-permute-start.24 = (bf16[128,1024]{1,0:T(8,128)(2,1)S(1)}, bf16[128,1024]{1,0:T(8,128)(2,1)S(1)}, u32[]{:S(2)}, u32[]{:S(2)}) collective-permute-start(bf16[128,1024]{1,0:T(8,128)(2,1)S(1)} %shard_map.90.refs_0_), channel_id=1, source_target_pairs={{0,4},{1,5},{2,6},{3,7},{4,0},{5,1},{6,2},{7,3},{8,12},{9,13},{10,... | collective-permute-start | bytes 786440 | tf_op jit(solution)/shard_map/ppermute | solution.py:45
  81.0 8.2 %collective-permute-done.26.refs_3_ = bf16[128,1024]{1,0:T(8,128)(2,1)S(1)} collective-permute-done((bf16[128,1024]{1,0:T(8,128)(2,1)S(1)}, bf16[128,1024]{1,0:T(8,128)(2,1)S(1)}, u32[]{:S(2)}, u32[]{:S(2)}) %collective-permute-start.26) | collective-permute-done | bytes 262176 | tf_op jit(solution)/shard_map/ppermute | solution.py:45
  92.2 1.3 %collective-permute-start.28 = (bf16[128,512]{1,0:T(8,128)(2,1)S(1)}, bf16[128,512]{1,0:T(8,128)(2,1)S(1)}, u32[]{:S(2)}, u32[]{:S(2)}) collective-permute-start(bf16[128,512]{1,0:T(8,128)(2,1)S(1)} %get-tuple-element.57), channel_id=1, source_target_pairs={{0,64},{1,65},{2,66},{3,67},{4,68},{5,69},{6,70},{7,71},{8,72},{9,... | collective-permute-start | bytes 393224 | tf_op jit(solution)/shard_map/ppermute | solution.py:45
  93.5 2.4 %collective-permute-start.29 = (bf16[128,512]{1,0:T(8,128)(2,1)S(1)}, bf16[128,512]{1,0:T(8,128)(2,1)S(1)}, u32[]{:S(2)}, u32[]{:S(2)}) collective-permute-start(bf16[128,512]{1,0:T(8,128)(2,1)S(1)} %get-tuple-element.58), channel_id=1, source_target_pairs={{0,128},{1,129},{2,130},{3,131},{4,132},{5,133},{6,134},{7,135},{8... | collective-permute-start | bytes 393224 | tf_op jit(solution)/shard_map/ppermute | solution.py:45
  95.9 1.1 collective-permute-start.30
  97.0 2.4 %collective-permute-done.28.a = bf16[128,512]{1,0:T(8,128)(2,1)S(1)} collective-permute-done((bf16[128,512]{1,0:T(8,128)(2,1)S(1)}, bf16[128,512]{1,0:T(8,128)(2,1)S(1)}, u32[]{:S(2)}, u32[]{:S(2)}) %collective-permute-start.28) | collective-permute-done | bytes 131104 | tf_op jit(solution)/shard_map/ppermute | solution.py:45
  99.4 2.8 %collective-permute-done.29.b = bf16[128,512]{1,0:T(8,128)(2,1)S(1)} collective-permute-done((bf16[128,512]{1,0:T(8,128)(2,1)S(1)}, bf16[128,512]{1,0:T(8,128)(2,1)S(1)}, u32[]{:S(2)}, u32[]{:S(2)}) %collective-permute-start.29) | collective-permute-done | bytes 131104 | tf_op jit(solution)/shard_map/ppermute | solution.py:45
  102.5 5.5 %collective-permute-start.31 = (bf16[128,512]{1,0:T(8,128)(2,1)S(1)}, bf16[128,512]{1,0:T(8,128)(2,1)S(1)}, u32[]{:S(2)}, u32[]{:S(2)}) collective-permute-start(bf16[128,512]{1,0:T(8,128)(2,1)S(1)} %get-tuple-element.66), channel_id=1, source_target_pairs={{0,32},{1,33},{2,34},{3,35},{4,36},{5,37},{6,38},{7,39},{8,40},{9,... | collective-permute-start | bytes 393224 | tf_op jit(solution)/shard_map/ppermute | solution.py:45
  107.9 3.1 %shard_map.94 = bf16[512,2048]{1,0:T(8,128)(2,1)} custom-call(bf16[512,512]{1,0:T(8,128)(2,1)S(1)} %get-tuple-element.61.codes, bf16[512,1024]{1,0:T(8,128)(2,1)S(1)} %get-tuple-element.62.own, bf16[512,1024]{1,0:T(8,128)(2,1)S(1)} %get-tuple-element.63.other, bf16[512,2048]{1,0:T(8,128)(2,1)S(1)} %bitcast.27, f32[512,1]{1,0:T(8,128)S(1)} %get-tuple-element.64.factor), custom_call_target="tpu_custom_call" | custom-call | flops 1073741824 | bytes 8388608 | tf_op jit(solution)/shard_map/pallas_call | solution.py:371
  111.1 3.0 %collective-permute-done.31.got = bf16[128,512]{1,0:T(8,128)(2,1)S(1)} collective-permute-done((bf16[128,512]{1,0:T(8,128)(2,1)S(1)}, bf16[128,512]{1,0:T(8,128)(2,1)S(1)}, u32[]{:S(2)}, u32[]{:S(2)}) %collective-permute-start.31) | collective-permute-done | bytes 131104 | tf_op jit(solution)/shard_map/ppermute | solution.py:45
  114.1 2.3 %collective-permute-start.34 = (bf16[128,512]{1,0:T(8,128)(2,1)S(1)}, bf16[128,512]{1,0:T(8,128)(2,1)S(1)}, u32[]{:S(2)}, u32[]{:S(2)}) collective-permute-start(bf16[128,512]{1,0:T(8,128)(2,1)S(1)} %shard_map.95.a), channel_id=1, source_target_pairs={{0,64},{1,65},{2,66},{3,67},{4,68},{5,69},{6,70},{7,71},{8,72},{9,... | collective-permute-start | bytes 393224 | tf_op jit(solution)/shard_map/ppermute | solution.py:45
  116.3 2.4 %collective-permute-start.33 = (bf16[128,512]{1,0:T(8,128)(2,1)S(1)}, bf16[128,512]{1,0:T(8,128)(2,1)S(1)}, u32[]{:S(2)}, u32[]{:S(2)}) collective-permute-start(bf16[128,512]{1,0:T(8,128)(2,1)S(1)} %shard_map.95.a), channel_id=1, source_target_pairs={{0,128},{1,129},{2,130},{3,131},{4,132},{5,133},{6,134},{7,135},{8... | collective-permute-start | bytes 393224 | tf_op jit(solution)/shard_map/ppermute | solution.py:45
  119.1 2.6 %collective-permute-done.34.d = bf16[128,512]{1,0:T(8,128)(2,1)S(1)} collective-permute-done((bf16[128,512]{1,0:T(8,128)(2,1)S(1)}, bf16[128,512]{1,0:T(8,128)(2,1)S(1)}, u32[]{:S(2)}, u32[]{:S(2)}) %collective-permute-start.34) | collective-permute-done | bytes 131104 | tf_op jit(solution)/shard_map/ppermute | solution.py:45
  121.7 1.9 %collective-permute-done.33.c = bf16[128,512]{1,0:T(8,128)(2,1)S(1)} collective-permute-done((bf16[128,512]{1,0:T(8,128)(2,1)S(1)}, bf16[128,512]{1,0:T(8,128)(2,1)S(1)}, u32[]{:S(2)}, u32[]{:S(2)}) %collective-permute-start.33) | collective-permute-done | bytes 131104 | tf_op jit(solution)/shard_map/ppermute | solution.py:45
  123.8 4.4 %shard_map.96 = bf16[2048,512]{1,0:T(8,128)(2,1)} custom-call(bf16[2048,512]{1,0:T(8,128)(2,1)S(1)} %shard_map.84.acts, bf16[128,512]{1,0:T(8,128)(2,1)S(1)} %shard_map.95.a, bf16[128,512]{1,0:T(8,128)(2,1)S(1)} %collective-permute-done.32.b, bf16[128,512]{1,0:T(8,128)(2,1)S(1)} %collective-permute-done.33.c, bf16[128,512]{1,0:T(8,128)(2,1)S(1)} %collective-permute-done.34.d), custom_call_target="tpu_custom_call" | custom-call | flops 1073741824 | bytes 5242880 | tf_op jit(solution)/shard_map/pallas_call | solution.py:391
  (64 shorter events, 10.7 us)
Async XLA Ops:
  0.6 15.5 %copy-start = (bf16[512,1,2048]{2,0,1:T(8,128)(2,1)S(1)}, bf16[512,1,2048]{2,0,1:T(8,128)(2,1)}, u32[]{:S(2)}) copy-start(bf16[512,1,2048]{2,0,1:T(8,128)(2,1)} %param.10) | copy-start | bytes 6291460
  4.3 18.9 %copy-start.3 = (s32[512,512]{1,0:T(8,128)S(1)}, s32[512,512]{1,0:T(8,128)}, u32[]{:S(2)}) copy-start(s32[512,512]{1,0:T(8,128)} %src) | copy-start | bytes 3145732
  4.3 6.8 %collective-permute-start = (bf16[128,512]{1,0:T(8,128)(2,1)}, bf16[128,512]{1,0:T(8,128)(2,1)S(1)}, u32[]{:S(2)}, u32[]{:S(2)}) collective-permute-start(bf16[128,512]{1,0:T(8,128)(2,1)} %get-tuple-element.36), channel_id=1, source_target_pairs={{0,64},{1,65},{2,66},{3,67},{4,68},{5,69},{6,70},{7,71},{8,72},{9,... | collective-permute-start | bytes 393224 | tf_op jit(solution)/shard_map/ppermute | solution.py:45
  6.0 9.1 %collective-permute-start.1 = (bf16[128,512]{1,0:T(8,128)(2,1)}, bf16[128,512]{1,0:T(8,128)(2,1)S(1)}, u32[]{:S(2)}, u32[]{:S(2)}) collective-permute-start(bf16[128,512]{1,0:T(8,128)(2,1)} %get-tuple-element.37), channel_id=1, source_target_pairs={{0,128},{1,129},{2,130},{3,131},{4,132},{5,133},{6,134},{7,135},{8... | collective-permute-start | bytes 393224 | tf_op jit(solution)/shard_map/ppermute | solution.py:45
  8.9 6.2 %collective-permute-start.2 = (bf16[128,512]{1,0:T(8,128)(2,1)}, bf16[128,512]{1,0:T(8,128)(2,1)S(1)}, u32[]{:S(2)}, u32[]{:S(2)}) collective-permute-start(bf16[128,512]{1,0:T(8,128)(2,1)} %get-tuple-element.38), channel_id=1, source_target_pairs={{0,192},{1,193},{2,194},{3,195},{4,196},{5,197},{6,198},{7,199},{8... | collective-permute-start | bytes 393224 | tf_op jit(solution)/shard_map/ppermute | solution.py:45
  15.1 1.0 copy-start.6
  16.2 14.0 %copy-start.8 = (f32[512]{0:T(512)S(1)}, f32[512]{0:T(512)}, u32[]{:S(2)}) copy-start(f32[512]{0:T(512)} %param.9) | copy-start | bytes 6148
  16.8 24.7 %collective-permute-start.11 = (bf16[512,1024]{1,0:T(8,128)(2,1)S(1)}, bf16[512,1024]{1,0:T(8,128)(2,1)S(1)}, u32[]{:S(2)}, u32[]{:S(2)}) collective-permute-start(bf16[512,1024]{1,0:T(8,128)(2,1)S(1)} %shard_map.81), channel_id=1, source_target_pairs={{0,1},{1,0},{2,3},{3,2},{4,5},{5,4},{6,7},{7,6},{8,9},{9,8},{10,11... | collective-permute-start | bytes 3145736 | tf_op jit(solution)/shard_map/ppermute | solution.py:45
  16.9 13.3 %collective-permute-start.3 = (bf16[128,512]{1,0:T(8,128)(2,1)S(1)}, bf16[128,512]{1,0:T(8,128)(2,1)S(1)}, u32[]{:S(2)}, u32[]{:S(2)}) collective-permute-start(bf16[128,512]{1,0:T(8,128)(2,1)S(1)} %get-tuple-element.40), channel_id=1, source_target_pairs={{0,32},{1,33},{2,34},{3,35},{4,36},{5,37},{6,38},{7,39},{8,40},{9,... | collective-permute-start | bytes 393224 | tf_op jit(solution)/shard_map/ppermute | solution.py:45
  30.2 7.3 %collective-permute-start.9 = (bf16[128,512]{1,0:T(8,128)(2,1)S(1)}, bf16[128,512]{1,0:T(8,128)(2,1)S(1)}, u32[]{:S(2)}, u32[]{:S(2)}) collective-permute-start(bf16[128,512]{1,0:T(8,128)(2,1)S(1)} %shard_map.80.refs_0_.a), channel_id=1, source_target_pairs={{0,64},{1,65},{2,66},{3,67},{4,68},{5,69},{6,70},{7,71},{8,72},{9,... | collective-permute-start | bytes 393224 | tf_op jit(solution)/shard_map/ppermute | solution.py:45
  31.6 8.4 %collective-permute-start.7 = (bf16[128,512]{1,0:T(8,128)(2,1)S(1)}, bf16[128,512]{1,0:T(8,128)(2,1)S(1)}, u32[]{:S(2)}, u32[]{:S(2)}) collective-permute-start(bf16[128,512]{1,0:T(8,128)(2,1)S(1)} %shard_map.80.refs_0_.a), channel_id=1, source_target_pairs={{0,128},{1,129},{2,130},{3,131},{4,132},{5,133},{6,134},{7,135},{8... | collective-permute-start | bytes 393224 | tf_op jit(solution)/shard_map/ppermute | solution.py:45
  34.0 6.2 %collective-permute-start.5 = (bf16[128,512]{1,0:T(8,128)(2,1)S(1)}, bf16[128,512]{1,0:T(8,128)(2,1)S(1)}, u32[]{:S(2)}, u32[]{:S(2)}) collective-permute-start(bf16[128,512]{1,0:T(8,128)(2,1)S(1)} %shard_map.80.refs_0_.a), channel_id=1, source_target_pairs={{0,192},{1,193},{2,194},{3,195},{4,196},{5,197},{6,198},{7,199},{8... | collective-permute-start | bytes 393224 | tf_op jit(solution)/shard_map/ppermute | solution.py:45
  35.5 5.6 %collective-permute-start.4 = (bf16[128,512]{1,0:T(8,128)(2,1)S(1)}, bf16[128,512]{1,0:T(8,128)(2,1)S(1)}, u32[]{:S(2)}, u32[]{:S(2)}) collective-permute-start(bf16[128,512]{1,0:T(8,128)(2,1)S(1)} %shard_map.80.refs_0_.a), channel_id=1, source_target_pairs={{0,1},{1,0},{2,3},{3,2},{4,5},{5,4},{6,7},{7,6},{8,9},{9,8},{10,11... | collective-permute-start | bytes 393224 | tf_op jit(solution)/shard_map/ppermute | solution.py:45
  37.5 3.6 %collective-permute-start.10 = (bf16[128,512]{1,0:T(8,128)(2,1)S(1)}, bf16[128,512]{1,0:T(8,128)(2,1)S(1)}, u32[]{:S(2)}, u32[]{:S(2)}) collective-permute-start(bf16[128,512]{1,0:T(8,128)(2,1)S(1)} %collective-permute-done.9.refs_3_.d), channel_id=1, source_target_pairs={{0,1},{1,0},{2,3},{3,2},{4,5},{5,4},{6,7},{7,6},{8,9},{9,8},{10,11... | collective-permute-start | bytes 393224 | tf_op jit(solution)/shard_map/ppermute | solution.py:45
  39.9 1.3 %collective-permute-start.8 = (bf16[128,512]{1,0:T(8,128)(2,1)S(1)}, bf16[128,512]{1,0:T(8,128)(2,1)S(1)}, u32[]{:S(2)}, u32[]{:S(2)}) collective-permute-start(bf16[128,512]{1,0:T(8,128)(2,1)S(1)} %collective-permute-done.7.refs_2_.c), channel_id=1, source_target_pairs={{0,1},{1,0},{2,3},{3,2},{4,5},{5,4},{6,7},{7,6},{8,9},{9,8},{10,11... | collective-permute-start | bytes 393224 | tf_op jit(solution)/shard_map/ppermute | solution.py:45
  40.1 1.0 copy-start.4
  40.1 1.3 %collective-permute-start.6 = (bf16[128,512]{1,0:T(8,128)(2,1)S(1)}, bf16[128,512]{1,0:T(8,128)(2,1)S(1)}, u32[]{:S(2)}, u32[]{:S(2)}) collective-permute-start(bf16[128,512]{1,0:T(8,128)(2,1)S(1)} %collective-permute-done.5.refs_1_.b), channel_id=1, source_target_pairs={{0,1},{1,0},{2,3},{3,2},{4,5},{5,4},{6,7},{7,6},{8,9},{9,8},{10,11... | collective-permute-start | bytes 393224 | tf_op jit(solution)/shard_map/ppermute | solution.py:45
  42.8 11.2 %collective-permute-start.12 = (bf16[128,1024]{1,0:T(8,128)(2,1)}, bf16[128,1024]{1,0:T(8,128)(2,1)}, u32[]{:S(2)}, u32[]{:S(2)}) collective-permute-start(bf16[128,1024]{1,0:T(8,128)(2,1)} %get-tuple-element.43), channel_id=1, source_target_pairs={{0,2},{1,3},{2,4},{3,5},{4,6},{5,7},{6,0},{7,1},{8,10},{9,11},{10,... | collective-permute-start | bytes 786440 | tf_op jit(solution)/shard_map/ppermute | solution.py:45
  44.3 13.5 %collective-permute-start.14 = (bf16[128,1024]{1,0:T(8,128)(2,1)}, bf16[128,1024]{1,0:T(8,128)(2,1)}, u32[]{:S(2)}, u32[]{:S(2)}) collective-permute-start(bf16[128,1024]{1,0:T(8,128)(2,1)} %get-tuple-element.44), channel_id=1, source_target_pairs={{0,6},{1,7},{2,0},{3,1},{4,2},{5,3},{6,4},{7,5},{8,14},{9,15},{10,... | collective-permute-start | bytes 786440 | tf_op jit(solution)/shard_map/ppermute | solution.py:45
  47.0 12.4 %collective-permute-start.13 = (bf16[128,1024]{1,0:T(8,128)(2,1)}, bf16[128,1024]{1,0:T(8,128)(2,1)}, u32[]{:S(2)}, u32[]{:S(2)}) collective-permute-start(bf16[128,1024]{1,0:T(8,128)(2,1)} %shard_map.86), channel_id=1, source_target_pairs={{0,4},{1,5},{2,6},{3,7},{4,0},{5,1},{6,2},{7,3},{8,12},{9,13},{10,... | collective-permute-start | bytes 786440 | tf_op jit(solution)/shard_map/ppermute | solution.py:45
  49.5 0.9 copy-start.5
  50.7 1.6 %copy-start.1 = (bf16[512,1,2048]{2,0,1:T(8,128)(2,1)S(1)}, bf16[512,1,2048]{2,0,1:T(8,128)(2,1)}, u32[]{:S(2)}) copy-start(bf16[512,1,2048]{2,0,1:T(8,128)(2,1)} %param.6) | copy-start | bytes 6291460
  52.3 12.0 %copy-start.2 = (bf16[512,1,2048]{2,0,1:T(8,128)(2,1)S(1)}, bf16[512,1,2048]{2,0,1:T(8,128)(2,1)}, u32[]{:S(2)}) copy-start(bf16[512,1,2048]{2,0,1:T(8,128)(2,1)} %param.6) | copy-start | bytes 6291460
  52.3 12.0 %copy-start.7 = (f32[1,2048]{1,0:T(1,128)S(1)}, f32[1,2048]{1,0:T(1,128)}, u32[]{:S(2)}) copy-start(f32[1,2048]{1,0:T(1,128)} %bias.1) | copy-start | bytes 24580
  60.7 4.4 %collective-permute-start.15 = (bf16[128,256]{1,0:T(8,128)(2,1)S(1)}, bf16[128,256]{1,0:T(8,128)(2,1)S(1)}, u32[]{:S(2)}, u32[]{:S(2)}) collective-permute-start(bf16[128,256]{1,0:T(8,128)(2,1)S(1)} %get-tuple-element.51), channel_id=1, source_target_pairs={{0,8},{1,9},{2,10},{3,11},{4,12},{5,13},{6,14},{7,15},{8,0},{9,1},... | collective-permute-start | bytes 196616 | tf_op jit(solution)/shard_map/ppermute | solution.py:45
  60.8 6.7 %collective-permute-start.16 = (bf16[128,256]{1,0:T(8,128)(2,1)S(1)}, bf16[128,256]{1,0:T(8,128)(2,1)S(1)}, u32[]{:S(2)}, u32[]{:S(2)}) collective-permute-start(bf16[128,256]{1,0:T(8,128)(2,1)S(1)} %get-tuple-element.52), channel_id=1, source_target_pairs={{0,16},{1,17},{2,18},{3,19},{4,20},{5,21},{6,22},{7,23},{8,24},{9,... | collective-permute-start | bytes 196616 | tf_op jit(solution)/shard_map/ppermute | solution.py:45
  63.4 6.4 %collective-permute-start.17 = (bf16[128,256]{1,0:T(8,128)(2,1)S(1)}, bf16[128,256]{1,0:T(8,128)(2,1)S(1)}, u32[]{:S(2)}, u32[]{:S(2)}) collective-permute-start(bf16[128,256]{1,0:T(8,128)(2,1)S(1)} %get-tuple-element.53), channel_id=1, source_target_pairs={{0,24},{1,25},{2,26},{3,27},{4,28},{5,29},{6,30},{7,31},{8,16},{9,... | collective-permute-start | bytes 196616 | tf_op jit(solution)/shard_map/ppermute | solution.py:45
  69.8 6.5 %collective-permute-start.20 = (bf16[128,256]{1,0:T(8,128)(2,1)S(1)}, bf16[128,256]{1,0:T(8,128)(2,1)S(1)}, u32[]{:S(2)}, u32[]{:S(2)}) collective-permute-start(bf16[128,256]{1,0:T(8,128)(2,1)S(1)} %shard_map.89.a), channel_id=1, source_target_pairs={{0,24},{1,25},{2,26},{3,27},{4,28},{5,29},{6,30},{7,31},{8,16},{9,... | collective-permute-start | bytes 196616 | tf_op jit(solution)/shard_map/ppermute | solution.py:45
  70.8 5.4 %collective-permute-start.19 = (bf16[128,256]{1,0:T(8,128)(2,1)S(1)}, bf16[128,256]{1,0:T(8,128)(2,1)S(1)}, u32[]{:S(2)}, u32[]{:S(2)}) collective-permute-start(bf16[128,256]{1,0:T(8,128)(2,1)S(1)} %shard_map.89.a), channel_id=1, source_target_pairs={{0,16},{1,17},{2,18},{3,19},{4,20},{5,21},{6,22},{7,23},{8,24},{9,... | collective-permute-start | bytes 196616 | tf_op jit(solution)/shard_map/ppermute | solution.py:45
  73.0 4.3 %collective-permute-start.18 = (bf16[128,256]{1,0:T(8,128)(2,1)S(1)}, bf16[128,256]{1,0:T(8,128)(2,1)S(1)}, u32[]{:S(2)}, u32[]{:S(2)}) collective-permute-start(bf16[128,256]{1,0:T(8,128)(2,1)S(1)} %shard_map.89.a), channel_id=1, source_target_pairs={{0,8},{1,9},{2,10},{3,11},{4,12},{5,13},{6,14},{7,15},{8,0},{9,1},... | collective-permute-start | bytes 196616 | tf_op jit(solution)/shard_map/ppermute | solution.py:45
  77.3 11.9 %collective-permute-start.26 = (bf16[128,1024]{1,0:T(8,128)(2,1)S(1)}, bf16[128,1024]{1,0:T(8,128)(2,1)S(1)}, u32[]{:S(2)}, u32[]{:S(2)}) collective-permute-start(bf16[128,1024]{1,0:T(8,128)(2,1)S(1)} %shard_map.90.refs_0_), channel_id=1, source_target_pairs={{0,2},{1,3},{2,4},{3,5},{4,6},{5,7},{6,0},{7,1},{8,10},{9,11},{10,... | collective-permute-start | bytes 786440 | tf_op jit(solution)/shard_map/ppermute | solution.py:45
  78.2 11.0 %collective-permute-start.24 = (bf16[128,1024]{1,0:T(8,128)(2,1)S(1)}, bf16[128,1024]{1,0:T(8,128)(2,1)S(1)}, u32[]{:S(2)}, u32[]{:S(2)}) collective-permute-start(bf16[128,1024]{1,0:T(8,128)(2,1)S(1)} %shard_map.90.refs_0_), channel_id=1, source_target_pairs={{0,4},{1,5},{2,6},{3,7},{4,0},{5,1},{6,2},{7,3},{8,12},{9,13},{10,... | collective-permute-start | bytes 786440 | tf_op jit(solution)/shard_map/ppermute | solution.py:45
  80.2 9.6 %collective-permute-start.22 = (bf16[128,1024]{1,0:T(8,128)(2,1)S(1)}, bf16[128,1024]{1,0:T(8,128)(2,1)S(1)}, u32[]{:S(2)}, u32[]{:S(2)}) collective-permute-start(bf16[128,1024]{1,0:T(8,128)(2,1)S(1)} %shard_map.90.refs_0_), channel_id=1, source_target_pairs={{0,6},{1,7},{2,0},{3,1},{4,2},{5,3},{6,4},{7,5},{8,14},{9,15},{10,... | collective-permute-start | bytes 786440 | tf_op jit(solution)/shard_map/ppermute | solution.py:45
  80.9 9.6 %collective-permute-start.21 = (bf16[128,1024]{1,0:T(8,128)(2,1)S(1)}, bf16[128,1024]{1,0:T(8,128)(2,1)S(1)}, u32[]{:S(2)}, u32[]{:S(2)}) collective-permute-start(bf16[128,1024]{1,0:T(8,128)(2,1)S(1)} %shard_map.90.refs_0_), channel_id=1, source_target_pairs={{0,1},{1,0},{2,3},{3,2},{4,5},{5,4},{6,7},{7,6},{8,9},{9,8},{10,11... | collective-permute-start | bytes 786440 | tf_op jit(solution)/shard_map/ppermute | solution.py:45
  89.2 1.5 %collective-permute-start.27 = (bf16[128,1024]{1,0:T(8,128)(2,1)S(1)}, bf16[128,1024]{1,0:T(8,128)(2,1)S(1)}, u32[]{:S(2)}, u32[]{:S(2)}) collective-permute-start(bf16[128,1024]{1,0:T(8,128)(2,1)S(1)} %collective-permute-done.26.refs_3_), channel_id=1, source_target_pairs={{0,1},{1,0},{2,3},{3,2},{4,5},{5,4},{6,7},{7,6},{8,9},{9,8},{10,11... | collective-permute-start | bytes 786440 | tf_op jit(solution)/shard_map/ppermute | solution.py:45
  89.2 1.9 %collective-permute-start.25 = (bf16[128,1024]{1,0:T(8,128)(2,1)S(1)}, bf16[128,1024]{1,0:T(8,128)(2,1)S(1)}, u32[]{:S(2)}, u32[]{:S(2)}) collective-permute-start(bf16[128,1024]{1,0:T(8,128)(2,1)S(1)} %collective-permute-done.24.refs_2_), channel_id=1, source_target_pairs={{0,1},{1,0},{2,3},{3,2},{4,5},{5,4},{6,7},{7,6},{8,9},{9,8},{10,11... | collective-permute-start | bytes 786440 | tf_op jit(solution)/shard_map/ppermute | solution.py:45
  89.8 1.6 %collective-permute-start.23 = (bf16[128,1024]{1,0:T(8,128)(2,1)S(1)}, bf16[128,1024]{1,0:T(8,128)(2,1)S(1)}, u32[]{:S(2)}, u32[]{:S(2)}) collective-permute-start(bf16[128,1024]{1,0:T(8,128)(2,1)S(1)} %collective-permute-done.22.refs_1_), channel_id=1, source_target_pairs={{0,1},{1,0},{2,3},{3,2},{4,5},{5,4},{6,7},{7,6},{8,9},{9,8},{10,11... | collective-permute-start | bytes 786440 | tf_op jit(solution)/shard_map/ppermute | solution.py:45
  92.2 7.2 %collective-permute-start.28 = (bf16[128,512]{1,0:T(8,128)(2,1)S(1)}, bf16[128,512]{1,0:T(8,128)(2,1)S(1)}, u32[]{:S(2)}, u32[]{:S(2)}) collective-permute-start(bf16[128,512]{1,0:T(8,128)(2,1)S(1)} %get-tuple-element.57), channel_id=1, source_target_pairs={{0,64},{1,65},{2,66},{3,67},{4,68},{5,69},{6,70},{7,71},{8,72},{9,... | collective-permute-start | bytes 393224 | tf_op jit(solution)/shard_map/ppermute | solution.py:45
  93.5 8.7 %collective-permute-start.29 = (bf16[128,512]{1,0:T(8,128)(2,1)S(1)}, bf16[128,512]{1,0:T(8,128)(2,1)S(1)}, u32[]{:S(2)}, u32[]{:S(2)}) collective-permute-start(bf16[128,512]{1,0:T(8,128)(2,1)S(1)} %get-tuple-element.58), channel_id=1, source_target_pairs={{0,128},{1,129},{2,130},{3,131},{4,132},{5,133},{6,134},{7,135},{8... | collective-permute-start | bytes 393224 | tf_op jit(solution)/shard_map/ppermute | solution.py:45
  95.9 6.5 %collective-permute-start.30 = (bf16[128,512]{1,0:T(8,128)(2,1)S(1)}, bf16[128,512]{1,0:T(8,128)(2,1)S(1)}, u32[]{:S(2)}, u32[]{:S(2)}) collective-permute-start(bf16[128,512]{1,0:T(8,128)(2,1)S(1)} %get-tuple-element.59), channel_id=1, source_target_pairs={{0,192},{1,193},{2,194},{3,195},{4,196},{5,197},{6,198},{7,199},{8... | collective-permute-start | bytes 393224 | tf_op jit(solution)/shard_map/ppermute | solution.py:45
  102.5 11.5 %collective-permute-start.31 = (bf16[128,512]{1,0:T(8,128)(2,1)S(1)}, bf16[128,512]{1,0:T(8,128)(2,1)S(1)}, u32[]{:S(2)}, u32[]{:S(2)}) collective-permute-start(bf16[128,512]{1,0:T(8,128)(2,1)S(1)} %get-tuple-element.66), channel_id=1, source_target_pairs={{0,32},{1,33},{2,34},{3,35},{4,36},{5,37},{6,38},{7,39},{8,40},{9,... | collective-permute-start | bytes 393224 | tf_op jit(solution)/shard_map/ppermute | solution.py:45
  114.1 7.7 %collective-permute-start.34 = (bf16[128,512]{1,0:T(8,128)(2,1)S(1)}, bf16[128,512]{1,0:T(8,128)(2,1)S(1)}, u32[]{:S(2)}, u32[]{:S(2)}) collective-permute-start(bf16[128,512]{1,0:T(8,128)(2,1)S(1)} %shard_map.95.a), channel_id=1, source_target_pairs={{0,64},{1,65},{2,66},{3,67},{4,68},{5,69},{6,70},{7,71},{8,72},{9,... | collective-permute-start | bytes 393224 | tf_op jit(solution)/shard_map/ppermute | solution.py:45
  116.3 7.2 %collective-permute-start.33 = (bf16[128,512]{1,0:T(8,128)(2,1)S(1)}, bf16[128,512]{1,0:T(8,128)(2,1)S(1)}, u32[]{:S(2)}, u32[]{:S(2)}) collective-permute-start(bf16[128,512]{1,0:T(8,128)(2,1)S(1)} %shard_map.95.a), channel_id=1, source_target_pairs={{0,128},{1,129},{2,130},{3,131},{4,132},{5,133},{6,134},{7,135},{8... | collective-permute-start | bytes 393224 | tf_op jit(solution)/shard_map/ppermute | solution.py:45
  118.8 5.0 %collective-permute-start.32 = (bf16[128,512]{1,0:T(8,128)(2,1)S(1)}, bf16[128,512]{1,0:T(8,128)(2,1)S(1)}, u32[]{:S(2)}, u32[]{:S(2)}) collective-permute-start(bf16[128,512]{1,0:T(8,128)(2,1)S(1)} %shard_map.95.a), channel_id=1, source_target_pairs={{0,192},{1,193},{2,194},{3,195},{4,196},{5,197},{6,198},{7,199},{8... | collective-permute-start | bytes 393224 | tf_op jit(solution)/shard_map/ppermute | solution.py:45

commit v3 on v2

--- a/solution.py
+++ b/solution.py
@@ -1,3 +1,5 @@
+import math
+
 import jax
 import jax.numpy as jnp
 from jax import lax
@@ -10,8 +12,9 @@
 bf16 = jnp.bfloat16
 f32 = jnp.float32
 MIB = 1024 * 1024
+FIRST_MIB = 52
 LIMIT = pltpu.CompilerParams(vmem_limit_bytes=40 * MIB)
-FIRST = pltpu.CompilerParams(vmem_limit_bytes=56 * MIB)
+FIRST = pltpu.CompilerParams(vmem_limit_bytes=FIRST_MIB * MIB)
 after = lax.optimization_barrier
 
 
@@ -59,6 +62,10 @@
     return jax.ShapeDtypeStruct(shape, dtype)
 
 
+def held(shape, dtype):
+    return pltpu.VMEM(shape, dtype)
+
+
 def cost(flops, size):
     return pl.CostEstimate(flops=flops, bytes_accessed=size, transcendentals=0)
 
@@ -67,7 +74,7 @@
     in_specs = [
         pl.BlockSpec(memory_space=pltpu.SMEM if a.dtype == jnp.int32 and a.ndim == 1 else pltpu.VMEM) for a in args
     ]
-    size = sum(a.size * a.dtype.itemsize for a in args) + sum(o.size * o.dtype.itemsize for o in outs)
+    size = sum(a.size * a.dtype.itemsize for a in args) + sum(math.prod(o.shape) * 4 for o in outs)
     return pl.pallas_call(
         kernel,
         out_shape=outs,
@@ -227,16 +234,24 @@
         out[:, at] = (loss_scale * (dot(codes[...], ref[...]) + factor[...] * dec[:, at].astype(f32))).astype(bf16)
 
 
-def grad_kernel(acts, a, b, c, d, out, rhs):
+def grad_kernel(acts, a, b, out):
+    m, n = a.shape[0], 512
+    rhs = jnp.concatenate([a[...], b[...]], 0)
+    for i in range(0, out.shape[0], n):
+        out[i : i + n, :] = dot(acts[i : i + n, : 2 * m], rhs)
+
+
+def grad_rest_kernel(acts, a, b, total, out, rhs):
     m, n = a.shape[0], out.shape[0]
     step = pl.program_id(0)
 
     @pl.when(step == 0)
     def _():
-        for j, ref in enumerate((a, b, c, d)):
-            rhs[j * m : (j + 1) * m, :] = ref[...]
-
-    out[...] = dot(acts[pl.ds(pl.multiple_of(step * n, n), n), :], rhs[...]).astype(bf16)
+        rhs[:m, :] = a[...]
+        rhs[m:, :] = b[...]
+
+    rows = pl.ds(pl.multiple_of(step * n, n), n)
+    out[...] = (total[rows, :] + dot(acts[rows, 2 * m :], rhs[...])).astype(bf16)
 
 
 def placed(kernel, idx, grid, ins, outs, *args, flops=0, size=MIB, scratch=(), limit=LIMIT):
@@ -270,12 +285,12 @@
     flat = acts.reshape(rows, width)
     enc = w_enc.reshape(width, latents)
     dec = w_dec.reshape(latents, width)
-    tile = sds((ny, latents), bf16)
+    tile = held((ny, latents), bf16)
 
     whole = lambda j, idx: (0, 0)
     *sends, keep = pl.pallas_call(
         pre_kernel,
-        out_shape=[tile] * 3 + [sds((ny, latents), f32)],
+        out_shape=[tile] * 3 + [held((ny, latents), f32)],
         in_specs=[pl.BlockSpec(memory_space=pl.ANY)] * 2,
         out_specs=[pl.BlockSpec(memory_space=pltpu.VMEM)] * 4,
         scratch_shapes=[
@@ -290,7 +305,7 @@
 
     def over_layers(sends, keep):
         got = {j: exchange(sends[j - 1], "y", j) for j in FAR_FIRST}
-        keep, send = local(sum_kernel, [sds((ny, latents), f32), tile], keep, got[1], got[2], got[3])
+        keep, send = local(sum_kernel, [held((ny, latents), f32), tile], keep, got[1], got[2], got[3])
         return keep, exchange(send, "h")
 
     keep, got = over_layers(sends, keep)
@@ -321,14 +336,14 @@
     codes_other = [exchange(v, "c") for v in codes]
 
     (recon_own,) = local(
-        recon_own_kernel, [sds((rows, half), f32)], *codes, dec, flops=matmul // 2,
+        recon_own_kernel, [held((rows, half), f32)], *codes, dec, flops=matmul // 2,
         scratch=[pltpu.VMEM((rows, latents), bf16)],
     )
 
     def recon(blocks, dtypes):
         return local(
             lambda *refs: recon_kernel(blocks, *refs),
-            [sds((ny, half), t) for t in dtypes],
+            [held((ny, half), t) for t in dtypes],
             *codes_other, dec_other, recon_own,
             flops=matmul * len(blocks) // 8,
             scratch=[pltpu.VMEM((len(blocks) * ny, latents), bf16)],
@@ -340,28 +355,28 @@
     flat_b, near_3 = after((flat, near_3))
     (acts_t,) = placed(
         turn_acts_kernel, idx, 4,
-        [((r, width), lambda j, idx, b=b: (idx[j] * 4 + idx[4 + b], 0)) for b in range(4)],
+        [((r, width), lambda j, idx, b=b: (idx[j * 3 % 4] * 4 + idx[4 + b], 0)) for b in range(4)],
         [((width, rows), bf16, (width, ny), lambda j, idx: (0, j))], *[flat_b] * 4, size=4 * MIB,
     )
     codes_t, factor = local(
-        turn_codes_kernel, [sds((latents, rows), bf16), sds((latents, 1), f32)], *codes, lengths[:, None]
+        turn_codes_kernel, [held((latents, rows), bf16), held((latents, 1), f32)], *codes, lengths[:, None]
     )
     got[1], acts_t, codes_t = after((got[1], acts_t, codes_t))
     keep, *sends = local(
-        split_kernel, [sds((ny, q), f32)] + [sds((ny, q), bf16)] * 3, keep, got[1], got[2], got[3]
+        split_kernel, [held((ny, q), f32)] + [held((ny, q), bf16)] * 3, keep, got[1], got[2], got[3]
     )
     got = {j: exchange(sends[j - 1], "z", j) for j in LINE}
-    (error,) = local(error_kernel, [sds((ny, q), bf16)], keep, got[1], got[2], got[3], offset)
-    (error,) = local(columns_kernel, [sds((ny, half), bf16)], *gather(error, "z", LINE))
+    (error,) = local(error_kernel, [held((ny, q), bf16)], keep, got[1], got[2], got[3], offset)
+    (error,) = local(columns_kernel, [held((ny, half), bf16)], *gather(error, "z", LINE))
     errors = gather(error, "x", FAR_FIRST)
     errors_other = [exchange(v, "c") for v in errors]
 
     error_own, back_own = local(
-        back_own_kernel, [sds((rows, half), bf16), sds((rows, latents), f32)], *errors, dec, lengths[None, :],
+        back_own_kernel, [held((rows, half), bf16), held((rows, latents), f32)], *errors, dec, lengths[None, :],
         flops=matmul // 2,
     )
     error_other, *sends, keep = local(
-        back_kernel, [sds((rows, half), bf16)] + [tile] * 3 + [sds((ny, latents), f32)],
+        back_kernel, [held((rows, half), bf16)] + [tile] * 3 + [held((ny, latents), f32)],
         *errors_other, dec, back_own,
         flops=matmul // 2,
     )
@@ -387,17 +402,18 @@
     (shard,) = local(dpre_kernel, [tile], keep, got, active)
     dpre = gather(shard, "y", FAR_FIRST)
 
-    m = width // 8
+    (total,) = local(grad_kernel, [held((width, latents), f32)], acts_t, dpre[0], dpre[3], flops=matmul // 2)
+    m = width // 4
     grad_enc = pl.pallas_call(
-        grad_kernel,
+        grad_rest_kernel,
         out_shape=sds((width, latents), bf16),
-        grid=(8,),
-        in_specs=[pl.BlockSpec(memory_space=pltpu.VMEM)] * 5,
+        grid=(4,),
+        in_specs=[pl.BlockSpec(memory_space=pltpu.VMEM)] * 4,
         out_specs=pl.BlockSpec((m, latents), lambda j: (j, 0)),
-        scratch_shapes=[pltpu.VMEM((rows, latents), bf16)],
+        scratch_shapes=[pltpu.VMEM((2 * ny, latents), bf16)],
         compiler_params=LIMIT,
-        cost_estimate=cost(matmul, 5 * MIB),
-    )(acts_t, *dpre)
+        cost_estimate=cost(matmul // 2, 5 * MIB),
+    )(acts_t, dpre[2], dpre[1], total)
     return (grad_enc.reshape(w_enc.shape), grad_dec.reshape(w_dec.shape))
 
 

time: 128 us -> 127 us (level)
    pallas_call x2, Pallas kernels: 8.06 us -> 6.13 us  [the longest x1 3.62 us: body(): pl.pallas_call(pre_kernel, out_shape=[tile] * 3 + [held((ny, latents), f3...]
    pallas_call x13 -> x14, Pallas kernels: 6.39 us -> 8.07 us  [local(): pl.pallas_call(kernel, out_shape=outs, in_specs=in_specs, out_specs=[pl.B...]
    unnamed x18 -> x16, local copies, waits for them, and re-layouts: 3.47 us -> 2.52 us
  transfers between devices with their start and end apart: 35 -> 35, of which waited for: 26 -> 25; matrix products, arithmetic and copies ran while one was open for 1% -> 1% of each run, Pallas kernels for 7% -> 8%
where the time goes in v3:
time: 127 us; the launch traced here: 126 us
  waiting for transfers between devices  52.1 us (41%)
  starting transfers between devices  49.4 us (39%)
  Pallas kernels  20.9 us (16%)
  local copies, waits for them, and re-layouts  2.76 us (2%)
    ppermute x35, waiting for transfers between devices, exchange(): return lax.ppermute(v, ('layer', 'latent'), perm)  52.1 us
    ppermute x35, starting transfers between devices, exchange(): return lax.ppermute(v, ('layer', 'latent'), perm)  49.4 us
    pallas_call x14, Pallas kernels, local(): pl.pallas_call(kernel, out_shape=outs, in_specs=in_specs, out_specs=[pl.B...  8.07 us
    pallas_call x4, Pallas kernels, placed(): pl.pallas_call(kernel, out_shape=[sds(o[0], o[1]) for o in outs], grid_sp...  3.69 us
    pallas_call x1, Pallas kernels, body(): pl.pallas_call(pre_kernel, out_shape=[tile] * 3 + [held((ny, latents), f3...  3.62 us
    pallas_call x1, Pallas kernels, body(): pl.pallas_call(cross_kernel, out_shape=sds((latents, width), bf16), grid=...  2.99 us
  transfers between devices with their start and end apart: 35, of which 25 were waited for; matrix products, arithmetic and copies ran while one was open for 1% of the time, Pallas kernels for 8%

profile of v3, /device:TPU:32, one launch (start us, length us, event | category | flops | bytes accessed | tf_op | source)
XLA Modules:
  0.0 126.4 jit_solution(3405725899318345507)
XLA Ops:
  0.6 3.6 %shard_map.77 = (bf16[128,512]{1,0:T(8,128)(2,1)}, bf16[128,512]{1,0:T(8,128)(2,1)}, bf16[128,512]{1,0:T(8,128)(2,1)}, f32[128,512]{1,0:T(8,128)S(1)}) custom-call(bf16[512,2048]{1,0:T(8,128)(2,1)} %bitcast.28, bf16[2048,512]{1,0:T(8,128)(2,1)} %bitcast.38), custom_call_target="tpu_custom_call" | custom-call | flops 1073741824 | bytes 6291456 | tf_op jit(solution)/shard_map/pallas_call | solution.py:291
  4.3 1.7 %collective-permute-start = (bf16[128,512]{1,0:T(8,128)(2,1)}, bf16[128,512]{1,0:T(8,128)(2,1)S(1)}, u32[]{:S(2)}, u32[]{:S(2)}) collective-permute-start(bf16[128,512]{1,0:T(8,128)(2,1)} %get-tuple-element.36), channel_id=1, source_target_pairs={{0,64},{1,65},{2,66},{3,67},{4,68},{5,69},{6,70},{7,71},{8,72},{9,... | collective-permute-start | bytes 393224 | tf_op jit(solution)/shard_map/ppermute | solution.py:48
  5.9 2.9 %collective-permute-start.1 = (bf16[128,512]{1,0:T(8,128)(2,1)}, bf16[128,512]{1,0:T(8,128)(2,1)}, u32[]{:S(2)}, u32[]{:S(2)}) collective-permute-start(bf16[128,512]{1,0:T(8,128)(2,1)} %get-tuple-element.37), channel_id=1, source_target_pairs={{0,128},{1,129},{2,130},{3,131},{4,132},{5,133},{6,134},{7,135},{8... | collective-permute-start | bytes 393224 | tf_op jit(solution)/shard_map/ppermute | solution.py:48
  8.8 1.3 %collective-permute-start.2 = (bf16[128,512]{1,0:T(8,128)(2,1)}, bf16[128,512]{1,0:T(8,128)(2,1)}, u32[]{:S(2)}, u32[]{:S(2)}) collective-permute-start(bf16[128,512]{1,0:T(8,128)(2,1)} %get-tuple-element.38), channel_id=1, source_target_pairs={{0,192},{1,193},{2,194},{3,195},{4,196},{5,197},{6,198},{7,199},{8... | collective-permute-start | bytes 393224 | tf_op jit(solution)/shard_map/ppermute | solution.py:48
  11.1 4.1 %collective-permute-done.1.b = bf16[128,512]{1,0:T(8,128)(2,1)} collective-permute-done((bf16[128,512]{1,0:T(8,128)(2,1)}, bf16[128,512]{1,0:T(8,128)(2,1)}, u32[]{:S(2)}, u32[]{:S(2)}) %collective-permute-start.1) | collective-permute-done | bytes 131104 | tf_op jit(solution)/shard_map/ppermute | solution.py:48
  15.2 1.0 shard_map.78
  16.9 6.4 %collective-permute-start.3 = (bf16[128,512]{1,0:T(8,128)(2,1)S(1)}, bf16[128,512]{1,0:T(8,128)(2,1)S(1)}, u32[]{:S(2)}, u32[]{:S(2)}) collective-permute-start(bf16[128,512]{1,0:T(8,128)(2,1)S(1)} %get-tuple-element.40), channel_id=1, source_target_pairs={{0,32},{1,33},{2,34},{3,35},{4,36},{5,37},{6,38},{7,39},{8,40},{9,... | collective-permute-start | bytes 393224 | tf_op jit(solution)/shard_map/ppermute | solution.py:48
  24.0 6.3 %collective-permute-done.3.got = bf16[128,512]{1,0:T(8,128)(2,1)S(1)} collective-permute-done((bf16[128,512]{1,0:T(8,128)(2,1)S(1)}, bf16[128,512]{1,0:T(8,128)(2,1)S(1)}, u32[]{:S(2)}, u32[]{:S(2)}) %collective-permute-start.3) | collective-permute-done | bytes 131104 | tf_op jit(solution)/shard_map/ppermute | solution.py:48
  30.3 1.3 %collective-permute-start.9 = (bf16[128,512]{1,0:T(8,128)(2,1)S(1)}, bf16[128,512]{1,0:T(8,128)(2,1)S(1)}, u32[]{:S(2)}, u32[]{:S(2)}) collective-permute-start(bf16[128,512]{1,0:T(8,128)(2,1)S(1)} %shard_map.80.refs_0_.a), channel_id=1, source_target_pairs={{0,64},{1,65},{2,66},{3,67},{4,68},{5,69},{6,70},{7,71},{8,72},{9,... | collective-permute-start | bytes 393224 | tf_op jit(solution)/shard_map/ppermute | solution.py:48
  31.6 2.4 %collective-permute-start.7 = (bf16[128,512]{1,0:T(8,128)(2,1)S(1)}, bf16[128,512]{1,0:T(8,128)(2,1)S(1)}, u32[]{:S(2)}, u32[]{:S(2)}) collective-permute-start(bf16[128,512]{1,0:T(8,128)(2,1)S(1)} %shard_map.80.refs_0_.a), channel_id=1, source_target_pairs={{0,128},{1,129},{2,130},{3,131},{4,132},{5,133},{6,134},{7,135},{8... | collective-permute-start | bytes 393224 | tf_op jit(solution)/shard_map/ppermute | solution.py:48
  34.0 1.6 %collective-permute-start.5 = (bf16[128,512]{1,0:T(8,128)(2,1)S(1)}, bf16[128,512]{1,0:T(8,128)(2,1)S(1)}, u32[]{:S(2)}, u32[]{:S(2)}) collective-permute-start(bf16[128,512]{1,0:T(8,128)(2,1)S(1)} %shard_map.80.refs_0_.a), channel_id=1, source_target_pairs={{0,192},{1,193},{2,194},{3,195},{4,196},{5,197},{6,198},{7,199},{8... | collective-permute-start | bytes 393224 | tf_op jit(solution)/shard_map/ppermute | solution.py:48
  35.6 2.0 %collective-permute-done.9.refs_3_.d = bf16[128,512]{1,0:T(8,128)(2,1)S(1)} collective-permute-done((bf16[128,512]{1,0:T(8,128)(2,1)S(1)}, bf16[128,512]{1,0:T(8,128)(2,1)S(1)}, u32[]{:S(2)}, u32[]{:S(2)}) %collective-permute-start.9) | collective-permute-done | bytes 131104 | tf_op jit(solution)/shard_map/ppermute | solution.py:48
  37.6 2.4 %collective-permute-done.7.refs_2_.c = bf16[128,512]{1,0:T(8,128)(2,1)S(1)} collective-permute-done((bf16[128,512]{1,0:T(8,128)(2,1)S(1)}, bf16[128,512]{1,0:T(8,128)(2,1)S(1)}, u32[]{:S(2)}, u32[]{:S(2)}) %collective-permute-start.7) | collective-permute-done | bytes 131104 | tf_op jit(solution)/shard_map/ppermute | solution.py:48
  41.5 1.3 %shard_map.83 = (bf16[128,1024]{1,0:T(8,128)(2,1)}, bf16[128,1024]{1,0:T(8,128)(2,1)}, f32[128,1024]{1,0:T(8,128)S(1)}) custom-call(bf16[128,512]{1,0:T(8,128)(2,1)S(1)} %collective-permute-done.4.refs_0_, bf16[128,512]{1,0:T(8,128)(2,1)S(1)} %collective-permute-done.6.refs_1_, bf16[128,512]{1,0:T(8,128)(2,1)S(1)} %collective-permute-done.8.refs_2_, ...), custom_call_target="tpu_custom_call" | custom-call | flops 402653184 | bytes 5242880 | tf_op jit(solution)/shard_map/pallas_call | solution.py:78
  42.8 1.5 %collective-permute-start.12 = (bf16[128,1024]{1,0:T(8,128)(2,1)}, bf16[128,1024]{1,0:T(8,128)(2,1)}, u32[]{:S(2)}, u32[]{:S(2)}) collective-permute-start(bf16[128,1024]{1,0:T(8,128)(2,1)} %get-tuple-element.43), channel_id=1, source_target_pairs={{0,2},{1,3},{2,4},{3,5},{4,6},{5,7},{6,0},{7,1},{8,10},{9,11},{10,... | collective-permute-start | bytes 786440 | tf_op jit(solution)/shard_map/ppermute | solution.py:48
  44.3 1.7 %collective-permute-start.14 = (bf16[128,1024]{1,0:T(8,128)(2,1)}, bf16[128,1024]{1,0:T(8,128)(2,1)}, u32[]{:S(2)}, u32[]{:S(2)}) collective-permute-start(bf16[128,1024]{1,0:T(8,128)(2,1)} %get-tuple-element.44), channel_id=1, source_target_pairs={{0,6},{1,7},{2,0},{3,1},{4,2},{5,3},{6,4},{7,5},{8,14},{9,15},{10,... | collective-permute-start | bytes 786440 | tf_op jit(solution)/shard_map/ppermute | solution.py:48
  46.1 1.0 shard_map.86
  47.1 1.8 %collective-permute-start.13 = (bf16[128,1024]{1,0:T(8,128)(2,1)}, bf16[128,1024]{1,0:T(8,128)(2,1)}, u32[]{:S(2)}, u32[]{:S(2)}) collective-permute-start(bf16[128,1024]{1,0:T(8,128)(2,1)} %shard_map.86), channel_id=1, source_target_pairs={{0,4},{1,5},{2,6},{3,7},{4,0},{5,1},{6,2},{7,3},{8,12},{9,13},{10,... | collective-permute-start | bytes 786440 | tf_op jit(solution)/shard_map/ppermute | solution.py:48
  49.6 0.9 copy-done.5
  50.8 1.6 %copy-done.1 = bf16[512,1,2048]{2,0,1:T(8,128)(2,1)S(1)} copy-done((bf16[512,1,2048]{2,0,1:T(8,128)(2,1)S(1)}, bf16[512,1,2048]{2,0,1:T(8,128)(2,1)}, u32[]{:S(2)}) %copy-start.1) | copy-done | bytes 2097176
  52.4 1.7 %shard_map.84.acts = bf16[2048,512]{1,0:T(8,128)(2,1)S(1)} custom-call(s32[14]{0:T(128)S(1)} %stack.59.idx, bf16[512,2048]{1,0:T(8,128)(2,1)S(1)} %bitcast.29, bf16[512,2048]{1,0:T(8,128)(2,1)S(1)} %bitcast.30, bf16[512,2048]{1,0:T(8,128)(2,1)S(1)} %bitcast.31, bf16[512,2048]{1,0:T(8,128)(2,1)S(1)} %bitcast.32), custom_call_target="tpu_custom_call" | custom-call | bytes 4194304 | tf_op jit(solution)/shard_map/pallas_call | solution.py:258
  54.1 3.7 %collective-permute-done.14.c = bf16[128,1024]{1,0:T(8,128)(2,1)} collective-permute-done((bf16[128,1024]{1,0:T(8,128)(2,1)}, bf16[128,1024]{1,0:T(8,128)(2,1)}, u32[]{:S(2)}, u32[]{:S(2)}) %collective-permute-start.14) | collective-permute-done | bytes 262176 | tf_op jit(solution)/shard_map/ppermute | solution.py:48
  57.8 1.7 %collective-permute-done.13.b = bf16[128,1024]{1,0:T(8,128)(2,1)} collective-permute-done((bf16[128,1024]{1,0:T(8,128)(2,1)}, bf16[128,1024]{1,0:T(8,128)(2,1)}, u32[]{:S(2)}, u32[]{:S(2)}) %collective-permute-start.13) | collective-permute-done | bytes 262176 | tf_op jit(solution)/shard_map/ppermute | solution.py:48
  59.5 1.3 shard_map.87
  60.9 2.5 %collective-permute-start.16 = (bf16[128,256]{1,0:T(8,128)(2,1)S(1)}, bf16[128,256]{1,0:T(8,128)(2,1)S(1)}, u32[]{:S(2)}, u32[]{:S(2)}) collective-permute-start(bf16[128,256]{1,0:T(8,128)(2,1)S(1)} %get-tuple-element.52), channel_id=1, source_target_pairs={{0,16},{1,17},{2,18},{3,19},{4,20},{5,21},{6,22},{7,23},{8,24},{9,... | collective-permute-start | bytes 196616 | tf_op jit(solution)/shard_map/ppermute | solution.py:48
  63.4 0.9 collective-permute-start.17
  65.1 2.5 %collective-permute-done.16.b = bf16[128,256]{1,0:T(8,128)(2,1)S(1)} collective-permute-done((bf16[128,256]{1,0:T(8,128)(2,1)S(1)}, bf16[128,256]{1,0:T(8,128)(2,1)S(1)}, u32[]{:S(2)}, u32[]{:S(2)}) %collective-permute-start.16) | collective-permute-done | bytes 65568 | tf_op jit(solution)/shard_map/ppermute | solution.py:48
  67.6 2.2 %collective-permute-done.17.c = bf16[128,256]{1,0:T(8,128)(2,1)S(1)} collective-permute-done((bf16[128,256]{1,0:T(8,128)(2,1)S(1)}, bf16[128,256]{1,0:T(8,128)(2,1)S(1)}, u32[]{:S(2)}, u32[]{:S(2)}) %collective-permute-start.17) | collective-permute-done | bytes 65568 | tf_op jit(solution)/shard_map/ppermute | solution.py:48
  69.8 1.1 collective-permute-start.20
  70.9 2.1 %collective-permute-start.19 = (bf16[128,256]{1,0:T(8,128)(2,1)S(1)}, bf16[128,256]{1,0:T(8,128)(2,1)S(1)}, u32[]{:S(2)}, u32[]{:S(2)}) collective-permute-start(bf16[128,256]{1,0:T(8,128)(2,1)S(1)} %shard_map.89.a), channel_id=1, source_target_pairs={{0,16},{1,17},{2,18},{3,19},{4,20},{5,21},{6,22},{7,23},{8,24},{9,... | collective-permute-start | bytes 196616 | tf_op jit(solution)/shard_map/ppermute | solution.py:48
  73.4 2.9 %collective-permute-done.20.d = bf16[128,256]{1,0:T(8,128)(2,1)S(1)} collective-permute-done((bf16[128,256]{1,0:T(8,128)(2,1)S(1)}, bf16[128,256]{1,0:T(8,128)(2,1)S(1)}, u32[]{:S(2)}, u32[]{:S(2)}) %collective-permute-start.20) | collective-permute-done | bytes 65568 | tf_op jit(solution)/shard_map/ppermute | solution.py:48
  76.3 1.0 collective-permute-done.18.b
  78.2 2.1 %collective-permute-start.24 = (bf16[128,1024]{1,0:T(8,128)(2,1)S(1)}, bf16[128,1024]{1,0:T(8,128)(2,1)S(1)}, u32[]{:S(2)}, u32[]{:S(2)}) collective-permute-start(bf16[128,1024]{1,0:T(8,128)(2,1)S(1)} %shard_map.90.refs_0_), channel_id=1, source_target_pairs={{0,4},{1,5},{2,6},{3,7},{4,0},{5,1},{6,2},{7,3},{8,12},{9,13},{10,... | collective-permute-start | bytes 786440 | tf_op jit(solution)/shard_map/ppermute | solution.py:48
  81.0 8.2 %collective-permute-done.26.refs_3_ = bf16[128,1024]{1,0:T(8,128)(2,1)S(1)} collective-permute-done((bf16[128,1024]{1,0:T(8,128)(2,1)S(1)}, bf16[128,1024]{1,0:T(8,128)(2,1)S(1)}, u32[]{:S(2)}, u32[]{:S(2)}) %collective-permute-start.26) | collective-permute-done | bytes 262176 | tf_op jit(solution)/shard_map/ppermute | solution.py:48
  92.3 1.3 %collective-permute-start.28 = (bf16[128,512]{1,0:T(8,128)(2,1)S(1)}, bf16[128,512]{1,0:T(8,128)(2,1)S(1)}, u32[]{:S(2)}, u32[]{:S(2)}) collective-permute-start(bf16[128,512]{1,0:T(8,128)(2,1)S(1)} %get-tuple-element.57), channel_id=1, source_target_pairs={{0,64},{1,65},{2,66},{3,67},{4,68},{5,69},{6,70},{7,71},{8,72},{9,... | collective-permute-start | bytes 393224 | tf_op jit(solution)/shard_map/ppermute | solution.py:48
  93.6 2.4 %collective-permute-start.29 = (bf16[128,512]{1,0:T(8,128)(2,1)S(1)}, bf16[128,512]{1,0:T(8,128)(2,1)S(1)}, u32[]{:S(2)}, u32[]{:S(2)}) collective-permute-start(bf16[128,512]{1,0:T(8,128)(2,1)S(1)} %get-tuple-element.58), channel_id=1, source_target_pairs={{0,128},{1,129},{2,130},{3,131},{4,132},{5,133},{6,134},{7,135},{8... | collective-permute-start | bytes 393224 | tf_op jit(solution)/shard_map/ppermute | solution.py:48
  96.0 1.1 collective-permute-start.30
  97.1 2.4 %collective-permute-done.28.a = bf16[128,512]{1,0:T(8,128)(2,1)S(1)} collective-permute-done((bf16[128,512]{1,0:T(8,128)(2,1)S(1)}, bf16[128,512]{1,0:T(8,128)(2,1)S(1)}, u32[]{:S(2)}, u32[]{:S(2)}) %collective-permute-start.28) | collective-permute-done | bytes 131104 | tf_op jit(solution)/shard_map/ppermute | solution.py:48
  99.5 2.8 %collective-permute-done.29.b = bf16[128,512]{1,0:T(8,128)(2,1)S(1)} collective-permute-done((bf16[128,512]{1,0:T(8,128)(2,1)S(1)}, bf16[128,512]{1,0:T(8,128)(2,1)S(1)}, u32[]{:S(2)}, u32[]{:S(2)}) %collective-permute-start.29) | collective-permute-done | bytes 131104 | tf_op jit(solution)/shard_map/ppermute | solution.py:48
  102.5 5.5 %collective-permute-start.31 = (bf16[128,512]{1,0:T(8,128)(2,1)S(1)}, bf16[128,512]{1,0:T(8,128)(2,1)S(1)}, u32[]{:S(2)}, u32[]{:S(2)}) collective-permute-start(bf16[128,512]{1,0:T(8,128)(2,1)S(1)} %get-tuple-element.66), channel_id=1, source_target_pairs={{0,32},{1,33},{2,34},{3,35},{4,36},{5,37},{6,38},{7,39},{8,40},{9,... | collective-permute-start | bytes 393224 | tf_op jit(solution)/shard_map/ppermute | solution.py:48
  108.0 3.0 %shard_map.94 = bf16[512,2048]{1,0:T(8,128)(2,1)} custom-call(bf16[512,512]{1,0:T(8,128)(2,1)S(1)} %get-tuple-element.61.codes, bf16[512,1024]{1,0:T(8,128)(2,1)S(1)} %get-tuple-element.62.own, bf16[512,1024]{1,0:T(8,128)(2,1)S(1)} %get-tuple-element.63.other, bf16[512,2048]{1,0:T(8,128)(2,1)S(1)} %bitcast.27, f32[512,1]{1,0:T(8,128)S(1)} %get-tuple-element.64.factor), custom_call_target="tpu_custom_call" | custom-call | flops 1073741824 | bytes 8388608 | tf_op jit(solution)/shard_map/pallas_call | solution.py:386
  111.0 3.1 %collective-permute-done.31.got = bf16[128,512]{1,0:T(8,128)(2,1)S(1)} collective-permute-done((bf16[128,512]{1,0:T(8,128)(2,1)S(1)}, bf16[128,512]{1,0:T(8,128)(2,1)S(1)}, u32[]{:S(2)}, u32[]{:S(2)}) %collective-permute-start.31) | collective-permute-done | bytes 131104 | tf_op jit(solution)/shard_map/ppermute | solution.py:48
  114.1 2.3 %collective-permute-start.34 = (bf16[128,512]{1,0:T(8,128)(2,1)S(1)}, bf16[128,512]{1,0:T(8,128)(2,1)S(1)}, u32[]{:S(2)}, u32[]{:S(2)}) collective-permute-start(bf16[128,512]{1,0:T(8,128)(2,1)S(1)} %shard_map.95.a), channel_id=1, source_target_pairs={{0,64},{1,65},{2,66},{3,67},{4,68},{5,69},{6,70},{7,71},{8,72},{9,... | collective-permute-start | bytes 393224 | tf_op jit(solution)/shard_map/ppermute | solution.py:48
  116.4 1.1 collective-permute-start.33
  117.5 1.4 %collective-permute-start.32 = (bf16[128,512]{1,0:T(8,128)(2,1)S(1)}, bf16[128,512]{1,0:T(8,128)(2,1)S(1)}, u32[]{:S(2)}, u32[]{:S(2)}) collective-permute-start(bf16[128,512]{1,0:T(8,128)(2,1)S(1)} %shard_map.95.a), channel_id=1, source_target_pairs={{0,128},{1,129},{2,130},{3,131},{4,132},{5,133},{6,134},{7,135},{8... | collective-permute-start | bytes 393224 | tf_op jit(solution)/shard_map/ppermute | solution.py:48
  118.8 2.9 %collective-permute-done.34.b = bf16[128,512]{1,0:T(8,128)(2,1)S(1)} collective-permute-done((bf16[128,512]{1,0:T(8,128)(2,1)S(1)}, bf16[128,512]{1,0:T(8,128)(2,1)S(1)}, u32[]{:S(2)}, u32[]{:S(2)}) %collective-permute-start.34) | collective-permute-done | bytes 131104 | tf_op jit(solution)/shard_map/ppermute | solution.py:48
  122.5 1.4 %collective-permute-done.32.a = bf16[128,512]{1,0:T(8,128)(2,1)S(1)} collective-permute-done((bf16[128,512]{1,0:T(8,128)(2,1)S(1)}, bf16[128,512]{1,0:T(8,128)(2,1)S(1)}, u32[]{:S(2)}, u32[]{:S(2)}) %collective-permute-start.32) | collective-permute-done | bytes 131104 | tf_op jit(solution)/shard_map/ppermute | solution.py:48
  123.9 2.5 %shard_map.97 = bf16[2048,512]{1,0:T(8,128)(2,1)} custom-call(bf16[2048,512]{1,0:T(8,128)(2,1)S(1)} %shard_map.84.acts, bf16[128,512]{1,0:T(8,128)(2,1)S(1)} %collective-permute-done.32.a, bf16[128,512]{1,0:T(8,128)(2,1)S(1)} %collective-permute-done.33.b, f32[2048,512]{1,0:T(8,128)S(1)} %shard_map.96.total), custom_call_target="tpu_custom_call" | custom-call | flops 536870912 | bytes 5242880 | tf_op jit(solution)/shard_map/pallas_call | solution.py:407
  (63 shorter events, 11.7 us)
Async XLA Ops:
  0.6 15.6 %copy-start = (bf16[512,1,2048]{2,0,1:T(8,128)(2,1)S(1)}, bf16[512,1,2048]{2,0,1:T(8,128)(2,1)}, u32[]{:S(2)}) copy-start(bf16[512,1,2048]{2,0,1:T(8,128)(2,1)} %param.10) | copy-start | bytes 6291460
  4.3 19.1 %copy-start.3 = (s32[512,512]{1,0:T(8,128)S(1)}, s32[512,512]{1,0:T(8,128)}, u32[]{:S(2)}) copy-start(s32[512,512]{1,0:T(8,128)} %src) | copy-start | bytes 3145732
  4.3 6.8 %collective-permute-start = (bf16[128,512]{1,0:T(8,128)(2,1)}, bf16[128,512]{1,0:T(8,128)(2,1)S(1)}, u32[]{:S(2)}, u32[]{:S(2)}) collective-permute-start(bf16[128,512]{1,0:T(8,128)(2,1)} %get-tuple-element.36), channel_id=1, source_target_pairs={{0,64},{1,65},{2,66},{3,67},{4,68},{5,69},{6,70},{7,71},{8,72},{9,... | collective-permute-start | bytes 393224 | tf_op jit(solution)/shard_map/ppermute | solution.py:48
  5.9 9.2 %collective-permute-start.1 = (bf16[128,512]{1,0:T(8,128)(2,1)}, bf16[128,512]{1,0:T(8,128)(2,1)}, u32[]{:S(2)}, u32[]{:S(2)}) collective-permute-start(bf16[128,512]{1,0:T(8,128)(2,1)} %get-tuple-element.37), channel_id=1, source_target_pairs={{0,128},{1,129},{2,130},{3,131},{4,132},{5,133},{6,134},{7,135},{8... | collective-permute-start | bytes 393224 | tf_op jit(solution)/shard_map/ppermute | solution.py:48
  8.8 6.3 %collective-permute-start.2 = (bf16[128,512]{1,0:T(8,128)(2,1)}, bf16[128,512]{1,0:T(8,128)(2,1)}, u32[]{:S(2)}, u32[]{:S(2)}) collective-permute-start(bf16[128,512]{1,0:T(8,128)(2,1)} %get-tuple-element.38), channel_id=1, source_target_pairs={{0,192},{1,193},{2,194},{3,195},{4,196},{5,197},{6,198},{7,199},{8... | collective-permute-start | bytes 393224 | tf_op jit(solution)/shard_map/ppermute | solution.py:48
  16.2 14.0 %copy-start.7 = (f32[512]{0:T(512)S(1)}, f32[512]{0:T(512)}, u32[]{:S(2)}) copy-start(f32[512]{0:T(512)} %param.9) | copy-start | bytes 6148
  16.8 24.7 %collective-permute-start.11 = (bf16[512,1024]{1,0:T(8,128)(2,1)S(1)}, bf16[512,1024]{1,0:T(8,128)(2,1)S(1)}, u32[]{:S(2)}, u32[]{:S(2)}) collective-permute-start(bf16[512,1024]{1,0:T(8,128)(2,1)S(1)} %shard_map.81), channel_id=1, source_target_pairs={{0,1},{1,0},{2,3},{3,2},{4,5},{5,4},{6,7},{7,6},{8,9},{9,8},{10,11... | collective-permute-start | bytes 3145736 | tf_op jit(solution)/shard_map/ppermute | solution.py:48
  16.9 13.3 %collective-permute-start.3 = (bf16[128,512]{1,0:T(8,128)(2,1)S(1)}, bf16[128,512]{1,0:T(8,128)(2,1)S(1)}, u32[]{:S(2)}, u32[]{:S(2)}) collective-permute-start(bf16[128,512]{1,0:T(8,128)(2,1)S(1)} %get-tuple-element.40), channel_id=1, source_target_pairs={{0,32},{1,33},{2,34},{3,35},{4,36},{5,37},{6,38},{7,39},{8,40},{9,... | collective-permute-start | bytes 393224 | tf_op jit(solution)/shard_map/ppermute | solution.py:48
  30.3 7.3 %collective-permute-start.9 = (bf16[128,512]{1,0:T(8,128)(2,1)S(1)}, bf16[128,512]{1,0:T(8,128)(2,1)S(1)}, u32[]{:S(2)}, u32[]{:S(2)}) collective-permute-start(bf16[128,512]{1,0:T(8,128)(2,1)S(1)} %shard_map.80.refs_0_.a), channel_id=1, source_target_pairs={{0,64},{1,65},{2,66},{3,67},{4,68},{5,69},{6,70},{7,71},{8,72},{9,... | collective-permute-start | bytes 393224 | tf_op jit(solution)/shard_map/ppermute | solution.py:48
  31.6 8.4 %collective-permute-start.7 = (bf16[128,512]{1,0:T(8,128)(2,1)S(1)}, bf16[128,512]{1,0:T(8,128)(2,1)S(1)}, u32[]{:S(2)}, u32[]{:S(2)}) collective-permute-start(bf16[128,512]{1,0:T(8,128)(2,1)S(1)} %shard_map.80.refs_0_.a), channel_id=1, source_target_pairs={{0,128},{1,129},{2,130},{3,131},{4,132},{5,133},{6,134},{7,135},{8... | collective-permute-start | bytes 393224 | tf_op jit(solution)/shard_map/ppermute | solution.py:48
  34.0 6.2 %collective-permute-start.5 = (bf16[128,512]{1,0:T(8,128)(2,1)S(1)}, bf16[128,512]{1,0:T(8,128)(2,1)S(1)}, u32[]{:S(2)}, u32[]{:S(2)}) collective-permute-start(bf16[128,512]{1,0:T(8,128)(2,1)S(1)} %shard_map.80.refs_0_.a), channel_id=1, source_target_pairs={{0,192},{1,193},{2,194},{3,195},{4,196},{5,197},{6,198},{7,199},{8... | collective-permute-start | bytes 393224 | tf_op jit(solution)/shard_map/ppermute | solution.py:48
  35.6 5.6 %collective-permute-start.4 = (bf16[128,512]{1,0:T(8,128)(2,1)S(1)}, bf16[128,512]{1,0:T(8,128)(2,1)S(1)}, u32[]{:S(2)}, u32[]{:S(2)}) collective-permute-start(bf16[128,512]{1,0:T(8,128)(2,1)S(1)} %shard_map.80.refs_0_.a), channel_id=1, source_target_pairs={{0,1},{1,0},{2,3},{3,2},{4,5},{5,4},{6,7},{7,6},{8,9},{9,8},{10,11... | collective-permute-start | bytes 393224 | tf_op jit(solution)/shard_map/ppermute | solution.py:48
  37.6 3.6 %collective-permute-start.10 = (bf16[128,512]{1,0:T(8,128)(2,1)S(1)}, bf16[128,512]{1,0:T(8,128)(2,1)S(1)}, u32[]{:S(2)}, u32[]{:S(2)}) collective-permute-start(bf16[128,512]{1,0:T(8,128)(2,1)S(1)} %collective-permute-done.9.refs_3_.d), channel_id=1, source_target_pairs={{0,1},{1,0},{2,3},{3,2},{4,5},{5,4},{6,7},{7,6},{8,9},{9,8},{10,11... | collective-permute-start | bytes 393224 | tf_op jit(solution)/shard_map/ppermute | solution.py:48
  40.0 1.3 %collective-permute-start.8 = (bf16[128,512]{1,0:T(8,128)(2,1)S(1)}, bf16[128,512]{1,0:T(8,128)(2,1)S(1)}, u32[]{:S(2)}, u32[]{:S(2)}) collective-permute-start(bf16[128,512]{1,0:T(8,128)(2,1)S(1)} %collective-permute-done.7.refs_2_.c), channel_id=1, source_target_pairs={{0,1},{1,0},{2,3},{3,2},{4,5},{5,4},{6,7},{7,6},{8,9},{9,8},{10,11... | collective-permute-start | bytes 393224 | tf_op jit(solution)/shard_map/ppermute | solution.py:48
  40.2 1.0 copy-start.4
  40.2 1.3 %collective-permute-start.6 = (bf16[128,512]{1,0:T(8,128)(2,1)S(1)}, bf16[128,512]{1,0:T(8,128)(2,1)S(1)}, u32[]{:S(2)}, u32[]{:S(2)}) collective-permute-start(bf16[128,512]{1,0:T(8,128)(2,1)S(1)} %collective-permute-done.5.refs_1_.b), channel_id=1, source_target_pairs={{0,1},{1,0},{2,3},{3,2},{4,5},{5,4},{6,7},{7,6},{8,9},{9,8},{10,11... | collective-permute-start | bytes 393224 | tf_op jit(solution)/shard_map/ppermute | solution.py:48
  42.8 11.3 %collective-permute-start.12 = (bf16[128,1024]{1,0:T(8,128)(2,1)}, bf16[128,1024]{1,0:T(8,128)(2,1)}, u32[]{:S(2)}, u32[]{:S(2)}) collective-permute-start(bf16[128,1024]{1,0:T(8,128)(2,1)} %get-tuple-element.43), channel_id=1, source_target_pairs={{0,2},{1,3},{2,4},{3,5},{4,6},{5,7},{6,0},{7,1},{8,10},{9,11},{10,... | collective-permute-start | bytes 786440 | tf_op jit(solution)/shard_map/ppermute | solution.py:48
  44.3 13.5 %collective-permute-start.14 = (bf16[128,1024]{1,0:T(8,128)(2,1)}, bf16[128,1024]{1,0:T(8,128)(2,1)}, u32[]{:S(2)}, u32[]{:S(2)}) collective-permute-start(bf16[128,1024]{1,0:T(8,128)(2,1)} %get-tuple-element.44), channel_id=1, source_target_pairs={{0,6},{1,7},{2,0},{3,1},{4,2},{5,3},{6,4},{7,5},{8,14},{9,15},{10,... | collective-permute-start | bytes 786440 | tf_op jit(solution)/shard_map/ppermute | solution.py:48
  47.1 12.4 %collective-permute-start.13 = (bf16[128,1024]{1,0:T(8,128)(2,1)}, bf16[128,1024]{1,0:T(8,128)(2,1)}, u32[]{:S(2)}, u32[]{:S(2)}) collective-permute-start(bf16[128,1024]{1,0:T(8,128)(2,1)} %shard_map.86), channel_id=1, source_target_pairs={{0,4},{1,5},{2,6},{3,7},{4,0},{5,1},{6,2},{7,3},{8,12},{9,13},{10,... | collective-permute-start | bytes 786440 | tf_op jit(solution)/shard_map/ppermute | solution.py:48
  49.6 0.9 copy-start.5
  50.8 1.6 %copy-start.1 = (bf16[512,1,2048]{2,0,1:T(8,128)(2,1)S(1)}, bf16[512,1,2048]{2,0,1:T(8,128)(2,1)}, u32[]{:S(2)}) copy-start(bf16[512,1,2048]{2,0,1:T(8,128)(2,1)} %param.6) | copy-start | bytes 6291460
  52.4 12.0 %copy-start.2 = (bf16[512,1,2048]{2,0,1:T(8,128)(2,1)S(1)}, bf16[512,1,2048]{2,0,1:T(8,128)(2,1)}, u32[]{:S(2)}) copy-start(bf16[512,1,2048]{2,0,1:T(8,128)(2,1)} %param.6) | copy-start | bytes 6291460
  52.4 12.0 %copy-start.6 = (f32[1,2048]{1,0:T(1,128)S(1)}, f32[1,2048]{1,0:T(1,128)}, u32[]{:S(2)}) copy-start(f32[1,2048]{1,0:T(1,128)} %bias.1) | copy-start | bytes 24580
  60.8 4.4 %collective-permute-start.15 = (bf16[128,256]{1,0:T(8,128)(2,1)S(1)}, bf16[128,256]{1,0:T(8,128)(2,1)S(1)}, u32[]{:S(2)}, u32[]{:S(2)}) collective-permute-start(bf16[128,256]{1,0:T(8,128)(2,1)S(1)} %get-tuple-element.51), channel_id=1, source_target_pairs={{0,8},{1,9},{2,10},{3,11},{4,12},{5,13},{6,14},{7,15},{8,0},{9,1},... | collective-permute-start | bytes 196616 | tf_op jit(solution)/shard_map/ppermute | solution.py:48
  60.9 6.7 %collective-permute-start.16 = (bf16[128,256]{1,0:T(8,128)(2,1)S(1)}, bf16[128,256]{1,0:T(8,128)(2,1)S(1)}, u32[]{:S(2)}, u32[]{:S(2)}) collective-permute-start(bf16[128,256]{1,0:T(8,128)(2,1)S(1)} %get-tuple-element.52), channel_id=1, source_target_pairs={{0,16},{1,17},{2,18},{3,19},{4,20},{5,21},{6,22},{7,23},{8,24},{9,... | collective-permute-start | bytes 196616 | tf_op jit(solution)/shard_map/ppermute | solution.py:48
  63.4 6.4 %collective-permute-start.17 = (bf16[128,256]{1,0:T(8,128)(2,1)S(1)}, bf16[128,256]{1,0:T(8,128)(2,1)S(1)}, u32[]{:S(2)}, u32[]{:S(2)}) collective-permute-start(bf16[128,256]{1,0:T(8,128)(2,1)S(1)} %get-tuple-element.53), channel_id=1, source_target_pairs={{0,24},{1,25},{2,26},{3,27},{4,28},{5,29},{6,30},{7,31},{8,16},{9,... | collective-permute-start | bytes 196616 | tf_op jit(solution)/shard_map/ppermute | solution.py:48
  69.8 6.5 %collective-permute-start.20 = (bf16[128,256]{1,0:T(8,128)(2,1)S(1)}, bf16[128,256]{1,0:T(8,128)(2,1)S(1)}, u32[]{:S(2)}, u32[]{:S(2)}) collective-permute-start(bf16[128,256]{1,0:T(8,128)(2,1)S(1)} %shard_map.89.a), channel_id=1, source_target_pairs={{0,24},{1,25},{2,26},{3,27},{4,28},{5,29},{6,30},{7,31},{8,16},{9,... | collective-permute-start | bytes 196616 | tf_op jit(solution)/shard_map/ppermute | solution.py:48
  70.9 5.4 %collective-permute-start.19 = (bf16[128,256]{1,0:T(8,128)(2,1)S(1)}, bf16[128,256]{1,0:T(8,128)(2,1)S(1)}, u32[]{:S(2)}, u32[]{:S(2)}) collective-permute-start(bf16[128,256]{1,0:T(8,128)(2,1)S(1)} %shard_map.89.a), channel_id=1, source_target_pairs={{0,16},{1,17},{2,18},{3,19},{4,20},{5,21},{6,22},{7,23},{8,24},{9,... | collective-permute-start | bytes 196616 | tf_op jit(solution)/shard_map/ppermute | solution.py:48
  73.0 4.3 %collective-permute-start.18 = (bf16[128,256]{1,0:T(8,128)(2,1)S(1)}, bf16[128,256]{1,0:T(8,128)(2,1)S(1)}, u32[]{:S(2)}, u32[]{:S(2)}) collective-permute-start(bf16[128,256]{1,0:T(8,128)(2,1)S(1)} %shard_map.89.a), channel_id=1, source_target_pairs={{0,8},{1,9},{2,10},{3,11},{4,12},{5,13},{6,14},{7,15},{8,0},{9,1},... | collective-permute-start | bytes 196616 | tf_op jit(solution)/shard_map/ppermute | solution.py:48
  77.3 11.9 %collective-permute-start.26 = (bf16[128,1024]{1,0:T(8,128)(2,1)S(1)}, bf16[128,1024]{1,0:T(8,128)(2,1)S(1)}, u32[]{:S(2)}, u32[]{:S(2)}) collective-permute-start(bf16[128,1024]{1,0:T(8,128)(2,1)S(1)} %shard_map.90.refs_0_), channel_id=1, source_target_pairs={{0,2},{1,3},{2,4},{3,5},{4,6},{5,7},{6,0},{7,1},{8,10},{9,11},{10,... | collective-permute-start | bytes 786440 | tf_op jit(solution)/shard_map/ppermute | solution.py:48
  78.2 11.0 %collective-permute-start.24 = (bf16[128,1024]{1,0:T(8,128)(2,1)S(1)}, bf16[128,1024]{1,0:T(8,128)(2,1)S(1)}, u32[]{:S(2)}, u32[]{:S(2)}) collective-permute-start(bf16[128,1024]{1,0:T(8,128)(2,1)S(1)} %shard_map.90.refs_0_), channel_id=1, source_target_pairs={{0,4},{1,5},{2,6},{3,7},{4,0},{5,1},{6,2},{7,3},{8,12},{9,13},{10,... | collective-permute-start | bytes 786440 | tf_op jit(solution)/shard_map/ppermute | solution.py:48
  80.3 9.6 %collective-permute-start.22 = (bf16[128,1024]{1,0:T(8,128)(2,1)S(1)}, bf16[128,1024]{1,0:T(8,128)(2,1)S(1)}, u32[]{:S(2)}, u32[]{:S(2)}) collective-permute-start(bf16[128,1024]{1,0:T(8,128)(2,1)S(1)} %shard_map.90.refs_0_), channel_id=1, source_target_pairs={{0,6},{1,7},{2,0},{3,1},{4,2},{5,3},{6,4},{7,5},{8,14},{9,15},{10,... | collective-permute-start | bytes 786440 | tf_op jit(solution)/shard_map/ppermute | solution.py:48
  81.0 9.6 %collective-permute-start.21 = (bf16[128,1024]{1,0:T(8,128)(2,1)S(1)}, bf16[128,1024]{1,0:T(8,128)(2,1)S(1)}, u32[]{:S(2)}, u32[]{:S(2)}) collective-permute-start(bf16[128,1024]{1,0:T(8,128)(2,1)S(1)} %shard_map.90.refs_0_), channel_id=1, source_target_pairs={{0,1},{1,0},{2,3},{3,2},{4,5},{5,4},{6,7},{7,6},{8,9},{9,8},{10,11... | collective-permute-start | bytes 786440 | tf_op jit(solution)/shard_map/ppermute | solution.py:48
  89.2 1.5 %collective-permute-start.27 = (bf16[128,1024]{1,0:T(8,128)(2,1)S(1)}, bf16[128,1024]{1,0:T(8,128)(2,1)S(1)}, u32[]{:S(2)}, u32[]{:S(2)}) collective-permute-start(bf16[128,1024]{1,0:T(8,128)(2,1)S(1)} %collective-permute-done.26.refs_3_), channel_id=1, source_target_pairs={{0,1},{1,0},{2,3},{3,2},{4,5},{5,4},{6,7},{7,6},{8,9},{9,8},{10,11... | collective-permute-start | bytes 786440 | tf_op jit(solution)/shard_map/ppermute | solution.py:48
  89.2 1.9 %collective-permute-start.25 = (bf16[128,1024]{1,0:T(8,128)(2,1)S(1)}, bf16[128,1024]{1,0:T(8,128)(2,1)S(1)}, u32[]{:S(2)}, u32[]{:S(2)}) collective-permute-start(bf16[128,1024]{1,0:T(8,128)(2,1)S(1)} %collective-permute-done.24.refs_2_), channel_id=1, source_target_pairs={{0,1},{1,0},{2,3},{3,2},{4,5},{5,4},{6,7},{7,6},{8,9},{9,8},{10,11... | collective-permute-start | bytes 786440 | tf_op jit(solution)/shard_map/ppermute | solution.py:48
  89.9 1.6 %collective-permute-start.23 = (bf16[128,1024]{1,0:T(8,128)(2,1)S(1)}, bf16[128,1024]{1,0:T(8,128)(2,1)S(1)}, u32[]{:S(2)}, u32[]{:S(2)}) collective-permute-start(bf16[128,1024]{1,0:T(8,128)(2,1)S(1)} %collective-permute-done.22.refs_1_), channel_id=1, source_target_pairs={{0,1},{1,0},{2,3},{3,2},{4,5},{5,4},{6,7},{7,6},{8,9},{9,8},{10,11... | collective-permute-start | bytes 786440 | tf_op jit(solution)/shard_map/ppermute | solution.py:48
  92.3 7.2 %collective-permute-start.28 = (bf16[128,512]{1,0:T(8,128)(2,1)S(1)}, bf16[128,512]{1,0:T(8,128)(2,1)S(1)}, u32[]{:S(2)}, u32[]{:S(2)}) collective-permute-start(bf16[128,512]{1,0:T(8,128)(2,1)S(1)} %get-tuple-element.57), channel_id=1, source_target_pairs={{0,64},{1,65},{2,66},{3,67},{4,68},{5,69},{6,70},{7,71},{8,72},{9,... | collective-permute-start | bytes 393224 | tf_op jit(solution)/shard_map/ppermute | solution.py:48
  93.6 8.7 %collective-permute-start.29 = (bf16[128,512]{1,0:T(8,128)(2,1)S(1)}, bf16[128,512]{1,0:T(8,128)(2,1)S(1)}, u32[]{:S(2)}, u32[]{:S(2)}) collective-permute-start(bf16[128,512]{1,0:T(8,128)(2,1)S(1)} %get-tuple-element.58), channel_id=1, source_target_pairs={{0,128},{1,129},{2,130},{3,131},{4,132},{5,133},{6,134},{7,135},{8... | collective-permute-start | bytes 393224 | tf_op jit(solution)/shard_map/ppermute | solution.py:48
  96.0 6.5 %collective-permute-start.30 = (bf16[128,512]{1,0:T(8,128)(2,1)S(1)}, bf16[128,512]{1,0:T(8,128)(2,1)S(1)}, u32[]{:S(2)}, u32[]{:S(2)}) collective-permute-start(bf16[128,512]{1,0:T(8,128)(2,1)S(1)} %get-tuple-element.59), channel_id=1, source_target_pairs={{0,192},{1,193},{2,194},{3,195},{4,196},{5,197},{6,198},{7,199},{8... | collective-permute-start | bytes 393224 | tf_op jit(solution)/shard_map/ppermute | solution.py:48
  102.5 11.5 %collective-permute-start.31 = (bf16[128,512]{1,0:T(8,128)(2,1)S(1)}, bf16[128,512]{1,0:T(8,128)(2,1)S(1)}, u32[]{:S(2)}, u32[]{:S(2)}) collective-permute-start(bf16[128,512]{1,0:T(8,128)(2,1)S(1)} %get-tuple-element.66), channel_id=1, source_target_pairs={{0,32},{1,33},{2,34},{3,35},{4,36},{5,37},{6,38},{7,39},{8,40},{9,... | collective-permute-start | bytes 393224 | tf_op jit(solution)/shard_map/ppermute | solution.py:48
  114.1 7.7 %collective-permute-start.34 = (bf16[128,512]{1,0:T(8,128)(2,1)S(1)}, bf16[128,512]{1,0:T(8,128)(2,1)S(1)}, u32[]{:S(2)}, u32[]{:S(2)}) collective-permute-start(bf16[128,512]{1,0:T(8,128)(2,1)S(1)} %shard_map.95.a), channel_id=1, source_target_pairs={{0,64},{1,65},{2,66},{3,67},{4,68},{5,69},{6,70},{7,71},{8,72},{9,... | collective-permute-start | bytes 393224 | tf_op jit(solution)/shard_map/ppermute | solution.py:48
  116.4 6.1 %collective-permute-start.33 = (bf16[128,512]{1,0:T(8,128)(2,1)S(1)}, bf16[128,512]{1,0:T(8,128)(2,1)S(1)}, u32[]{:S(2)}, u32[]{:S(2)}) collective-permute-start(bf16[128,512]{1,0:T(8,128)(2,1)S(1)} %shard_map.95.a), channel_id=1, source_target_pairs={{0,192},{1,193},{2,194},{3,195},{4,196},{5,197},{6,198},{7,199},{8... | collective-permute-start | bytes 393224 | tf_op jit(solution)/shard_map/ppermute | solution.py:48
  117.5 6.5 %collective-permute-start.32 = (bf16[128,512]{1,0:T(8,128)(2,1)S(1)}, bf16[128,512]{1,0:T(8,128)(2,1)S(1)}, u32[]{:S(2)}, u32[]{:S(2)}) collective-permute-start(bf16[128,512]{1,0:T(8,128)(2,1)S(1)} %shard_map.95.a), channel_id=1, source_target_pairs={{0,128},{1,129},{2,130},{3,131},{4,132},{5,133},{6,134},{7,135},{8... | collective-permute-start | bytes 393224 | tf_op jit(solution)/shard_map/ppermute | solution.py:48

commit v4 on v3

--- a/solution.py
+++ b/solution.py
@@ -50,7 +50,7 @@
 
 FAR_FIRST = (2, 1, 3)
 PARTS = 4
-LINE = (3, 2, 1)
+LINE = (1, 2, 3)
 
 
 def gather(v, axis, ks):

time: 127 us -> 127 us (level)
  no operation moved by 1% of the time
where the time goes in v4:
time: 127 us; the launch traced here: 126 us
  waiting for transfers between devices  52.1 us (41%)
  starting transfers between devices  49.4 us (39%)
  Pallas kernels  20.9 us (16%)
  local copies, waits for them, and re-layouts  2.76 us (2%)
    ppermute x35, waiting for transfers between devices, exchange(): return lax.ppermute(v, ('layer', 'latent'), perm)  52.1 us
    ppermute x35, starting transfers between devices, exchange(): return lax.ppermute(v, ('layer', 'latent'), perm)  49.4 us
    pallas_call x14, Pallas kernels, local(): pl.pallas_call(kernel, out_shape=outs, in_specs=in_specs, out_specs=[pl.B...  8.07 us
    pallas_call x4, Pallas kernels, placed(): pl.pallas_call(kernel, out_shape=[sds(o[0], o[1]) for o in outs], grid_sp...  3.69 us
    pallas_call x1, Pallas kernels, body(): pl.pallas_call(pre_kernel, out_shape=[tile] * 3 + [held((ny, latents), f3...  3.62 us
    pallas_call x1, Pallas kernels, body(): pl.pallas_call(cross_kernel, out_shape=sds((latents, width), bf16), grid=...  2.99 us
  transfers between devices with their start and end apart: 35, of which 25 were waited for; matrix products, arithmetic and copies ran while one was open for 1% of the time, Pallas kernels for 8%

profile of v4, /device:TPU:32, one launch (start us, length us, event | category | flops | bytes accessed | tf_op | source)
XLA Modules:
  0.0 126.4 jit_solution(3405725899318345507)
XLA Ops:
  0.6 3.6 %shard_map.77 = (bf16[128,512]{1,0:T(8,128)(2,1)}, bf16[128,512]{1,0:T(8,128)(2,1)}, bf16[128,512]{1,0:T(8,128)(2,1)}, f32[128,512]{1,0:T(8,128)S(1)}) custom-call(bf16[512,2048]{1,0:T(8,128)(2,1)} %bitcast.28, bf16[2048,512]{1,0:T(8,128)(2,1)} %bitcast.38), custom_call_target="tpu_custom_call" | custom-call | flops 1073741824 | bytes 6291456 | tf_op jit(solution)/shard_map/pallas_call | solution.py:291
  4.3 1.7 %collective-permute-start = (bf16[128,512]{1,0:T(8,128)(2,1)}, bf16[128,512]{1,0:T(8,128)(2,1)S(1)}, u32[]{:S(2)}, u32[]{:S(2)}) collective-permute-start(bf16[128,512]{1,0:T(8,128)(2,1)} %get-tuple-element.36), channel_id=1, source_target_pairs={{0,64},{1,65},{2,66},{3,67},{4,68},{5,69},{6,70},{7,71},{8,72},{9,... | collective-permute-start | bytes 393224 | tf_op jit(solution)/shard_map/ppermute | solution.py:48
  5.9 2.9 %collective-permute-start.1 = (bf16[128,512]{1,0:T(8,128)(2,1)}, bf16[128,512]{1,0:T(8,128)(2,1)}, u32[]{:S(2)}, u32[]{:S(2)}) collective-permute-start(bf16[128,512]{1,0:T(8,128)(2,1)} %get-tuple-element.37), channel_id=1, source_target_pairs={{0,128},{1,129},{2,130},{3,131},{4,132},{5,133},{6,134},{7,135},{8... | collective-permute-start | bytes 393224 | tf_op jit(solution)/shard_map/ppermute | solution.py:48
  8.8 1.3 %collective-permute-start.2 = (bf16[128,512]{1,0:T(8,128)(2,1)}, bf16[128,512]{1,0:T(8,128)(2,1)}, u32[]{:S(2)}, u32[]{:S(2)}) collective-permute-start(bf16[128,512]{1,0:T(8,128)(2,1)} %get-tuple-element.38), channel_id=1, source_target_pairs={{0,192},{1,193},{2,194},{3,195},{4,196},{5,197},{6,198},{7,199},{8... | collective-permute-start | bytes 393224 | tf_op jit(solution)/shard_map/ppermute | solution.py:48
  11.1 4.1 %collective-permute-done.1.b = bf16[128,512]{1,0:T(8,128)(2,1)} collective-permute-done((bf16[128,512]{1,0:T(8,128)(2,1)}, bf16[128,512]{1,0:T(8,128)(2,1)}, u32[]{:S(2)}, u32[]{:S(2)}) %collective-permute-start.1) | collective-permute-done | bytes 131104 | tf_op jit(solution)/shard_map/ppermute | solution.py:48
  15.2 1.0 shard_map.78
  16.9 6.4 %collective-permute-start.3 = (bf16[128,512]{1,0:T(8,128)(2,1)S(1)}, bf16[128,512]{1,0:T(8,128)(2,1)S(1)}, u32[]{:S(2)}, u32[]{:S(2)}) collective-permute-start(bf16[128,512]{1,0:T(8,128)(2,1)S(1)} %get-tuple-element.40), channel_id=1, source_target_pairs={{0,32},{1,33},{2,34},{3,35},{4,36},{5,37},{6,38},{7,39},{8,40},{9,... | collective-permute-start | bytes 393224 | tf_op jit(solution)/shard_map/ppermute | solution.py:48
  24.0 6.3 %collective-permute-done.3.got = bf16[128,512]{1,0:T(8,128)(2,1)S(1)} collective-permute-done((bf16[128,512]{1,0:T(8,128)(2,1)S(1)}, bf16[128,512]{1,0:T(8,128)(2,1)S(1)}, u32[]{:S(2)}, u32[]{:S(2)}) %collective-permute-start.3) | collective-permute-done | bytes 131104 | tf_op jit(solution)/shard_map/ppermute | solution.py:48
  30.3 1.3 %collective-permute-start.9 = (bf16[128,512]{1,0:T(8,128)(2,1)S(1)}, bf16[128,512]{1,0:T(8,128)(2,1)S(1)}, u32[]{:S(2)}, u32[]{:S(2)}) collective-permute-start(bf16[128,512]{1,0:T(8,128)(2,1)S(1)} %shard_map.80.refs_0_.a), channel_id=1, source_target_pairs={{0,64},{1,65},{2,66},{3,67},{4,68},{5,69},{6,70},{7,71},{8,72},{9,... | collective-permute-start | bytes 393224 | tf_op jit(solution)/shard_map/ppermute | solution.py:48
  31.6 2.4 %collective-permute-start.7 = (bf16[128,512]{1,0:T(8,128)(2,1)S(1)}, bf16[128,512]{1,0:T(8,128)(2,1)S(1)}, u32[]{:S(2)}, u32[]{:S(2)}) collective-permute-start(bf16[128,512]{1,0:T(8,128)(2,1)S(1)} %shard_map.80.refs_0_.a), channel_id=1, source_target_pairs={{0,128},{1,129},{2,130},{3,131},{4,132},{5,133},{6,134},{7,135},{8... | collective-permute-start | bytes 393224 | tf_op jit(solution)/shard_map/ppermute | solution.py:48
  34.0 1.6 %collective-permute-start.5 = (bf16[128,512]{1,0:T(8,128)(2,1)S(1)}, bf16[128,512]{1,0:T(8,128)(2,1)S(1)}, u32[]{:S(2)}, u32[]{:S(2)}) collective-permute-start(bf16[128,512]{1,0:T(8,128)(2,1)S(1)} %shard_map.80.refs_0_.a), channel_id=1, source_target_pairs={{0,192},{1,193},{2,194},{3,195},{4,196},{5,197},{6,198},{7,199},{8... | collective-permute-start | bytes 393224 | tf_op jit(solution)/shard_map/ppermute | solution.py:48
  35.6 2.0 %collective-permute-done.9.refs_3_.d = bf16[128,512]{1,0:T(8,128)(2,1)S(1)} collective-permute-done((bf16[128,512]{1,0:T(8,128)(2,1)S(1)}, bf16[128,512]{1,0:T(8,128)(2,1)S(1)}, u32[]{:S(2)}, u32[]{:S(2)}) %collective-permute-start.9) | collective-permute-done | bytes 131104 | tf_op jit(solution)/shard_map/ppermute | solution.py:48
  37.6 2.4 %collective-permute-done.7.refs_2_.c = bf16[128,512]{1,0:T(8,128)(2,1)S(1)} collective-permute-done((bf16[128,512]{1,0:T(8,128)(2,1)S(1)}, bf16[128,512]{1,0:T(8,128)(2,1)S(1)}, u32[]{:S(2)}, u32[]{:S(2)}) %collective-permute-start.7) | collective-permute-done | bytes 131104 | tf_op jit(solution)/shard_map/ppermute | solution.py:48
  41.5 1.3 %shard_map.83 = (bf16[128,1024]{1,0:T(8,128)(2,1)}, bf16[128,1024]{1,0:T(8,128)(2,1)}, f32[128,1024]{1,0:T(8,128)S(1)}) custom-call(bf16[128,512]{1,0:T(8,128)(2,1)S(1)} %collective-permute-done.4.refs_0_, bf16[128,512]{1,0:T(8,128)(2,1)S(1)} %collective-permute-done.6.refs_1_, bf16[128,512]{1,0:T(8,128)(2,1)S(1)} %collective-permute-done.8.refs_2_, ...), custom_call_target="tpu_custom_call" | custom-call | flops 402653184 | bytes 5242880 | tf_op jit(solution)/shard_map/pallas_call | solution.py:78
  42.8 1.5 %collective-permute-start.12 = (bf16[128,1024]{1,0:T(8,128)(2,1)}, bf16[128,1024]{1,0:T(8,128)(2,1)}, u32[]{:S(2)}, u32[]{:S(2)}) collective-permute-start(bf16[128,1024]{1,0:T(8,128)(2,1)} %get-tuple-element.43), channel_id=1, source_target_pairs={{0,2},{1,3},{2,4},{3,5},{4,6},{5,7},{6,0},{7,1},{8,10},{9,11},{10,... | collective-permute-start | bytes 786440 | tf_op jit(solution)/shard_map/ppermute | solution.py:48
  44.3 1.7 %collective-permute-start.14 = (bf16[128,1024]{1,0:T(8,128)(2,1)}, bf16[128,1024]{1,0:T(8,128)(2,1)}, u32[]{:S(2)}, u32[]{:S(2)}) collective-permute-start(bf16[128,1024]{1,0:T(8,128)(2,1)} %get-tuple-element.44), channel_id=1, source_target_pairs={{0,6},{1,7},{2,0},{3,1},{4,2},{5,3},{6,4},{7,5},{8,14},{9,15},{10,... | collective-permute-start | bytes 786440 | tf_op jit(solution)/shard_map/ppermute | solution.py:48
  46.1 1.0 shard_map.86
  47.1 1.8 %collective-permute-start.13 = (bf16[128,1024]{1,0:T(8,128)(2,1)}, bf16[128,1024]{1,0:T(8,128)(2,1)}, u32[]{:S(2)}, u32[]{:S(2)}) collective-permute-start(bf16[128,1024]{1,0:T(8,128)(2,1)} %shard_map.86), channel_id=1, source_target_pairs={{0,4},{1,5},{2,6},{3,7},{4,0},{5,1},{6,2},{7,3},{8,12},{9,13},{10,... | collective-permute-start | bytes 786440 | tf_op jit(solution)/shard_map/ppermute | solution.py:48
  49.6 0.9 copy-done.5
  50.8 1.6 %copy-done.1 = bf16[512,1,2048]{2,0,1:T(8,128)(2,1)S(1)} copy-done((bf16[512,1,2048]{2,0,1:T(8,128)(2,1)S(1)}, bf16[512,1,2048]{2,0,1:T(8,128)(2,1)}, u32[]{:S(2)}) %copy-start.1) | copy-done | bytes 2097176
  52.4 1.7 %shard_map.84.acts = bf16[2048,512]{1,0:T(8,128)(2,1)S(1)} custom-call(s32[14]{0:T(128)S(1)} %stack.59.idx, bf16[512,2048]{1,0:T(8,128)(2,1)S(1)} %bitcast.29, bf16[512,2048]{1,0:T(8,128)(2,1)S(1)} %bitcast.30, bf16[512,2048]{1,0:T(8,128)(2,1)S(1)} %bitcast.31, bf16[512,2048]{1,0:T(8,128)(2,1)S(1)} %bitcast.32), custom_call_target="tpu_custom_call" | custom-call | bytes 4194304 | tf_op jit(solution)/shard_map/pallas_call | solution.py:258
  54.1 3.7 %collective-permute-done.14.c = bf16[128,1024]{1,0:T(8,128)(2,1)} collective-permute-done((bf16[128,1024]{1,0:T(8,128)(2,1)}, bf16[128,1024]{1,0:T(8,128)(2,1)}, u32[]{:S(2)}, u32[]{:S(2)}) %collective-permute-start.14) | collective-permute-done | bytes 262176 | tf_op jit(solution)/shard_map/ppermute | solution.py:48
  57.8 1.7 %collective-permute-done.13.b = bf16[128,1024]{1,0:T(8,128)(2,1)} collective-permute-done((bf16[128,1024]{1,0:T(8,128)(2,1)}, bf16[128,1024]{1,0:T(8,128)(2,1)}, u32[]{:S(2)}, u32[]{:S(2)}) %collective-permute-start.13) | collective-permute-done | bytes 262176 | tf_op jit(solution)/shard_map/ppermute | solution.py:48
  59.5 1.3 shard_map.87
  60.9 2.5 %collective-permute-start.16 = (bf16[128,256]{1,0:T(8,128)(2,1)S(1)}, bf16[128,256]{1,0:T(8,128)(2,1)S(1)}, u32[]{:S(2)}, u32[]{:S(2)}) collective-permute-start(bf16[128,256]{1,0:T(8,128)(2,1)S(1)} %get-tuple-element.52), channel_id=1, source_target_pairs={{0,16},{1,17},{2,18},{3,19},{4,20},{5,21},{6,22},{7,23},{8,24},{9,... | collective-permute-start | bytes 196616 | tf_op jit(solution)/shard_map/ppermute | solution.py:48
  63.4 0.9 collective-permute-start.17
  65.1 2.5 %collective-permute-done.16.b = bf16[128,256]{1,0:T(8,128)(2,1)S(1)} collective-permute-done((bf16[128,256]{1,0:T(8,128)(2,1)S(1)}, bf16[128,256]{1,0:T(8,128)(2,1)S(1)}, u32[]{:S(2)}, u32[]{:S(2)}) %collective-permute-start.16) | collective-permute-done | bytes 65568 | tf_op jit(solution)/shard_map/ppermute | solution.py:48
  67.6 2.2 %collective-permute-done.17.c = bf16[128,256]{1,0:T(8,128)(2,1)S(1)} collective-permute-done((bf16[128,256]{1,0:T(8,128)(2,1)S(1)}, bf16[128,256]{1,0:T(8,128)(2,1)S(1)}, u32[]{:S(2)}, u32[]{:S(2)}) %collective-permute-start.17) | collective-permute-done | bytes 65568 | tf_op jit(solution)/shard_map/ppermute | solution.py:48
  69.8 1.1 collective-permute-start.20
  70.9 2.1 %collective-permute-start.19 = (bf16[128,256]{1,0:T(8,128)(2,1)S(1)}, bf16[128,256]{1,0:T(8,128)(2,1)S(1)}, u32[]{:S(2)}, u32[]{:S(2)}) collective-permute-start(bf16[128,256]{1,0:T(8,128)(2,1)S(1)} %shard_map.89.a), channel_id=1, source_target_pairs={{0,16},{1,17},{2,18},{3,19},{4,20},{5,21},{6,22},{7,23},{8,24},{9,... | collective-permute-start | bytes 196616 | tf_op jit(solution)/shard_map/ppermute | solution.py:48
  73.4 2.9 %collective-permute-done.20.d = bf16[128,256]{1,0:T(8,128)(2,1)S(1)} collective-permute-done((bf16[128,256]{1,0:T(8,128)(2,1)S(1)}, bf16[128,256]{1,0:T(8,128)(2,1)S(1)}, u32[]{:S(2)}, u32[]{:S(2)}) %collective-permute-start.20) | collective-permute-done | bytes 65568 | tf_op jit(solution)/shard_map/ppermute | solution.py:48
  76.3 1.0 collective-permute-done.18.b
  78.2 2.1 %collective-permute-start.24 = (bf16[128,1024]{1,0:T(8,128)(2,1)S(1)}, bf16[128,1024]{1,0:T(8,128)(2,1)S(1)}, u32[]{:S(2)}, u32[]{:S(2)}) collective-permute-start(bf16[128,1024]{1,0:T(8,128)(2,1)S(1)} %shard_map.90.refs_0_), channel_id=1, source_target_pairs={{0,4},{1,5},{2,6},{3,7},{4,0},{5,1},{6,2},{7,3},{8,12},{9,13},{10,... | collective-permute-start | bytes 786440 | tf_op jit(solution)/shard_map/ppermute | solution.py:48
  81.0 8.2 %collective-permute-done.26.refs_3_ = bf16[128,1024]{1,0:T(8,128)(2,1)S(1)} collective-permute-done((bf16[128,1024]{1,0:T(8,128)(2,1)S(1)}, bf16[128,1024]{1,0:T(8,128)(2,1)S(1)}, u32[]{:S(2)}, u32[]{:S(2)}) %collective-permute-start.26) | collective-permute-done | bytes 262176 | tf_op jit(solution)/shard_map/ppermute | solution.py:48
  92.3 1.3 %collective-permute-start.28 = (bf16[128,512]{1,0:T(8,128)(2,1)S(1)}, bf16[128,512]{1,0:T(8,128)(2,1)S(1)}, u32[]{:S(2)}, u32[]{:S(2)}) collective-permute-start(bf16[128,512]{1,0:T(8,128)(2,1)S(1)} %get-tuple-element.57), channel_id=1, source_target_pairs={{0,64},{1,65},{2,66},{3,67},{4,68},{5,69},{6,70},{7,71},{8,72},{9,... | collective-permute-start | bytes 393224 | tf_op jit(solution)/shard_map/ppermute | solution.py:48
  93.6 2.4 %collective-permute-start.29 = (bf16[128,512]{1,0:T(8,128)(2,1)S(1)}, bf16[128,512]{1,0:T(8,128)(2,1)S(1)}, u32[]{:S(2)}, u32[]{:S(2)}) collective-permute-start(bf16[128,512]{1,0:T(8,128)(2,1)S(1)} %get-tuple-element.58), channel_id=1, source_target_pairs={{0,128},{1,129},{2,130},{3,131},{4,132},{5,133},{6,134},{7,135},{8... | collective-permute-start | bytes 393224 | tf_op jit(solution)/shard_map/ppermute | solution.py:48
  96.0 1.1 collective-permute-start.30
  97.1 2.4 %collective-permute-done.28.a = bf16[128,512]{1,0:T(8,128)(2,1)S(1)} collective-permute-done((bf16[128,512]{1,0:T(8,128)(2,1)S(1)}, bf16[128,512]{1,0:T(8,128)(2,1)S(1)}, u32[]{:S(2)}, u32[]{:S(2)}) %collective-permute-start.28) | collective-permute-done | bytes 131104 | tf_op jit(solution)/shard_map/ppermute | solution.py:48
  99.5 2.8 %collective-permute-done.29.b = bf16[128,512]{1,0:T(8,128)(2,1)S(1)} collective-permute-done((bf16[128,512]{1,0:T(8,128)(2,1)S(1)}, bf16[128,512]{1,0:T(8,128)(2,1)S(1)}, u32[]{:S(2)}, u32[]{:S(2)}) %collective-permute-start.29) | collective-permute-done | bytes 131104 | tf_op jit(solution)/shard_map/ppermute | solution.py:48
  102.5 5.5 %collective-permute-start.31 = (bf16[128,512]{1,0:T(8,128)(2,1)S(1)}, bf16[128,512]{1,0:T(8,128)(2,1)S(1)}, u32[]{:S(2)}, u32[]{:S(2)}) collective-permute-start(bf16[128,512]{1,0:T(8,128)(2,1)S(1)} %get-tuple-element.66), channel_id=1, source_target_pairs={{0,32},{1,33},{2,34},{3,35},{4,36},{5,37},{6,38},{7,39},{8,40},{9,... | collective-permute-start | bytes 393224 | tf_op jit(solution)/shard_map/ppermute | solution.py:48
  108.0 3.0 %shard_map.94 = bf16[512,2048]{1,0:T(8,128)(2,1)} custom-call(bf16[512,512]{1,0:T(8,128)(2,1)S(1)} %get-tuple-element.61.codes, bf16[512,1024]{1,0:T(8,128)(2,1)S(1)} %get-tuple-element.62.own, bf16[512,1024]{1,0:T(8,128)(2,1)S(1)} %get-tuple-element.63.other, bf16[512,2048]{1,0:T(8,128)(2,1)S(1)} %bitcast.27, f32[512,1]{1,0:T(8,128)S(1)} %get-tuple-element.64.factor), custom_call_target="tpu_custom_call" | custom-call | flops 1073741824 | bytes 8388608 | tf_op jit(solution)/shard_map/pallas_call | solution.py:386
  111.0 3.1 %collective-permute-done.31.got = bf16[128,512]{1,0:T(8,128)(2,1)S(1)} collective-permute-done((bf16[128,512]{1,0:T(8,128)(2,1)S(1)}, bf16[128,512]{1,0:T(8,128)(2,1)S(1)}, u32[]{:S(2)}, u32[]{:S(2)}) %collective-permute-start.31) | collective-permute-done | bytes 131104 | tf_op jit(solution)/shard_map/ppermute | solution.py:48
  114.1 2.3 %collective-permute-start.34 = (bf16[128,512]{1,0:T(8,128)(2,1)S(1)}, bf16[128,512]{1,0:T(8,128)(2,1)S(1)}, u32[]{:S(2)}, u32[]{:S(2)}) collective-permute-start(bf16[128,512]{1,0:T(8,128)(2,1)S(1)} %shard_map.95.a), channel_id=1, source_target_pairs={{0,64},{1,65},{2,66},{3,67},{4,68},{5,69},{6,70},{7,71},{8,72},{9,... | collective-permute-start | bytes 393224 | tf_op jit(solution)/shard_map/ppermute | solution.py:48
  116.4 1.1 collective-permute-start.33
  117.5 1.4 %collective-permute-start.32 = (bf16[128,512]{1,0:T(8,128)(2,1)S(1)}, bf16[128,512]{1,0:T(8,128)(2,1)S(1)}, u32[]{:S(2)}, u32[]{:S(2)}) collective-permute-start(bf16[128,512]{1,0:T(8,128)(2,1)S(1)} %shard_map.95.a), channel_id=1, source_target_pairs={{0,128},{1,129},{2,130},{3,131},{4,132},{5,133},{6,134},{7,135},{8... | collective-permute-start | bytes 393224 | tf_op jit(solution)/shard_map/ppermute | solution.py:48
  118.8 2.9 %collective-permute-done.34.b = bf16[128,512]{1,0:T(8,128)(2,1)S(1)} collective-permute-done((bf16[128,512]{1,0:T(8,128)(2,1)S(1)}, bf16[128,512]{1,0:T(8,128)(2,1)S(1)}, u32[]{:S(2)}, u32[]{:S(2)}) %collective-permute-start.34) | collective-permute-done | bytes 131104 | tf_op jit(solution)/shard_map/ppermute | solution.py:48
  122.5 1.4 %collective-permute-done.32.a = bf16[128,512]{1,0:T(8,128)(2,1)S(1)} collective-permute-done((bf16[128,512]{1,0:T(8,128)(2,1)S(1)}, bf16[128,512]{1,0:T(8,128)(2,1)S(1)}, u32[]{:S(2)}, u32[]{:S(2)}) %collective-permute-start.32) | collective-permute-done | bytes 131104 | tf_op jit(solution)/shard_map/ppermute | solution.py:48
  123.9 2.5 %shard_map.97 = bf16[2048,512]{1,0:T(8,128)(2,1)} custom-call(bf16[2048,512]{1,0:T(8,128)(2,1)S(1)} %shard_map.84.acts, bf16[128,512]{1,0:T(8,128)(2,1)S(1)} %collective-permute-done.32.a, bf16[128,512]{1,0:T(8,128)(2,1)S(1)} %collective-permute-done.33.b, f32[2048,512]{1,0:T(8,128)S(1)} %shard_map.96.total), custom_call_target="tpu_custom_call" | custom-call | flops 536870912 | bytes 5242880 | tf_op jit(solution)/shard_map/pallas_call | solution.py:407
  (63 shorter events, 11.7 us)
Async XLA Ops:
  0.6 15.6 %copy-start = (bf16[512,1,2048]{2,0,1:T(8,128)(2,1)S(1)}, bf16[512,1,2048]{2,0,1:T(8,128)(2,1)}, u32[]{:S(2)}) copy-start(bf16[512,1,2048]{2,0,1:T(8,128)(2,1)} %param.10) | copy-start | bytes 6291460
  4.3 19.1 %copy-start.3 = (s32[512,512]{1,0:T(8,128)S(1)}, s32[512,512]{1,0:T(8,128)}, u32[]{:S(2)}) copy-start(s32[512,512]{1,0:T(8,128)} %src) | copy-start | bytes 3145732
  4.3 6.8 %collective-permute-start = (bf16[128,512]{1,0:T(8,128)(2,1)}, bf16[128,512]{1,0:T(8,128)(2,1)S(1)}, u32[]{:S(2)}, u32[]{:S(2)}) collective-permute-start(bf16[128,512]{1,0:T(8,128)(2,1)} %get-tuple-element.36), channel_id=1, source_target_pairs={{0,64},{1,65},{2,66},{3,67},{4,68},{5,69},{6,70},{7,71},{8,72},{9,... | collective-permute-start | bytes 393224 | tf_op jit(solution)/shard_map/ppermute | solution.py:48
  5.9 9.2 %collective-permute-start.1 = (bf16[128,512]{1,0:T(8,128)(2,1)}, bf16[128,512]{1,0:T(8,128)(2,1)}, u32[]{:S(2)}, u32[]{:S(2)}) collective-permute-start(bf16[128,512]{1,0:T(8,128)(2,1)} %get-tuple-element.37), channel_id=1, source_target_pairs={{0,128},{1,129},{2,130},{3,131},{4,132},{5,133},{6,134},{7,135},{8... | collective-permute-start | bytes 393224 | tf_op jit(solution)/shard_map/ppermute | solution.py:48
  8.8 6.3 %collective-permute-start.2 = (bf16[128,512]{1,0:T(8,128)(2,1)}, bf16[128,512]{1,0:T(8,128)(2,1)}, u32[]{:S(2)}, u32[]{:S(2)}) collective-permute-start(bf16[128,512]{1,0:T(8,128)(2,1)} %get-tuple-element.38), channel_id=1, source_target_pairs={{0,192},{1,193},{2,194},{3,195},{4,196},{5,197},{6,198},{7,199},{8... | collective-permute-start | bytes 393224 | tf_op jit(solution)/shard_map/ppermute | solution.py:48
  16.2 14.0 %copy-start.7 = (f32[512]{0:T(512)S(1)}, f32[512]{0:T(512)}, u32[]{:S(2)}) copy-start(f32[512]{0:T(512)} %param.9) | copy-start | bytes 6148
  16.8 24.7 %collective-permute-start.11 = (bf16[512,1024]{1,0:T(8,128)(2,1)S(1)}, bf16[512,1024]{1,0:T(8,128)(2,1)S(1)}, u32[]{:S(2)}, u32[]{:S(2)}) collective-permute-start(bf16[512,1024]{1,0:T(8,128)(2,1)S(1)} %shard_map.81), channel_id=1, source_target_pairs={{0,1},{1,0},{2,3},{3,2},{4,5},{5,4},{6,7},{7,6},{8,9},{9,8},{10,11... | collective-permute-start | bytes 3145736 | tf_op jit(solution)/shard_map/ppermute | solution.py:48
  16.9 13.3 %collective-permute-start.3 = (bf16[128,512]{1,0:T(8,128)(2,1)S(1)}, bf16[128,512]{1,0:T(8,128)(2,1)S(1)}, u32[]{:S(2)}, u32[]{:S(2)}) collective-permute-start(bf16[128,512]{1,0:T(8,128)(2,1)S(1)} %get-tuple-element.40), channel_id=1, source_target_pairs={{0,32},{1,33},{2,34},{3,35},{4,36},{5,37},{6,38},{7,39},{8,40},{9,... | collective-permute-start | bytes 393224 | tf_op jit(solution)/shard_map/ppermute | solution.py:48
  30.3 7.3 %collective-permute-start.9 = (bf16[128,512]{1,0:T(8,128)(2,1)S(1)}, bf16[128,512]{1,0:T(8,128)(2,1)S(1)}, u32[]{:S(2)}, u32[]{:S(2)}) collective-permute-start(bf16[128,512]{1,0:T(8,128)(2,1)S(1)} %shard_map.80.refs_0_.a), channel_id=1, source_target_pairs={{0,64},{1,65},{2,66},{3,67},{4,68},{5,69},{6,70},{7,71},{8,72},{9,... | collective-permute-start | bytes 393224 | tf_op jit(solution)/shard_map/ppermute | solution.py:48
  31.6 8.4 %collective-permute-start.7 = (bf16[128,512]{1,0:T(8,128)(2,1)S(1)}, bf16[128,512]{1,0:T(8,128)(2,1)S(1)}, u32[]{:S(2)}, u32[]{:S(2)}) collective-permute-start(bf16[128,512]{1,0:T(8,128)(2,1)S(1)} %shard_map.80.refs_0_.a), channel_id=1, source_target_pairs={{0,128},{1,129},{2,130},{3,131},{4,132},{5,133},{6,134},{7,135},{8... | collective-permute-start | bytes 393224 | tf_op jit(solution)/shard_map/ppermute | solution.py:48
  34.0 6.2 %collective-permute-start.5 = (bf16[128,512]{1,0:T(8,128)(2,1)S(1)}, bf16[128,512]{1,0:T(8,128)(2,1)S(1)}, u32[]{:S(2)}, u32[]{:S(2)}) collective-permute-start(bf16[128,512]{1,0:T(8,128)(2,1)S(1)} %shard_map.80.refs_0_.a), channel_id=1, source_target_pairs={{0,192},{1,193},{2,194},{3,195},{4,196},{5,197},{6,198},{7,199},{8... | collective-permute-start | bytes 393224 | tf_op jit(solution)/shard_map/ppermute | solution.py:48
  35.6 5.6 %collective-permute-start.4 = (bf16[128,512]{1,0:T(8,128)(2,1)S(1)}, bf16[128,512]{1,0:T(8,128)(2,1)S(1)}, u32[]{:S(2)}, u32[]{:S(2)}) collective-permute-start(bf16[128,512]{1,0:T(8,128)(2,1)S(1)} %shard_map.80.refs_0_.a), channel_id=1, source_target_pairs={{0,1},{1,0},{2,3},{3,2},{4,5},{5,4},{6,7},{7,6},{8,9},{9,8},{10,11... | collective-permute-start | bytes 393224 | tf_op jit(solution)/shard_map/ppermute | solution.py:48
  37.6 3.6 %collective-permute-start.10 = (bf16[128,512]{1,0:T(8,128)(2,1)S(1)}, bf16[128,512]{1,0:T(8,128)(2,1)S(1)}, u32[]{:S(2)}, u32[]{:S(2)}) collective-permute-start(bf16[128,512]{1,0:T(8,128)(2,1)S(1)} %collective-permute-done.9.refs_3_.d), channel_id=1, source_target_pairs={{0,1},{1,0},{2,3},{3,2},{4,5},{5,4},{6,7},{7,6},{8,9},{9,8},{10,11... | collective-permute-start | bytes 393224 | tf_op jit(solution)/shard_map/ppermute | solution.py:48
  40.0 1.3 %collective-permute-start.8 = (bf16[128,512]{1,0:T(8,128)(2,1)S(1)}, bf16[128,512]{1,0:T(8,128)(2,1)S(1)}, u32[]{:S(2)}, u32[]{:S(2)}) collective-permute-start(bf16[128,512]{1,0:T(8,128)(2,1)S(1)} %collective-permute-done.7.refs_2_.c), channel_id=1, source_target_pairs={{0,1},{1,0},{2,3},{3,2},{4,5},{5,4},{6,7},{7,6},{8,9},{9,8},{10,11... | collective-permute-start | bytes 393224 | tf_op jit(solution)/shard_map/ppermute | solution.py:48
  40.2 1.0 copy-start.4
  40.2 1.3 %collective-permute-start.6 = (bf16[128,512]{1,0:T(8,128)(2,1)S(1)}, bf16[128,512]{1,0:T(8,128)(2,1)S(1)}, u32[]{:S(2)}, u32[]{:S(2)}) collective-permute-start(bf16[128,512]{1,0:T(8,128)(2,1)S(1)} %collective-permute-done.5.refs_1_.b), channel_id=1, source_target_pairs={{0,1},{1,0},{2,3},{3,2},{4,5},{5,4},{6,7},{7,6},{8,9},{9,8},{10,11... | collective-permute-start | bytes 393224 | tf_op jit(solution)/shard_map/ppermute | solution.py:48
  42.8 11.3 %collective-permute-start.12 = (bf16[128,1024]{1,0:T(8,128)(2,1)}, bf16[128,1024]{1,0:T(8,128)(2,1)}, u32[]{:S(2)}, u32[]{:S(2)}) collective-permute-start(bf16[128,1024]{1,0:T(8,128)(2,1)} %get-tuple-element.43), channel_id=1, source_target_pairs={{0,2},{1,3},{2,4},{3,5},{4,6},{5,7},{6,0},{7,1},{8,10},{9,11},{10,... | collective-permute-start | bytes 786440 | tf_op jit(solution)/shard_map/ppermute | solution.py:48
  44.3 13.5 %collective-permute-start.14 = (bf16[128,1024]{1,0:T(8,128)(2,1)}, bf16[128,1024]{1,0:T(8,128)(2,1)}, u32[]{:S(2)}, u32[]{:S(2)}) collective-permute-start(bf16[128,1024]{1,0:T(8,128)(2,1)} %get-tuple-element.44), channel_id=1, source_target_pairs={{0,6},{1,7},{2,0},{3,1},{4,2},{5,3},{6,4},{7,5},{8,14},{9,15},{10,... | collective-permute-start | bytes 786440 | tf_op jit(solution)/shard_map/ppermute | solution.py:48
  47.1 12.4 %collective-permute-start.13 = (bf16[128,1024]{1,0:T(8,128)(2,1)}, bf16[128,1024]{1,0:T(8,128)(2,1)}, u32[]{:S(2)}, u32[]{:S(2)}) collective-permute-start(bf16[128,1024]{1,0:T(8,128)(2,1)} %shard_map.86), channel_id=1, source_target_pairs={{0,4},{1,5},{2,6},{3,7},{4,0},{5,1},{6,2},{7,3},{8,12},{9,13},{10,... | collective-permute-start | bytes 786440 | tf_op jit(solution)/shard_map/ppermute | solution.py:48
  49.6 0.9 copy-start.5
  50.8 1.6 %copy-start.1 = (bf16[512,1,2048]{2,0,1:T(8,128)(2,1)S(1)}, bf16[512,1,2048]{2,0,1:T(8,128)(2,1)}, u32[]{:S(2)}) copy-start(bf16[512,1,2048]{2,0,1:T(8,128)(2,1)} %param.6) | copy-start | bytes 6291460
  52.4 12.0 %copy-start.2 = (bf16[512,1,2048]{2,0,1:T(8,128)(2,1)S(1)}, bf16[512,1,2048]{2,0,1:T(8,128)(2,1)}, u32[]{:S(2)}) copy-start(bf16[512,1,2048]{2,0,1:T(8,128)(2,1)} %param.6) | copy-start | bytes 6291460
  52.4 12.0 %copy-start.6 = (f32[1,2048]{1,0:T(1,128)S(1)}, f32[1,2048]{1,0:T(1,128)}, u32[]{:S(2)}) copy-start(f32[1,2048]{1,0:T(1,128)} %bias.1) | copy-start | bytes 24580
  60.8 4.4 %collective-permute-start.15 = (bf16[128,256]{1,0:T(8,128)(2,1)S(1)}, bf16[128,256]{1,0:T(8,128)(2,1)S(1)}, u32[]{:S(2)}, u32[]{:S(2)}) collective-permute-start(bf16[128,256]{1,0:T(8,128)(2,1)S(1)} %get-tuple-element.51), channel_id=1, source_target_pairs={{0,8},{1,9},{2,10},{3,11},{4,12},{5,13},{6,14},{7,15},{8,0},{9,1},... | collective-permute-start | bytes 196616 | tf_op jit(solution)/shard_map/ppermute | solution.py:48
  60.9 6.7 %collective-permute-start.16 = (bf16[128,256]{1,0:T(8,128)(2,1)S(1)}, bf16[128,256]{1,0:T(8,128)(2,1)S(1)}, u32[]{:S(2)}, u32[]{:S(2)}) collective-permute-start(bf16[128,256]{1,0:T(8,128)(2,1)S(1)} %get-tuple-element.52), channel_id=1, source_target_pairs={{0,16},{1,17},{2,18},{3,19},{4,20},{5,21},{6,22},{7,23},{8,24},{9,... | collective-permute-start | bytes 196616 | tf_op jit(solution)/shard_map/ppermute | solution.py:48
  63.4 6.4 %collective-permute-start.17 = (bf16[128,256]{1,0:T(8,128)(2,1)S(1)}, bf16[128,256]{1,0:T(8,128)(2,1)S(1)}, u32[]{:S(2)}, u32[]{:S(2)}) collective-permute-start(bf16[128,256]{1,0:T(8,128)(2,1)S(1)} %get-tuple-element.53), channel_id=1, source_target_pairs={{0,24},{1,25},{2,26},{3,27},{4,28},{5,29},{6,30},{7,31},{8,16},{9,... | collective-permute-start | bytes 196616 | tf_op jit(solution)/shard_map/ppermute | solution.py:48
  69.8 6.5 %collective-permute-start.20 = (bf16[128,256]{1,0:T(8,128)(2,1)S(1)}, bf16[128,256]{1,0:T(8,128)(2,1)S(1)}, u32[]{:S(2)}, u32[]{:S(2)}) collective-permute-start(bf16[128,256]{1,0:T(8,128)(2,1)S(1)} %shard_map.89.a), channel_id=1, source_target_pairs={{0,24},{1,25},{2,26},{3,27},{4,28},{5,29},{6,30},{7,31},{8,16},{9,... | collective-permute-start | bytes 196616 | tf_op jit(solution)/shard_map/ppermute | solution.py:48
  70.9 5.4 %collective-permute-start.19 = (bf16[128,256]{1,0:T(8,128)(2,1)S(1)}, bf16[128,256]{1,0:T(8,128)(2,1)S(1)}, u32[]{:S(2)}, u32[]{:S(2)}) collective-permute-start(bf16[128,256]{1,0:T(8,128)(2,1)S(1)} %shard_map.89.a), channel_id=1, source_target_pairs={{0,16},{1,17},{2,18},{3,19},{4,20},{5,21},{6,22},{7,23},{8,24},{9,... | collective-permute-start | bytes 196616 | tf_op jit(solution)/shard_map/ppermute | solution.py:48
  73.0 4.3 %collective-permute-start.18 = (bf16[128,256]{1,0:T(8,128)(2,1)S(1)}, bf16[128,256]{1,0:T(8,128)(2,1)S(1)}, u32[]{:S(2)}, u32[]{:S(2)}) collective-permute-start(bf16[128,256]{1,0:T(8,128)(2,1)S(1)} %shard_map.89.a), channel_id=1, source_target_pairs={{0,8},{1,9},{2,10},{3,11},{4,12},{5,13},{6,14},{7,15},{8,0},{9,1},... | collective-permute-start | bytes 196616 | tf_op jit(solution)/shard_map/ppermute | solution.py:48
  77.3 11.9 %collective-permute-start.26 = (bf16[128,1024]{1,0:T(8,128)(2,1)S(1)}, bf16[128,1024]{1,0:T(8,128)(2,1)S(1)}, u32[]{:S(2)}, u32[]{:S(2)}) collective-permute-start(bf16[128,1024]{1,0:T(8,128)(2,1)S(1)} %shard_map.90.refs_0_), channel_id=1, source_target_pairs={{0,2},{1,3},{2,4},{3,5},{4,6},{5,7},{6,0},{7,1},{8,10},{9,11},{10,... | collective-permute-start | bytes 786440 | tf_op jit(solution)/shard_map/ppermute | solution.py:48
  78.2 11.0 %collective-permute-start.24 = (bf16[128,1024]{1,0:T(8,128)(2,1)S(1)}, bf16[128,1024]{1,0:T(8,128)(2,1)S(1)}, u32[]{:S(2)}, u32[]{:S(2)}) collective-permute-start(bf16[128,1024]{1,0:T(8,128)(2,1)S(1)} %shard_map.90.refs_0_), channel_id=1, source_target_pairs={{0,4},{1,5},{2,6},{3,7},{4,0},{5,1},{6,2},{7,3},{8,12},{9,13},{10,... | collective-permute-start | bytes 786440 | tf_op jit(solution)/shard_map/ppermute | solution.py:48
  80.3 9.6 %collective-permute-start.22 = (bf16[128,1024]{1,0:T(8,128)(2,1)S(1)}, bf16[128,1024]{1,0:T(8,128)(2,1)S(1)}, u32[]{:S(2)}, u32[]{:S(2)}) collective-permute-start(bf16[128,1024]{1,0:T(8,128)(2,1)S(1)} %shard_map.90.refs_0_), channel_id=1, source_target_pairs={{0,6},{1,7},{2,0},{3,1},{4,2},{5,3},{6,4},{7,5},{8,14},{9,15},{10,... | collective-permute-start | bytes 786440 | tf_op jit(solution)/shard_map/ppermute | solution.py:48
  81.0 9.6 %collective-permute-start.21 = (bf16[128,1024]{1,0:T(8,128)(2,1)S(1)}, bf16[128,1024]{1,0:T(8,128)(2,1)S(1)}, u32[]{:S(2)}, u32[]{:S(2)}) collective-permute-start(bf16[128,1024]{1,0:T(8,128)(2,1)S(1)} %shard_map.90.refs_0_), channel_id=1, source_target_pairs={{0,1},{1,0},{2,3},{3,2},{4,5},{5,4},{6,7},{7,6},{8,9},{9,8},{10,11... | collective-permute-start | bytes 786440 | tf_op jit(solution)/shard_map/ppermute | solution.py:48
  89.2 1.5 %collective-permute-start.27 = (bf16[128,1024]{1,0:T(8,128)(2,1)S(1)}, bf16[128,1024]{1,0:T(8,128)(2,1)S(1)}, u32[]{:S(2)}, u32[]{:S(2)}) collective-permute-start(bf16[128,1024]{1,0:T(8,128)(2,1)S(1)} %collective-permute-done.26.refs_3_), channel_id=1, source_target_pairs={{0,1},{1,0},{2,3},{3,2},{4,5},{5,4},{6,7},{7,6},{8,9},{9,8},{10,11... | collective-permute-start | bytes 786440 | tf_op jit(solution)/shard_map/ppermute | solution.py:48
  89.2 1.9 %collective-permute-start.25 = (bf16[128,1024]{1,0:T(8,128)(2,1)S(1)}, bf16[128,1024]{1,0:T(8,128)(2,1)S(1)}, u32[]{:S(2)}, u32[]{:S(2)}) collective-permute-start(bf16[128,1024]{1,0:T(8,128)(2,1)S(1)} %collective-permute-done.24.refs_2_), channel_id=1, source_target_pairs={{0,1},{1,0},{2,3},{3,2},{4,5},{5,4},{6,7},{7,6},{8,9},{9,8},{10,11... | collective-permute-start | bytes 786440 | tf_op jit(solution)/shard_map/ppermute | solution.py:48
  89.9 1.6 %collective-permute-start.23 = (bf16[128,1024]{1,0:T(8,128)(2,1)S(1)}, bf16[128,1024]{1,0:T(8,128)(2,1)S(1)}, u32[]{:S(2)}, u32[]{:S(2)}) collective-permute-start(bf16[128,1024]{1,0:T(8,128)(2,1)S(1)} %collective-permute-done.22.refs_1_), channel_id=1, source_target_pairs={{0,1},{1,0},{2,3},{3,2},{4,5},{5,4},{6,7},{7,6},{8,9},{9,8},{10,11... | collective-permute-start | bytes 786440 | tf_op jit(solution)/shard_map/ppermute | solution.py:48
  92.3 7.2 %collective-permute-start.28 = (bf16[128,512]{1,0:T(8,128)(2,1)S(1)}, bf16[128,512]{1,0:T(8,128)(2,1)S(1)}, u32[]{:S(2)}, u32[]{:S(2)}) collective-permute-start(bf16[128,512]{1,0:T(8,128)(2,1)S(1)} %get-tuple-element.57), channel_id=1, source_target_pairs={{0,64},{1,65},{2,66},{3,67},{4,68},{5,69},{6,70},{7,71},{8,72},{9,... | collective-permute-start | bytes 393224 | tf_op jit(solution)/shard_map/ppermute | solution.py:48
  93.6 8.7 %collective-permute-start.29 = (bf16[128,512]{1,0:T(8,128)(2,1)S(1)}, bf16[128,512]{1,0:T(8,128)(2,1)S(1)}, u32[]{:S(2)}, u32[]{:S(2)}) collective-permute-start(bf16[128,512]{1,0:T(8,128)(2,1)S(1)} %get-tuple-element.58), channel_id=1, source_target_pairs={{0,128},{1,129},{2,130},{3,131},{4,132},{5,133},{6,134},{7,135},{8... | collective-permute-start | bytes 393224 | tf_op jit(solution)/shard_map/ppermute | solution.py:48
  96.0 6.5 %collective-permute-start.30 = (bf16[128,512]{1,0:T(8,128)(2,1)S(1)}, bf16[128,512]{1,0:T(8,128)(2,1)S(1)}, u32[]{:S(2)}, u32[]{:S(2)}) collective-permute-start(bf16[128,512]{1,0:T(8,128)(2,1)S(1)} %get-tuple-element.59), channel_id=1, source_target_pairs={{0,192},{1,193},{2,194},{3,195},{4,196},{5,197},{6,198},{7,199},{8... | collective-permute-start | bytes 393224 | tf_op jit(solution)/shard_map/ppermute | solution.py:48
  102.5 11.5 %collective-permute-start.31 = (bf16[128,512]{1,0:T(8,128)(2,1)S(1)}, bf16[128,512]{1,0:T(8,128)(2,1)S(1)}, u32[]{:S(2)}, u32[]{:S(2)}) collective-permute-start(bf16[128,512]{1,0:T(8,128)(2,1)S(1)} %get-tuple-element.66), channel_id=1, source_target_pairs={{0,32},{1,33},{2,34},{3,35},{4,36},{5,37},{6,38},{7,39},{8,40},{9,... | collective-permute-start | bytes 393224 | tf_op jit(solution)/shard_map/ppermute | solution.py:48
  114.1 7.7 %collective-permute-start.34 = (bf16[128,512]{1,0:T(8,128)(2,1)S(1)}, bf16[128,512]{1,0:T(8,128)(2,1)S(1)}, u32[]{:S(2)}, u32[]{:S(2)}) collective-permute-start(bf16[128,512]{1,0:T(8,128)(2,1)S(1)} %shard_map.95.a), channel_id=1, source_target_pairs={{0,64},{1,65},{2,66},{3,67},{4,68},{5,69},{6,70},{7,71},{8,72},{9,... | collective-permute-start | bytes 393224 | tf_op jit(solution)/shard_map/ppermute | solution.py:48
  116.4 6.1 %collective-permute-start.33 = (bf16[128,512]{1,0:T(8,128)(2,1)S(1)}, bf16[128,512]{1,0:T(8,128)(2,1)S(1)}, u32[]{:S(2)}, u32[]{:S(2)}) collective-permute-start(bf16[128,512]{1,0:T(8,128)(2,1)S(1)} %shard_map.95.a), channel_id=1, source_target_pairs={{0,192},{1,193},{2,194},{3,195},{4,196},{5,197},{6,198},{7,199},{8... | collective-permute-start | bytes 393224 | tf_op jit(solution)/shard_map/ppermute | solution.py:48
  117.5 6.5 %collective-permute-start.32 = (bf16[128,512]{1,0:T(8,128)(2,1)S(1)}, bf16[128,512]{1,0:T(8,128)(2,1)S(1)}, u32[]{:S(2)}, u32[]{:S(2)}) collective-permute-start(bf16[128,512]{1,0:T(8,128)(2,1)S(1)} %shard_map.95.a), channel_id=1, source_target_pairs={{0,128},{1,129},{2,130},{3,131},{4,132},{5,133},{6,134},{7,135},{8... | collective-permute-start | bytes 393224 | tf_op jit(solution)/shard_map/ppermute | solution.py:48
